TPU v7x, 128 devices: a whole 4x4x4 slice. The times are simulated.
128 devices in a mesh: pipe: 2 (over y_hi), dp: 16 (over z, y_lo, core), tensor: 4 (over x).
Axes of the slice: x: 4, y: 4 (y_hi: 2, y_lo: 2; y = y_hi * 2 + y_lo), z: 4, core: 2. Of those that a mesh axis runs over, the one named last changes fastest.
Arguments:
- boundary: float32 [2, 4, 4096, 768], P('pipe', None, 'dp'), may hold values from -6 to 6
- segment_ids: int32 [4, 4, 1024], replicated, may hold values from 0 to 4, as said below
- attn_gain: float32 [2, 768], P('pipe'), may hold values from 0.1 to 1.9
- attn_shift: float32 [2, 768], P('pipe'), may hold values from -1.5 to 1.5
- mlp_gain: float32 [2, 768], P('pipe'), may hold values from 0.1 to 1.9
- mlp_shift: float32 [2, 768], P('pipe'), may hold values from -1.5 to 1.5
- qkv_weight: bfloat16 [2, 768, 2304], P('pipe', None, 'tensor'), may hold values from -0.21875 to 0.21875
- qkv_bias: float32 [2, 2304], P('pipe', 'tensor'), may hold values from -2.5 to 2.5
- dense_weight: bfloat16 [2, 768, 768], P('pipe', 'tensor'), may hold values from -1.75 to 1.75
- dense_bias: float32 [2, 768], P('pipe'), may hold values from -2.5 to 2.5
- up_weight: bfloat16 [2, 768, 3072], P('pipe', None, 'tensor'), may hold values from -0.21875 to 0.21875
- up_bias: float32 [2, 3072], P('pipe', 'tensor'), may hold values from -2.5 to 2.5
- down_weight: bfloat16 [2, 3072, 768], P('pipe', 'tensor'), may hold values from -0.109375 to 0.109375
- down_bias: float32 [2, 768], P('pipe'), may hold values from -2.5 to 2.5
Outputs:
- boundary_out: float32 [2, 4, 4096, 768], P('pipe', None, 'dp')
- attn_gain_grad: float32 [2, 768], P('pipe')
- attn_shift_grad: float32 [2, 768], P('pipe')
- mlp_gain_grad: float32 [2, 768], P('pipe')
- mlp_shift_grad: float32 [2, 768], P('pipe')
- qkv_weight_grad: float32 [2, 768, 2304], P('pipe', None, 'tensor')
- qkv_bias_grad: float32 [2, 2304], P('pipe', 'tensor')
- dense_weight_grad: float32 [2, 768, 768], P('pipe', 'tensor')
- dense_bias_grad: float32 [2, 768], P('pipe')
- up_weight_grad: float32 [2, 768, 3072], P('pipe', None, 'tensor')
- up_bias_grad: float32 [2, 3072], P('pipe', 'tensor')
- down_weight_grad: float32 [2, 3072, 768], P('pipe', 'tensor')
- down_bias_grad: float32 [2, 768], P('pipe')
Inputs may be any that keep to these rules, and one draw needn't show every extreme that they name: `segment_ids`: within each sequence the numbers start at 0, never fall and rise by at most one from token to token; each document but the last of a sequence has at least 204 tokens; in every draw one whole sequence is a single document.
All inputs are finite; a program needn't handle non-finite values.
Results may differ from a plain program's by a relative error of at most 0.028.
Values may be sent and summed in bfloat16 or wider, within the bound.
A program may use at most 192 MiB of HBM per device.

v0:
```python
from functools import partial

import jax
import jax.numpy as jnp
from jax import lax
from jax.sharding import PartitionSpec as P

HEAD_DIM = 64
ROT = 16


EPS = 1e-05
MASKED = -1e30


def passed_along(value, axis, steps):
    count = lax.axis_size(axis)
    first, last = (max(0, -steps), min(count, count - steps))
    return lax.ppermute(value, axis, [(source, source + steps) for source in range(first, last)])


def layer_norm(flat, gain, shift):
    middle = jnp.mean(flat, axis=-1, keepdims=True)
    centred = flat - middle
    inverse = lax.rsqrt(jnp.mean(centred * centred, axis=-1, keepdims=True) + EPS)
    normed = centred * inverse
    return (normed * gain + shift, normed, inverse)


def norm_back(grad, normed, inverse, gain):
    scaled = grad * gain
    inner = scaled - jnp.mean(scaled, axis=-1, keepdims=True)
    inner = inner - normed * jnp.mean(scaled * normed, axis=-1, keepdims=True)
    return (inner * inverse, jnp.sum(grad * normed, axis=0), jnp.sum(grad, axis=0))


def rotary_tables(places, rot_dims):
    half = rot_dims // 2
    freqs = 10000.0 ** (-(2.0 * jnp.arange(half, dtype=jnp.float32)) / rot_dims)
    angles = places.astype(jnp.float32)[..., None] * freqs
    angles = jnp.concatenate([angles, angles], axis=-1)
    return (jnp.cos(angles), jnp.sin(angles))


def rotate(vector, cosine, sine, rot_dims):
    portion = vector[..., :rot_dims]
    half = rot_dims // 2
    turned = jnp.concatenate([-portion[..., half:], portion[..., :half]], axis=-1)
    return jnp.concatenate([portion * cosine + turned * sine, vector[..., rot_dims:]], axis=-1)


def unrotate(grad, cosine, sine, rot_dims):
    portion = grad[..., :rot_dims]
    half = rot_dims // 2
    moved = portion * sine
    back = jnp.concatenate([moved[..., half:], -moved[..., :half]], axis=-1)
    return jnp.concatenate([portion * cosine + back, grad[..., rot_dims:]], axis=-1)


def local(
    boundary,
    segment_ids,
    attn_gain,
    attn_shift,
    mlp_gain,
    mlp_shift,
    qkv_weight,
    qkv_bias,
    dense_weight,
    dense_bias,
    up_weight,
    up_bias,
    down_weight,
    down_bias,
):
    micro = boundary.shape[1]
    tok_dev = boundary.shape[2]
    width = boundary.shape[3]
    seq_len = segment_ids.shape[2]
    group = min(tok_dev, seq_len)
    nseq = tok_dev // group
    pieces = seq_len // group
    heads_here = dense_weight.shape[1] // HEAD_DIM
    inner_width = heads_here * HEAD_DIM
    scale = HEAD_DIM ** (-0.5)
    section = lax.axis_index("pipe")
    place = lax.axis_index("dp")
    member = place % pieces
    first_seq = place * tok_dev // seq_len
    bf16 = jnp.bfloat16
    f32 = jnp.float32
    gain_one = attn_gain[0]
    shift_one = attn_shift[0]
    gain_two = mlp_gain[0]
    shift_two = mlp_shift[0]
    packer = qkv_weight[0]
    packer_bias = qkv_bias[0]
    dense = dense_weight[0]
    upward = up_weight[0]
    upward_bias = up_bias[0]
    downward = down_weight[0]
    extra_bias = dense_bias[0] + down_bias[0]

    def collect(both, again):
        buffer = jnp.zeros((nseq, seq_len, 2 * inner_width), bf16)
        buffer = lax.dynamic_update_slice_in_dim(buffer, both, member * group, 1)
        for back in range(1, pieces):
            if again:
                got = passed_along(both, "dp", back)
            else:
                got = passed_along(both, "dp", back)
            start = jnp.maximum(member - back, 0) * group
            older = lax.dynamic_slice_in_dim(buffer, start, group, 1)
            buffer = lax.dynamic_update_slice_in_dim(
                buffer, jnp.where(member >= back, got, older), start, 1
            )
        return buffer

    def scores_of(query, keys_all, allowed):
        raw = jnp.einsum("sqhd,skhd->shqk", query, keys_all, preferred_element_type=f32) * scale
        return jnp.where(allowed[:, None], raw, MASKED)

    def split_pair(both_all):
        shaped = both_all.reshape(nseq, seq_len, 2, heads_here, HEAD_DIM)
        return (shaped[:, :, 0], shaped[:, :, 1])

    nothing = jnp.zeros((tok_dev, width), f32)
    received = nothing
    kept_list = []
    results = []
    for step in range(micro + 1):
        index = jnp.clip(step - section, 0, micro - 1)
        own = boundary[0, min(step, micro - 1)]
        flat = jnp.where(section == 0, own, received)
        whole = lax.dynamic_index_in_dim(segment_ids, index, 0, keepdims=False)
        held = lax.dynamic_slice_in_dim(whole, first_seq, nseq, 0)
        mine = lax.dynamic_slice_in_dim(held, member * group, group, 1)
        spots = member * group + jnp.arange(group, dtype=jnp.int32)
        before = jnp.sum((held[:, None, :] < mine[:, :, None]).astype(jnp.int32), axis=-1)
        places = spots[None, :] - before
        positions = jnp.arange(seq_len, dtype=jnp.int32)
        micro_allowed = (held[:, None, :] == mine[:, :, None]) & (
            positions[None, None, :] <= spots[None, :, None]
        )
        micro_cosine, micro_sine = rotary_tables(places, ROT)
        forward_cosine = micro_cosine[:, :, None, :]
        forward_sine = micro_sine[:, :, None, :]
        first, forward_normed_one, forward_inverse_one = layer_norm(flat, gain_one, shift_one)
        second, forward_normed_two, forward_inverse_two = layer_norm(flat, gain_two, shift_two)
        forward_first_low = first.astype(bf16)
        forward_second_low = second.astype(bf16)
        packed = jnp.dot(forward_first_low, packer, preferred_element_type=f32) + packer_bias
        packed = packed.reshape(nseq, group, heads_here, 3, HEAD_DIM)
        forward_query = rotate(packed[:, :, :, 0], forward_cosine, forward_sine, ROT).astype(bf16)
        key_new = rotate(packed[:, :, :, 1], forward_cosine, forward_sine, ROT).astype(bf16)
        value_new = packed[:, :, :, 2].astype(bf16)
        forward_both = jnp.stack([key_new, value_new], axis=2).reshape(nseq, group, 2 * inner_width)
        forward_both_all = collect(forward_both, False)
        forward_keys_all, forward_values_all = split_pair(forward_both_all)
        forward_score = scores_of(forward_query, forward_keys_all, micro_allowed)
        top = jnp.max(forward_score, axis=-1, keepdims=True)
        expo = jnp.exp(forward_score - top)
        total = jnp.sum(expo, axis=-1, keepdims=True)
        forward_log_total = top + jnp.log(total)
        weights = (expo / total).astype(bf16)
        mixed = jnp.einsum(
            "shqk,skhd->sqhd", weights, forward_values_all, preferred_element_type=f32
        )
        forward_mixed_low = mixed.reshape(tok_dev, inner_width).astype(bf16)
        forward_hidden = (
            jnp.dot(forward_second_low, upward, preferred_element_type=f32) + upward_bias
        )
        forward_active_low = jax.nn.gelu(forward_hidden, approximate=False).astype(bf16)
        partial_out = jnp.dot(forward_mixed_low, dense, preferred_element_type=f32)
        partial_out = partial_out + jnp.dot(
            forward_active_low, downward, preferred_element_type=f32
        )
        branch = lax.psum(partial_out.astype(jnp.bfloat16), "tensor").astype(jnp.float32)
        result = flat + (branch + extra_bias)
        forward_kept = (
            forward_normed_one,
            forward_inverse_one,
            forward_normed_two,
            forward_inverse_two,
            forward_first_low,
            forward_second_low,
            forward_query,
            forward_both,
            forward_log_total,
            forward_mixed_low,
            forward_hidden,
            forward_active_low,
            micro_allowed,
            forward_cosine,
            forward_sine,
        )
        result, kept = (result, forward_kept)
        kept_list.append(kept)
        results.append(result)
        if step < micro:
            received = passed_along(result.astype(jnp.bfloat16), "pipe", 1).astype(result.dtype)
    received = nothing
    outer_total = None
    inner_total = None
    grad_list = []
    for step in range(micro + 1):
        later = min(step + 1, micro)
        earlier = max(step - 1, 0)
        kept = jax.tree.map(
            lambda first_one, second_one: jnp.where(section == 1, first_one, second_one),
            kept_list[later],
            kept_list[earlier],
        )
        own = boundary[0, min(step, micro - 1)]
        if step == micro:
            own = nothing
        grad = jnp.where(section == 1, own, received)
        last = step == micro

        def finish(parts, last=last, outer_total=outer_total):
            merged = (
                parts if outer_total is None else tuple((a + b for a, b in zip(outer_total, parts)))
            )
            return merged

        (
            normed_one,
            inverse_one,
            normed_two,
            inverse_two,
            first_low,
            second_low,
            backward_query,
            key_store,
            log_total,
            mixed_low,
            hidden,
            active_low,
            backward_allowed,
            cosine,
            sine,
        ) = kept
        grad_low = grad.astype(bf16)
        d_out_bias = jnp.sum(grad_low.astype(f32), axis=0)
        d_dense = jnp.einsum("rk,rn->kn", mixed_low, grad_low, preferred_element_type=f32)
        d_down = jnp.einsum("rk,rn->kn", active_low, grad_low, preferred_element_type=f32)
        d_active = jnp.einsum("rn,kn->rk", grad_low, downward, preferred_element_type=f32)
        d_hidden = jax.vjp(partial(jax.nn.gelu, approximate=False), hidden)[1](d_active)[0]
        d_hidden_low = d_hidden.astype(bf16)
        d_up = jnp.einsum("rk,rn->kn", second_low, d_hidden_low, preferred_element_type=f32)
        d_up_bias = jnp.sum(d_hidden_low.astype(f32), axis=0)
        d_second = jnp.einsum("rn,kn->rk", d_hidden_low, upward, preferred_element_type=f32)
        outer = finish((d_dense, d_out_bias, d_up, d_up_bias, d_down, d_out_bias))
        d_mixed = jnp.einsum("rn,kn->rk", grad_low, dense, preferred_element_type=f32)
        d_mixed = d_mixed.astype(bf16).reshape(nseq, group, heads_here, HEAD_DIM)
        backward_both_all = collect(key_store, True)
        backward_keys_all, values_all = split_pair(backward_both_all)
        score = scores_of(backward_query, backward_keys_all, backward_allowed)
        prob = jnp.exp(score - log_total)
        prob_low = prob.astype(bf16)
        d_prob = jnp.einsum("sqhd,skhd->shqk", d_mixed, values_all, preferred_element_type=f32)
        d_score = prob * (d_prob - jnp.sum(prob * d_prob, axis=-1, keepdims=True))
        d_score_low = d_score.astype(bf16)
        d_query = (
            jnp.einsum(
                "shqk,skhd->sqhd", d_score_low, backward_keys_all, preferred_element_type=f32
            )
            * scale
        )
        d_key_all = (
            jnp.einsum("shqk,sqhd->skhd", d_score_low, backward_query, preferred_element_type=f32)
            * scale
        )
        d_value_all = jnp.einsum("shqk,sqhd->skhd", prob_low, d_mixed, preferred_element_type=f32)
        d_both_all = jnp.stack([d_key_all, d_value_all], axis=2).reshape(
            nseq, seq_len, 2 * inner_width
        )
        d_both = lax.dynamic_slice_in_dim(d_both_all, member * group, group, 1)
        for backward_back in range(1, pieces):
            backward_start = jnp.maximum(member - backward_back, 0) * group
            outgoing = lax.dynamic_slice_in_dim(d_both_all, backward_start, group, 1)
            outgoing = jnp.where(member >= backward_back, outgoing, jnp.zeros_like(outgoing))
            d_both = d_both + passed_along(
                outgoing.astype(jnp.bfloat16), "dp", -backward_back
            ).astype(outgoing.dtype)
        d_both = d_both.reshape(nseq, group, 2, heads_here, HEAD_DIM)
        d_query = unrotate(d_query, cosine, sine, ROT)
        d_key = unrotate(d_both[:, :, 0], cosine, sine, ROT)
        d_packed = jnp.stack([d_query, d_key, d_both[:, :, 1]], axis=3)
        d_packed = d_packed.reshape(tok_dev, 3 * inner_width).astype(bf16)
        d_packer = jnp.einsum("rk,rn->kn", first_low, d_packed, preferred_element_type=f32)
        d_packer_bias = jnp.sum(d_packed.astype(f32), axis=0)
        d_first = jnp.einsum("rn,kn->rk", d_packed, packer, preferred_element_type=f32)
        d_first, d_second = (
            lax.psum(d_first.astype(jnp.bfloat16), "tensor").astype(jnp.float32),
            lax.psum(d_second.astype(jnp.bfloat16), "tensor").astype(jnp.float32),
        )
        back_one, d_gain_one, d_shift_one = norm_back(d_first, normed_one, inverse_one, gain_one)
        back_two, d_gain_two, d_shift_two = norm_back(d_second, normed_two, inverse_two, gain_two)
        d_flat = grad + back_one + back_two
        inner = (d_gain_one, d_shift_one, d_gain_two, d_shift_two, d_packer, d_packer_bias)
        d_flat, outer_total, inner_step = (d_flat, outer, inner)
        inner_total = (
            inner_step
            if inner_total is None
            else tuple((a + b for a, b in zip(inner_total, inner_step)))
        )
        grad_list.append(d_flat)
        if step < micro:
            received = passed_along(d_flat.astype(jnp.bfloat16), "pipe", -1).astype(d_flat.dtype)
    summed = (
        lax.psum(outer_total[0].astype(jnp.bfloat16), "dp").astype(jnp.float32),
        lax.psum(outer_total[1].astype(jnp.bfloat16), "dp").astype(jnp.float32),
        lax.psum(outer_total[2].astype(jnp.bfloat16), "dp").astype(jnp.float32),
        lax.psum(outer_total[3].astype(jnp.bfloat16), "dp").astype(jnp.float32),
        lax.psum(outer_total[4].astype(jnp.bfloat16), "dp").astype(jnp.float32),
        lax.psum(outer_total[5].astype(jnp.bfloat16), "dp").astype(jnp.float32),
        lax.psum(inner_total[0].astype(jnp.bfloat16), "dp").astype(jnp.float32),
        lax.psum(inner_total[1].astype(jnp.bfloat16), "dp").astype(jnp.float32),
        lax.psum(inner_total[2].astype(jnp.bfloat16), "dp").astype(jnp.float32),
        lax.psum(inner_total[3].astype(jnp.bfloat16), "dp").astype(jnp.float32),
        lax.psum(inner_total[4].astype(jnp.bfloat16), "dp").astype(jnp.float32),
        lax.psum(inner_total[5].astype(jnp.bfloat16), "dp").astype(jnp.float32),
    )
    outer_total = summed[:6]
    inner_total = summed[6:]
    pieces_out = [
        jnp.where(section == 0, grad_list[index + 1], results[index + 1]) for index in range(micro)
    ]
    boundary_out = jnp.stack(pieces_out)[None]
    return (
        boundary_out,
        inner_total[0][None],
        inner_total[1][None],
        inner_total[2][None],
        inner_total[3][None],
        inner_total[4][None],
        inner_total[5][None],
        outer_total[0][None],
        outer_total[1][None],
        outer_total[2][None],
        outer_total[3][None],
        outer_total[4][None],
        outer_total[5][None],
    )


def solution(mesh):
    in_specs = (
        P("pipe", None, "dp", None),
        P(),
        P("pipe", None),
        P("pipe", None),
        P("pipe", None),
        P("pipe", None),
        P("pipe", None, "tensor"),
        P("pipe", "tensor"),
        P("pipe", "tensor", None),
        P("pipe", None),
        P("pipe", None, "tensor"),
        P("pipe", "tensor"),
        P("pipe", "tensor", None),
        P("pipe", None),
    )
    out_specs = (
        P("pipe", None, "dp", None),
        P("pipe", None),
        P("pipe", None),
        P("pipe", None),
        P("pipe", None),
        P("pipe", None, "tensor"),
        P("pipe", "tensor"),
        P("pipe", "tensor", None),
        P("pipe", None),
        P("pipe", None, "tensor"),
        P("pipe", "tensor"),
        P("pipe", "tensor", None),
        P("pipe", None),
    )
    return jax.shard_map(local, mesh=mesh, in_specs=in_specs, out_specs=out_specs, check_vma=False)
```

profile of v0, /device:TPU:1, one launch (start us, length us, event | category | flops | bytes accessed | tf_op | source)
XLA Modules:
  0.0 830.4 jit_solution(5080252318583474641)
XLA Ops:
  19.9 4.6 collective-permute-start
  43.5 42.5 %all-reduce.15.cloned.1.call-done = bf16[256,768]{1,0:T(8,128)(2,1)} async-done(((bf16[256,768]{1,0:T(8,128)(2,1)}), bf16[256,768]{1,0:T(8,128)(2,1)}) %all-reduce.15.cloned.1.call-update) | async-done | bytes 393232 | tf_op jit(solution)/shard_map/psum | solution.py:178
  87.3 4.8 collective-permute-start.3
  101.5 5.8 collective-permute-start.7
  107.4 4.1 collective-permute-start.8
  113.0 5.2 collective-permute-start.4
  123.2 4.3 convert_reduce_fusion.19
  157.7 46.4 %all-reduce.27.cloned.1.call-done = (bf16[256,768]{1,0:T(8,128)(2,1)}, bf16[256,768]{1,0:T(8,128)(2,1)}, bf16[256,768]{1,0:T(8,128)(2,1)}) async-done(((bf16[256,768]{1,0:T(8,128)(2,1)}, bf16[256,768]{1,0:T(8,128)(2,1)}, bf16[256,768]{1,0:T(8,128)(2,1)}), (bf16[256,768]{1,0:T(8,128)(2,1)}, bf16[256,768]{1,0:T(8,128)(2,1)}, bf16[256,768]{1,0:T(8,128)(2,1)})) %all-reduce.27.cloned.1.call-update) | async-done | bytes 1179664 | tf_op jit(solution)/shard_map/psum | solution.py:178
  209.3 5.5 collective-permute-start.14
  215.6 4.5 collective-permute-done.13
  223.8 6.1 collective-permute-start.18
  235.6 4.3 collective-permute-start.15
  267.4 4.7 collective-permute-done.22
  285.1 40.4 %all-reduce.25.cloned.1.call-done = (bf16[256,768]{1,0:T(8,128)(2,1)}, bf16[256,768]{1,0:T(8,128)(2,1)}, bf16[256,768]{1,0:T(8,128)(2,1)}) async-done(((bf16[256,768]{1,0:T(8,128)(2,1)}, bf16[256,768]{1,0:T(8,128)(2,1)}, bf16[256,768]{1,0:T(8,128)(2,1)}), (bf16[256,768]{1,0:T(8,128)(2,1)}, bf16[256,768]{1,0:T(8,128)(2,1)}, bf16[256,768]{1,0:T(8,128)(2,1)})) %all-reduce.25.cloned.1.call-update) | async-done | bytes 1179664 | tf_op jit(solution)/shard_map/psum | solution.py:178
  333.1 5.7 collective-permute-start.25
  347.6 6.1 collective-permute-start.29
  359.3 4.3 collective-permute-start.26
  391.4 4.7 collective-permute-done.33
  411.4 38.0 %all-reduce.23.cloned.1.call-done = (bf16[256,768]{1,0:T(8,128)(2,1)}, bf16[256,768]{1,0:T(8,128)(2,1)}, bf16[256,768]{1,0:T(8,128)(2,1)}) async-done(((bf16[256,768]{1,0:T(8,128)(2,1)}, bf16[256,768]{1,0:T(8,128)(2,1)}, bf16[256,768]{1,0:T(8,128)(2,1)}), (bf16[256,768]{1,0:T(8,128)(2,1)}, bf16[256,768]{1,0:T(8,128)(2,1)}, bf16[256,768]{1,0:T(8,128)(2,1)})) %all-reduce.23.cloned.1.call-update) | async-done | bytes 1179664 | tf_op jit(solution)/shard_map/psum | solution.py:178
  457.0 5.7 collective-permute-start.36
  472.1 6.1 collective-permute-start.37
  483.7 4.3 collective-permute-start.40
  505.3 4.3 collective-permute-start.47
  529.6 4.7 collective-permute-start.43
  534.3 4.5 collective-permute-done.44
  550.1 40.0 %all-reduce.21.cloned.1.call-done = (bf16[256,768]{1,0:T(8,128)(2,1)}, bf16[256,768]{1,0:T(8,128)(2,1)}) async-done(((bf16[256,768]{1,0:T(8,128)(2,1)}, bf16[256,768]{1,0:T(8,128)(2,1)}), (bf16[256,768]{1,0:T(8,128)(2,1)}, bf16[256,768]{1,0:T(8,128)(2,1)})) %all-reduce.21.cloned.1.call-update) | async-done | bytes 786448 | tf_op jit(solution)/shard_map/psum | solution.py:296
  599.1 8.6 %collective-permute-done.46 = bf16[256,768]{1,0:T(8,128)(2,1)S(1)} collective-permute-done((bf16[256,768]{1,0:T(8,128)(2,1)S(1)}, bf16[256,768]{1,0:T(8,128)(2,1)S(1)}, u32[]{:S(2)}, u32[]{:S(2)}) %collective-permute-start.46) | collective-permute-done | bytes 393248 | tf_op jit(solution)/shard_map/ppermute | solution.py:19
  615.0 5.2 collective-permute-start.50
  634.7 5.6 fusion.55
  644.5 32.8 %all-reduce.19.cloned.1.call-done = (bf16[256,768]{1,0:T(8,128)(2,1)}, bf16[256,768]{1,0:T(8,128)(2,1)}, bf16[256,768]{1,0:T(8,128)(2,1)}) async-done(((bf16[256,768]{1,0:T(8,128)(2,1)}, bf16[256,768]{1,0:T(8,128)(2,1)}, bf16[256,768]{1,0:T(8,128)(2,1)}), (bf16[256,768]{1,0:T(8,128)(2,1)}, bf16[256,768]{1,0:T(8,128)(2,1)}, bf16[256,768]{1,0:T(8,128)(2,1)})) %all-reduce.19.cloned.1.call-update) | async-done | bytes 1179664 | tf_op jit(solution)/shard_map/psum | solution.py:296
  686.9 52.4 %all-reduce = (bf16[1,768]{1,0:T(2,128)(2,1)S(1)}, bf16[1,768]{1,0:T(2,128)(2,1)S(1)}, bf16[1,768]{1,0:T(2,128)(2,1)S(1)}, bf16[1,768]{1,0:T(2,128)(2,1)S(1)}, b...) all-reduce(bf16[1,768]{1,0:T(2,128)(2,1)} %broadcast_in_dim.135, ...), channel_id=1, replica_groups=mesh['pipe'=2,'dp'=16,'tensor'=4] {'dp'}, use_global_device_ids=true, to_apply=%region_70.71 | all-reduce | flops 5184 | bytes 20736 | tf_op jit(solution)/shard_map/psum | solution.py:318
  746.5 68.5 %all-reduce.17.cloned.1.call-done = (bf16[1,768,576]{1,2,0:T(8,128)(2,1)}, bf16[1,192,768]{2,1,0:T(8,128)(2,1)}, bf16[1,768,768]{2,1,0:T(8,128)(2,1)}, bf16[1,768,768]{2,1,0:T(8,128)(2,1)}) async-done(((bf16[1,768,576]{1,2,0:T(8,128)(2,1)}, bf16[1,192,768]{2,1,0:T(8,128)(2,1)}, bf16[1,768,768]{2,1,0:T(8,128)(2,1)}, bf16[1,768,768]{2,1,0:T(8,128)(2,1)}), (bf16[1,768,576]{1,2,0:T(8,128)(2,1)}, ...) | async-done | bytes 3538960 | tf_op jit(solution)/shard_map/psum | solution.py:322
  (1012 shorter events, 325.8 us)
Async XLA Ops:
  7.2 78.7 %all-reduce.15.cloned.1.call-start = ((), (), s32[]{:S(2)}) async-start(), calls=%async_computation | async-start | bytes 786432 | tf_op jit(solution)/shard_map/psum | solution.py:178
  19.9 17.4 %collective-permute-start = (bf16[1,256,384]{1,2,0:T(8,128)(2,1)S(1)}, bf16[1,256,384]{1,2,0:T(8,128)(2,1)S(1)}, u32[]{:S(2)}, u32[]{:S(2)}) collective-permute-start(bf16[1,256,384]{1,2,0:T(8,128)(2,1)S(1)} %bitcast.721), channel_id=1, source_target_pairs={{0,4},{4,8},{8,12},{12,16},{16,20},{20,24},{24,28},{28,32},{32,36}... | collective-permute-start | bytes 589832 | tf_op jit(solution)/shard_map/ppermute | solution.py:19
  43.4 160.7 %all-reduce.27.cloned.1.call-start = ((), (), s32[]{:S(2)}) async-start(), calls=%async_computation.6 | async-start | bytes 2359296 | tf_op jit(solution)/shard_map/psum | solution.py:178
  101.5 27.3 %collective-permute-start.7 = (bf16[1,256,384]{1,2,0:T(8,128)(2,1)S(1)}, bf16[1,256,384]{1,2,0:T(8,128)(2,1)S(1)}, u32[]{:S(2)}, u32[]{:S(2)}) collective-permute-start(bf16[1,256,384]{1,2,0:T(8,128)(2,1)S(1)} %bitcast.717), channel_id=1, source_target_pairs={{0,4},{4,8},{8,12},{12,16},{16,20},{20,24},{24,28},{28,32},{32,36}... | collective-permute-start | bytes 589832 | tf_op jit(solution)/shard_map/ppermute | solution.py:19
  107.4 24.5 %collective-permute-start.8 = (bf16[1,256,384]{1,2,0:T(8,128)(2,1)S(1)}, bf16[1,256,384]{1,2,0:T(8,128)(2,1)S(1)}, u32[]{:S(2)}, u32[]{:S(2)}) collective-permute-start(bf16[1,256,384]{1,2,0:T(8,128)(2,1)S(1)} %bitcast.718), channel_id=1, source_target_pairs={{0,8},{4,12},{8,16},{12,20},{16,24},{20,28},{24,32},{28,36},{32,40... | collective-permute-start | bytes 589832 | tf_op jit(solution)/shard_map/ppermute | solution.py:19
  111.5 20.5 %collective-permute-start.9 = (bf16[1,256,384]{1,2,0:T(8,128)(2,1)S(1)}, bf16[1,256,384]{1,2,0:T(8,128)(2,1)S(1)}, u32[]{:S(2)}, u32[]{:S(2)}) collective-permute-start(bf16[1,256,384]{1,2,0:T(8,128)(2,1)S(1)} %bitcast.719), channel_id=1, source_target_pairs={{0,12},{4,16},{8,20},{12,24},{16,28},{20,32},{24,36},{28,40},{32,4... | collective-permute-start | bytes 589832 | tf_op jit(solution)/shard_map/ppermute | solution.py:19
  113.0 22.6 %collective-permute-start.4 = (bf16[1,256,384]{1,2,0:T(8,128)(2,1)S(1)}, bf16[1,256,384]{1,2,0:T(8,128)(2,1)S(1)}, u32[]{:S(2)}, u32[]{:S(2)}) collective-permute-start(bf16[1,256,384]{1,2,0:T(8,128)(2,1)S(1)} %get-tuple-element.310), channel_id=1, source_target_pairs={{0,4},{4,8},{8,12},{12,16},{16,20},{20,24},{24,28},{28,32},{32,36}... | collective-permute-start | bytes 589832 | tf_op jit(solution)/shard_map/ppermute | solution.py:19
  118.2 17.4 %collective-permute-start.5 = (bf16[1,256,384]{1,2,0:T(8,128)(2,1)S(1)}, bf16[1,256,384]{1,2,0:T(8,128)(2,1)S(1)}, u32[]{:S(2)}, u32[]{:S(2)}) collective-permute-start(bf16[1,256,384]{1,2,0:T(8,128)(2,1)S(1)} %get-tuple-element.310), channel_id=1, source_target_pairs={{0,8},{4,12},{8,16},{12,20},{16,24},{20,28},{24,32},{28,36},{32,40... | collective-permute-start | bytes 589832 | tf_op jit(solution)/shard_map/ppermute | solution.py:19
  157.3 168.2 %all-reduce.25.cloned.1.call-start = ((), (), s32[]{:S(2)}) async-start(), calls=%async_computation.5 | async-start | bytes 2359296 | tf_op jit(solution)/shard_map/psum | solution.py:178
  223.8 26.2 %collective-permute-start.18 = (bf16[1,256,384]{1,2,0:T(8,128)(2,1)S(1)}, bf16[1,256,384]{1,2,0:T(8,128)(2,1)S(1)}, u32[]{:S(2)}, u32[]{:S(2)}) collective-permute-start(bf16[1,256,384]{1,2,0:T(8,128)(2,1)S(1)} %bitcast.709), channel_id=1, source_target_pairs={{0,4},{4,8},{8,12},{12,16},{16,20},{20,24},{24,28},{28,32},{32,36}... | collective-permute-start | bytes 589832 | tf_op jit(solution)/shard_map/ppermute | solution.py:19
  229.9 22.3 %collective-permute-start.19 = (bf16[1,256,384]{1,2,0:T(8,128)(2,1)S(1)}, bf16[1,256,384]{1,2,0:T(8,128)(2,1)S(1)}, u32[]{:S(2)}, u32[]{:S(2)}) collective-permute-start(bf16[1,256,384]{1,2,0:T(8,128)(2,1)S(1)} %bitcast.710), channel_id=1, source_target_pairs={{0,8},{4,12},{8,16},{12,20},{16,24},{20,28},{24,32},{28,36},{32,40... | collective-permute-start | bytes 589832 | tf_op jit(solution)/shard_map/ppermute | solution.py:19
  233.1 19.2 %collective-permute-start.20 = (bf16[1,256,384]{1,2,0:T(8,128)(2,1)S(1)}, bf16[1,256,384]{1,2,0:T(8,128)(2,1)S(1)}, u32[]{:S(2)}, u32[]{:S(2)}) collective-permute-start(bf16[1,256,384]{1,2,0:T(8,128)(2,1)S(1)} %bitcast.711), channel_id=1, source_target_pairs={{0,12},{4,16},{8,20},{12,24},{16,28},{20,32},{24,36},{28,40},{32,4... | collective-permute-start | bytes 589832 | tf_op jit(solution)/shard_map/ppermute | solution.py:19
  235.6 19.8 %collective-permute-start.15 = (bf16[1,256,384]{1,2,0:T(8,128)(2,1)S(1)}, bf16[1,256,384]{1,2,0:T(8,128)(2,1)S(1)}, u32[]{:S(2)}, u32[]{:S(2)}) collective-permute-start(bf16[1,256,384]{1,2,0:T(8,128)(2,1)S(1)} %get-tuple-element.318), channel_id=1, source_target_pairs={{0,4},{4,8},{8,12},{12,16},{16,20},{20,24},{24,28},{28,32},{32,36}... | collective-permute-start | bytes 589832 | tf_op jit(solution)/shard_map/ppermute | solution.py:19
  239.9 15.5 %collective-permute-start.16 = (bf16[1,256,384]{1,2,0:T(8,128)(2,1)S(1)}, bf16[1,256,384]{1,2,0:T(8,128)(2,1)S(1)}, u32[]{:S(2)}, u32[]{:S(2)}) collective-permute-start(bf16[1,256,384]{1,2,0:T(8,128)(2,1)S(1)} %get-tuple-element.318), channel_id=1, source_target_pairs={{0,8},{4,12},{8,16},{12,20},{16,24},{20,28},{24,32},{28,36},{32,40... | collective-permute-start | bytes 589832 | tf_op jit(solution)/shard_map/ppermute | solution.py:19
  277.0 172.3 %all-reduce.23.cloned.1.call-start = ((), (), s32[]{:S(2)}) async-start(), calls=%async_computation.4 | async-start | bytes 2359296 | tf_op jit(solution)/shard_map/psum | solution.py:178
  347.6 26.2 %collective-permute-start.29 = (bf16[1,256,384]{1,2,0:T(8,128)(2,1)S(1)}, bf16[1,256,384]{1,2,0:T(8,128)(2,1)S(1)}, u32[]{:S(2)}, u32[]{:S(2)}) collective-permute-start(bf16[1,256,384]{1,2,0:T(8,128)(2,1)S(1)} %bitcast.713), channel_id=1, source_target_pairs={{0,4},{4,8},{8,12},{12,16},{16,20},{20,24},{24,28},{28,32},{32,36}... | collective-permute-start | bytes 589832 | tf_op jit(solution)/shard_map/ppermute | solution.py:19
  353.7 22.5 %collective-permute-start.30 = (bf16[1,256,384]{1,2,0:T(8,128)(2,1)S(1)}, bf16[1,256,384]{1,2,0:T(8,128)(2,1)S(1)}, u32[]{:S(2)}, u32[]{:S(2)}) collective-permute-start(bf16[1,256,384]{1,2,0:T(8,128)(2,1)S(1)} %bitcast.714), channel_id=1, source_target_pairs={{0,8},{4,12},{8,16},{12,20},{16,24},{20,28},{24,32},{28,36},{32,40... | collective-permute-start | bytes 589832 | tf_op jit(solution)/shard_map/ppermute | solution.py:19
  356.9 19.4 %collective-permute-start.31 = (bf16[1,256,384]{1,2,0:T(8,128)(2,1)S(1)}, bf16[1,256,384]{1,2,0:T(8,128)(2,1)S(1)}, u32[]{:S(2)}, u32[]{:S(2)}) collective-permute-start(bf16[1,256,384]{1,2,0:T(8,128)(2,1)S(1)} %bitcast.715), channel_id=1, source_target_pairs={{0,12},{4,16},{8,20},{12,24},{16,28},{20,32},{24,36},{28,40},{32,4... | collective-permute-start | bytes 589832 | tf_op jit(solution)/shard_map/ppermute | solution.py:19
  359.3 20.0 %collective-permute-start.26 = (bf16[1,256,384]{1,2,0:T(8,128)(2,1)S(1)}, bf16[1,256,384]{1,2,0:T(8,128)(2,1)S(1)}, u32[]{:S(2)}, u32[]{:S(2)}) collective-permute-start(bf16[1,256,384]{1,2,0:T(8,128)(2,1)S(1)} %get-tuple-element.326), channel_id=1, source_target_pairs={{0,4},{4,8},{8,12},{12,16},{16,20},{20,24},{24,28},{28,32},{32,36}... | collective-permute-start | bytes 589832 | tf_op jit(solution)/shard_map/ppermute | solution.py:19
  363.7 15.8 %collective-permute-start.27 = (bf16[1,256,384]{1,2,0:T(8,128)(2,1)S(1)}, bf16[1,256,384]{1,2,0:T(8,128)(2,1)S(1)}, u32[]{:S(2)}, u32[]{:S(2)}) collective-permute-start(bf16[1,256,384]{1,2,0:T(8,128)(2,1)S(1)} %get-tuple-element.326), channel_id=1, source_target_pairs={{0,8},{4,12},{8,16},{12,20},{16,24},{20,28},{24,32},{28,36},{32,40... | collective-permute-start | bytes 589832 | tf_op jit(solution)/shard_map/ppermute | solution.py:19
  401.1 189.0 %all-reduce.21.cloned.1.call-start = ((), (), s32[]{:S(2)}) async-start(), calls=%async_computation.3 | async-start | bytes 1572864 | tf_op jit(solution)/shard_map/psum | solution.py:296
  472.1 43.4 %collective-permute-start.37 = (bf16[1,256,384]{1,2,0:T(8,128)(2,1)S(1)}, bf16[1,256,384]{1,2,0:T(8,128)(2,1)S(1)}, u32[]{:S(2)}, u32[]{:S(2)}) collective-permute-start(bf16[1,256,384]{1,2,0:T(8,128)(2,1)S(1)} %get-tuple-element.170), channel_id=1, source_target_pairs={{0,4},{4,8},{8,12},{12,16},{16,20},{20,24},{24,28},{28,32},{32,36}... | collective-permute-start | bytes 589832 | tf_op jit(solution)/shard_map/ppermute | solution.py:19
  478.2 40.3 %collective-permute-start.38 = (bf16[1,256,384]{1,2,0:T(8,128)(2,1)S(1)}, bf16[1,256,384]{1,2,0:T(8,128)(2,1)S(1)}, u32[]{:S(2)}, u32[]{:S(2)}) collective-permute-start(bf16[1,256,384]{1,2,0:T(8,128)(2,1)S(1)} %get-tuple-element.170), channel_id=1, source_target_pairs={{0,8},{4,12},{8,16},{12,20},{16,24},{20,28},{24,32},{28,36},{32,40... | collective-permute-start | bytes 589832 | tf_op jit(solution)/shard_map/ppermute | solution.py:19
  481.4 37.2 %collective-permute-start.39 = (bf16[1,256,384]{1,2,0:T(8,128)(2,1)S(1)}, bf16[1,256,384]{1,2,0:T(8,128)(2,1)S(1)}, u32[]{:S(2)}, u32[]{:S(2)}) collective-permute-start(bf16[1,256,384]{1,2,0:T(8,128)(2,1)S(1)} %get-tuple-element.170), channel_id=1, source_target_pairs={{0,12},{4,16},{8,20},{12,24},{16,28},{20,32},{24,36},{28,40},{32,4... | collective-permute-start | bytes 589832 | tf_op jit(solution)/shard_map/ppermute | solution.py:19
  483.7 19.6 %collective-permute-start.40 = (bf16[1,256,384]{1,2,0:T(8,128)(2,1)S(1)}, bf16[1,256,384]{1,2,0:T(8,128)(2,1)S(1)}, u32[]{:S(2)}, u32[]{:S(2)}) collective-permute-start(bf16[1,256,384]{1,2,0:T(8,128)(2,1)S(1)} %bitcast.743), channel_id=1, source_target_pairs={{0,4},{4,8},{8,12},{12,16},{16,20},{20,24},{24,28},{28,32},{32,36}... | collective-permute-start | bytes 589832 | tf_op jit(solution)/shard_map/ppermute | solution.py:19
  488.0 17.3 %collective-permute-start.41 = (bf16[1,256,384]{1,2,0:T(8,128)(2,1)S(1)}, bf16[1,256,384]{1,2,0:T(8,128)(2,1)S(1)}, u32[]{:S(2)}, u32[]{:S(2)}) collective-permute-start(bf16[1,256,384]{1,2,0:T(8,128)(2,1)S(1)} %bitcast.744), channel_id=1, source_target_pairs={{0,8},{4,12},{8,16},{12,20},{16,24},{20,28},{24,32},{28,36},{32,40... | collective-permute-start | bytes 589832 | tf_op jit(solution)/shard_map/ppermute | solution.py:19
  505.3 24.3 %collective-permute-start.47 = (bf16[1,256,384]{1,2,0:T(8,128)(2,1)}, bf16[1,256,384]{1,2,0:T(8,128)(2,1)S(1)}, u32[]{:S(2)}, u32[]{:S(2)}) collective-permute-start(bf16[1,256,384]{1,2,0:T(8,128)(2,1)} %get-tuple-element.169), channel_id=1, source_target_pairs={{0,4},{4,8},{8,12},{12,16},{16,20},{20,24},{24,28},{28,32},{32,36}... | collective-permute-start | bytes 589832 | tf_op jit(solution)/shard_map/ppermute | solution.py:19
  509.7 33.9 %collective-permute-start.48 = (bf16[1,256,384]{1,2,0:T(8,128)(2,1)}, bf16[1,256,384]{1,2,0:T(8,128)(2,1)}, u32[]{:S(2)}, u32[]{:S(2)}) collective-permute-start(bf16[1,256,384]{1,2,0:T(8,128)(2,1)} %get-tuple-element.169), channel_id=1, source_target_pairs={{0,8},{4,12},{8,16},{12,20},{16,24},{20,28},{24,32},{28,36},{32,40... | collective-permute-start | bytes 589832 | tf_op jit(solution)/shard_map/ppermute | solution.py:19
  515.6 81.8 %collective-permute-start.49 = (bf16[1,256,384]{1,2,0:T(8,128)(2,1)}, bf16[1,256,384]{1,2,0:T(8,128)(2,1)}, u32[]{:S(2)}, u32[]{:S(2)}) collective-permute-start(bf16[1,256,384]{1,2,0:T(8,128)(2,1)} %get-tuple-element.169), channel_id=1, source_target_pairs={{0,12},{4,16},{8,20},{12,24},{16,28},{20,32},{24,36},{28,40},{32,4... | collective-permute-start | bytes 589832 | tf_op jit(solution)/shard_map/ppermute | solution.py:19
  543.5 133.8 %all-reduce.19.cloned.1.call-start = ((), (), s32[]{:S(2)}) async-start(), calls=%async_computation.2 | async-start | bytes 2359296 | tf_op jit(solution)/shard_map/psum | solution.py:296
  612.1 14.9 %collective-permute-start.52 = (bf16[1,256,384]{1,2,0:T(8,128)(2,1)S(1)}, bf16[1,256,384]{1,2,0:T(8,128)(2,1)S(1)}, u32[]{:S(2)}, u32[]{:S(2)}) collective-permute-start(bf16[1,256,384]{1,2,0:T(8,128)(2,1)S(1)} %get-tuple-element.132), channel_id=1, source_target_pairs={{12,0},{16,4},{20,8},{24,12},{28,16},{32,20},{36,24},{40,28},{44,3... | collective-permute-start | bytes 589832 | tf_op jit(solution)/shard_map/ppermute | solution.py:19
  631.1 183.8 %all-reduce.17.cloned.1.call-start = ((), (), s32[]{:S(2)}) async-start(), calls=%async_computation.1 | async-start | bytes 7077888 | tf_op jit(solution)/shard_map/psum | solution.py:322
  (290 other events, 2969.6 us)
Sparse Core Ops, SparseCore 0:
  43.5 42.3 all-reduce.14
  157.4 46.6 all-reduce.26
  277.2 48.3 all-reduce.24
  401.2 48.0 all-reduce.22
  543.6 46.4 all-reduce.20
  631.3 46.0 all-reduce.18
  681.5 133.4 all-reduce.16
where the time goes:
time: 843 us; the launch traced here: 830 us
  waiting for transfers between devices  360 us (43%)
  starting transfers between devices  166 us (20%)
  matrix products  131 us (16%)
  other arithmetic  85 us (10%)
  blocking collectives  52.4 us (6%)
  between operations  20 us (2%)
  local copies, waits for them, and re-layouts  16.6 us (2%)
    psum x4, waiting for transfers between devices, local(): lax.psum(partial_out.astype(jnp.bfloat16), 'tensor').astype(jnp.float32)  167 us
    ppermute x53, starting transfers between devices, passed_along(): lax.ppermute(value, axis, [(source, source + steps) for source in range(f...  166 us
    psum x2, waiting for transfers between devices, local(): lax.psum(d_second.astype(jnp.bfloat16), 'tensor').astype(jnp.float32)  72.8 us
    psum x1, waiting for transfers between devices, local(): lax.psum(inner_total[4].astype(jnp.bfloat16), 'dp').astype(jnp.float32)  68.5 us
    psum x1, blocking collectives, local(): lax.psum(inner_total[0].astype(jnp.bfloat16), 'dp').astype(jnp.float32)  52.4 us
    ppermute x53, waiting for transfers between devices, passed_along(): lax.ppermute(value, axis, [(source, source + steps) for source in range(f...  50.9 us
  transfers between devices with their start and end apart: 60, of which 28 were waited for; matrix products, arithmetic and copies ran while one was open for 17% of the time, Pallas kernels for 0%

commit v1 on v0

v1 whole, which is shorter than its diff:
```python
import functools

import jax
import jax.numpy as jnp
from jax import lax
from jax.experimental import pallas as pl
from jax.experimental.pallas import tpu as pltpu
from jax.sharding import PartitionSpec as P

MESH = pl.DeviceIdType.MESH
HEAD_DIM = 64
ROT = 16
EPS = 1e-05
MASKED = -1e30
WIDTH = 768
SEQ = 1024
BLOCK = 256
HEADS = 3
INNER = HEADS * HEAD_DIM
GRAD_ROWS = 2304
bf16 = jnp.bfloat16
f32 = jnp.float32
VMEM_LIMIT = 56 * 1024 * 1024


class Place:
    def __init__(self):
        self.p = lax.axis_index("pipe")
        self.d = lax.axis_index("dp")
        self.x = lax.axis_index("tensor")
        self.z = self.d // 4
        self.low = (self.d // 2) % 2
        self.c = self.d % 2
        self.y = 2 * self.p + self.low

    def at_x(self, steps):
        return (self.p, self.d, (self.x + steps) % 4)

    def at_y(self, steps):
        y = (self.y + steps) % 4
        return (y // 2, self.z * 4 + (y % 2) * 2 + self.c, self.x)

    def at_z(self, steps):
        return (self.p, ((self.z + steps) % 4) * 4 + self.d % 4, self.x)

    def sibling(self):
        return (self.p, self.d + 1 - 2 * self.c, self.x)

    def partner(self):
        return (1 - self.p, self.z * 4 + (1 - self.low) * 2 + self.c, self.x)

    def beside(self):
        return (self.p, self.z * 4 + (1 - self.low) * 2 + self.c, self.x)


def greet(devices):
    barrier = pltpu.get_barrier_semaphore()
    for device in devices:
        pl.semaphore_signal(barrier, inc=1, device_id=device, device_id_type=MESH)
    pl.semaphore_wait(barrier, len(devices))


class Copies:
    def __init__(self, send_sems, recv_sems, somebody):
        self.send_sems, self.recv_sems = send_sems, recv_sems
        self.somebody = somebody
        self.count = 0
        self.started = []

    def send(self, src, dst, device):
        k = self.count
        self.count += 1
        copy = pltpu.make_async_remote_copy(
            src_ref=src,
            dst_ref=dst,
            send_sem=self.send_sems.at[k],
            recv_sem=self.recv_sems.at[k],
            device_id=device,
            device_id_type=MESH,
        )
        copy.start()
        self.started.append(copy)
        return k

    def landed(self, k, dst):
        pltpu.make_async_remote_copy(
            src_ref=dst,
            dst_ref=dst,
            send_sem=self.send_sems.at[k],
            recv_sem=self.recv_sems.at[k],
            device_id=self.somebody,
            device_id_type=MESH,
        ).wait_recv()

    def drain(self):
        for copy in self.started:
            copy.wait_send()


class RingSum:
    def __init__(self, copies, me, right, left, chunk, relay, direct, final):
        self.copies, self.me, self.right, self.left = copies, me, right, left
        self.chunk, self.relay_in, self.direct, self.final = chunk, relay, direct, final

    def start(self):
        me, send = self.me, self.copies.send
        far, after, before = (me + 2) % 4, (me + 1) % 4, (me + 3) % 4
        self.k = [
            send(self.chunk(far, 0), self.relay_in[0], self.right),
            send(self.chunk(far, 1), self.relay_in[1], self.left),
            send(self.chunk(after, 1), self.direct[1], self.right),
            send(self.chunk(before, 0), self.direct[0], self.left),
        ]

    def relay(self):
        me, copies = self.me, self.copies
        after, before = (me + 1) % 4, (me + 3) % 4
        copies.landed(self.k[0], self.relay_in[0])
        add_into(self.relay_in[0], self.chunk(after, 0))
        k0 = copies.send(self.relay_in[0], self.final[0], self.right)
        copies.landed(self.k[1], self.relay_in[1])
        add_into(self.relay_in[1], self.chunk(before, 1))
        k1 = copies.send(self.relay_in[1], self.final[1], self.left)
        self.k += [k0, k1]

    def finish(self, out):
        copies = self.copies
        copies.landed(self.k[3], self.direct[0])
        copies.landed(self.k[4], self.final[0])
        store_sum(out(0), self.chunk(self.me, 0), self.direct[0], self.final[0])
        copies.landed(self.k[2], self.direct[1])
        copies.landed(self.k[5], self.final[1])
        store_sum(out(1), self.chunk(self.me, 1), self.direct[1], self.final[1])


class RingGather:
    def __init__(self, copies, me, right, left, piece, halves):
        self.copies, self.me, self.right, self.left = copies, me, right, left
        self.piece, self.halves = piece, halves

    def start(self):
        mine = self.piece(self.me)
        self.k = [
            self.copies.send(mine, mine, self.right),
            self.copies.send(mine, mine, self.left),
        ]

    def relay(self):
        before, after = (self.me + 3) % 4, (self.me + 1) % 4
        self.copies.landed(self.k[0], self.piece(before))
        view = self.halves(before, 0)
        k0 = self.copies.send(view, view, self.right)
        self.copies.landed(self.k[1], self.piece(after))
        view = self.halves(after, 1)
        k1 = self.copies.send(view, view, self.left)
        self.k += [k0, k1]

    def finish(self):
        far = (self.me + 2) % 4
        self.copies.landed(self.k[2], self.halves(far, 0))
        self.copies.landed(self.k[3], self.halves(far, 1))


def add_into(ref, other):
    ref[...] = (ref[...].astype(f32) + other[...].astype(f32)).astype(ref.dtype)


def store_sum(out, *parts):
    total = parts[0][...].astype(f32)
    for part in parts[1:]:
        total = total + part[...].astype(f32)
    out[...] = total.astype(out.dtype)


def rows(start, size, step=16):
    return pl.ds(pl.multiple_of(start, step), size)


def spread_kernel(block, wq, wd, wu, wn, small, xg, oq, od, ou, on, osm, send_sems, recv_sems, local_sems):
    at = Place()
    p, x, y, z, c = at.p, at.x, at.y, at.z, at.c
    greet(
        [at.at_x(1), at.at_x(3), at.at_y(1), at.at_y(2), at.at_y(3), at.at_z(1), at.at_z(3), at.sibling()]
    )
    copies = Copies(send_sems, recv_sems, at.at_x(1))
    weights = [(wq, oq), (wd, od), (wu, ou), (wn, on)]

    def piece(ref, zz, cc):
        if ref.shape[-2] == INNER:
            return ref.at[rows(48 * zz, 48), pl.ds(pl.multiple_of(384 * cc, 128), 384)]
        return ref.at[rows(192 * zz + 96 * cc, 96)]

    def half(ref, zz, cc, h):
        if ref.shape[-2] == INNER:
            return ref.at[rows(48 * zz + 32 * h, 32 - 16 * h), pl.ds(pl.multiple_of(384 * cc, 128), 384)]
        return ref.at[rows(192 * zz + 96 * cc + 48 * h, 48)]

    quarter = rows(64 * x, 64)
    first = [
        copies.send(block.at[(y + k) % 4, quarter], xg.at[p, at.low, quarter], at.at_y(k)) for k in (1, 3, 2)
    ]
    sent = [
        copies.send(piece(src, z, c), piece(dst.at[p], z, c), at.partner()) for src, dst in weights
    ]
    sent_small = copies.send(small, osm.at[p], at.partner())
    local = [
        pltpu.make_async_copy(src, dst, local_sems.at[n])
        for n, (src, dst) in enumerate(
            [(block.at[y], xg.at[p, at.low]), (small, osm.at[p])] + [(s, d.at[p]) for s, d in weights]
        )
    ]
    for copy in local:
        copy.start()
    gathers = []
    for k, index in zip((1, 3, 2), first):
        source = (y + 4 - k) % 4
        slot = xg.at[source // 2, source % 2]
        copies.landed(index, slot.at[quarter])
        gather = RingGather(
            copies,
            x,
            at.at_x(1),
            at.at_x(3),
            lambda j, slot=slot: slot.at[rows(64 * j, 64)],
            lambda j, h, slot=slot: slot.at[rows(64 * j + 32 * h, 32)],
        )
        gather.start()
        gathers.append(gather)
    others = [dst.at[1 - p] for _, dst in weights]
    rings, shared = [], []
    for other, index in zip(others, sent):
        copies.landed(index, piece(other, z, c))
        ring = RingGather(
            copies,
            z,
            at.at_z(1),
            at.at_z(3),
            lambda j, other=other: piece(other, j, c),
            lambda j, h, other=other: half(other, j, c, h),
        )
        ring.start()
        rings.append(ring)
        mine = piece(other, z, c)
        shared.append((copies.send(mine, mine, at.sibling()), piece(other, z, 1 - c)))
    for gather in gathers:
        gather.relay()
    for other, ring in zip(others, rings):
        ring.relay()
        for j in ((z + 3) % 4, (z + 1) % 4):
            mine = piece(other, j, c)
            shared.append((copies.send(mine, mine, at.sibling()), piece(other, j, 1 - c)))
    for gather in gathers:
        gather.finish()
    for other, ring in zip(others, rings):
        ring.finish()
        j = (z + 2) % 4
        mine = piece(other, j, c)
        shared.append((copies.send(mine, mine, at.sibling()), piece(other, j, 1 - c)))
    copies.landed(sent_small, osm.at[1 - p])
    for index, view in shared:
        copies.landed(index, view)
    for copy in local:
        copy.wait()
    copies.drain()


SPREAD_COPIES = 3 + 4 + 1 + 12 + 16 + 16


def spread(block, wq, wd, wu, wn, small):
    any_space = pl.BlockSpec(memory_space=pl.ANY)
    shapes = [(2, 2, BLOCK, WIDTH)] + [(2,) + w.shape for w in (wq, wd, wu, wn)]
    return pl.pallas_call(
        spread_kernel,
        out_shape=[jax.ShapeDtypeStruct(s, bf16) for s in shapes]
        + [jax.ShapeDtypeStruct((2,) + small.shape, f32)],
        in_specs=[any_space] * 6,
        out_specs=[any_space] * 6,
        scratch_shapes=[
            pltpu.SemaphoreType.DMA((SPREAD_COPIES,)),
            pltpu.SemaphoreType.DMA((SPREAD_COPIES,)),
            pltpu.SemaphoreType.DMA((6,)),
        ],
        compiler_params=pltpu.CompilerParams(collective_id=0, has_side_effects=True),
        name="spread",
    )(block, wq, wd, wu, wn, small)


def x_sums(at, copies, parts, bufs):
    sums = []
    for n, part in enumerate(parts):
        sums.append(
            RingSum(
                copies,
                at.x,
                at.at_x(1),
                at.at_x(3),
                lambda j, h, part=part: part.at[h, rows(64 * j, 64)],
                [bufs.at[n, 0], bufs.at[n, 1]],
                [bufs.at[n, 2], bufs.at[n, 3]],
                [bufs.at[n, 4], bufs.at[n, 5]],
            )
        )
    return sums


SPLITS = 2


def total_kernel(part, out, bufs, send_sems, recv_sems):
    at = Place()
    greet([at.at_x(1), at.at_x(3)])
    copies = Copies(send_sems, recv_sems, at.at_x(1))
    wide = WIDTH // SPLITS
    cols = [pl.ds(n * wide, wide) for n in range(SPLITS)]
    sums = x_sums(at, copies, [part.at[:, :, col] for col in cols], bufs)
    for ring in sums:
        ring.start()
    for ring in sums:
        ring.relay()
    gathers = []
    for ring, col in zip(sums, cols):
        ring.finish(lambda h, col=col: out.at[h, rows(64 * at.x, 64), col])
        gather = RingGather(
            copies,
            at.x,
            at.at_x(1),
            at.at_x(3),
            lambda j, col=col: out.at[:, rows(64 * j, 64), col],
            lambda j, h, col=col: out.at[h, rows(64 * j, 64), col],
        )
        gather.start()
        gathers.append(gather)
    for gather in gathers:
        gather.relay()
    for gather in gathers:
        gather.finish()
    copies.drain()


def total_over_tensor(part):
    vmem = pl.BlockSpec(memory_space=pltpu.VMEM)
    count = SPLITS * 10
    return pl.pallas_call(
        total_kernel,
        out_shape=jax.ShapeDtypeStruct((2, BLOCK, WIDTH), bf16),
        in_specs=[vmem],
        out_specs=vmem,
        scratch_shapes=[
            pltpu.VMEM((SPLITS, 6, 64, WIDTH // SPLITS), bf16),
            pltpu.SemaphoreType.DMA((count,)),
            pltpu.SemaphoreType.DMA((count,)),
        ],
        compiler_params=pltpu.CompilerParams(
            collective_id=1, has_side_effects=True, vmem_limit_bytes=VMEM_LIMIT
        ),
        name="total",
    )(part)


def pieces_kernel(one, two, out, bufs, send_sems, recv_sems):
    at = Place()
    greet([at.at_x(1), at.at_x(3)])
    copies = Copies(send_sems, recv_sems, at.at_x(1))
    sums = x_sums(at, copies, [one, two], bufs)
    for ring in sums:
        ring.start()
    for ring in sums:
        ring.relay()
    for n, ring in enumerate(sums):
        ring.finish(lambda h, n=n: out.at[n, h])
    copies.drain()


def pieces_over_tensor(one, two):
    vmem = pl.BlockSpec(memory_space=pltpu.VMEM)
    return pl.pallas_call(
        pieces_kernel,
        out_shape=jax.ShapeDtypeStruct((2, 2, 64, WIDTH), bf16),
        in_specs=[vmem, vmem],
        out_specs=vmem,
        scratch_shapes=[
            pltpu.VMEM((2, 6, 64, WIDTH), bf16),
            pltpu.SemaphoreType.DMA((12,)),
            pltpu.SemaphoreType.DMA((12,)),
        ],
        compiler_params=pltpu.CompilerParams(
            collective_id=2, has_side_effects=True, vmem_limit_bytes=VMEM_LIMIT
        ),
        name="pieces",
    )(one, two)


def final_kernel(
    grads, small, slices, out, small_out, back,
    chip, a_one, b_one, a_bufs, b_bufs, a_tail, a_tail2, b_tail, b_tail2, got, send_sems, recv_sems, local_sem,
):
    at = Place()
    x, y, z, c, low = at.x, at.y, at.z, at.c, at.low
    greet(
        [at.at_x(k) for k in (1, 2, 3)]
        + [at.at_y(k) for k in (1, 2, 3)]
        + [at.at_z(k) for k in (1, 2, 3)]
        + [at.sibling()]
    )
    copies = Copies(send_sems, recv_sems, at.at_x(1))
    send, landed = copies.send, copies.landed
    left_cols, right_cols = pl.ds(0, 384), pl.ds(384, 384)
    quarter = rows(64 * x, 64)
    mine, theirs = rows(1152 * c, 1152), rows(1152 * (1 - c), 1152)

    core = []
    for cols in (left_cols, right_cols):
        for layer in range(2):
            core.append(send(grads.at[layer, theirs, cols], chip.at[layer, :, cols], at.sibling()))
    home = []
    for k in (1, 3, 2):
        j = (y + k) % 4
        home.append((k, send(slices.at[j // 2, j % 2], back.at[y, quarter], at.at_y(k))))
    own = pltpu.make_async_copy(slices.at[y // 2, y % 2], back.at[y, quarter], local_sem)
    own.start()
    small_x = [(k, send(small, got.at[k - 1], at.at_x(k))) for k in (1, 3, 2)]

    def add_core(n, layer, cols):
        landed(core[n], chip.at[layer, :, cols])

        def body(i, carry):
            here = rows(i * 128, 128)
            there = rows(1152 * c + i * 128, 128)
            chip[layer, here, cols] = (
                chip[layer, here, cols].astype(f32) + grads[layer, there, cols].astype(f32)
            ).astype(bf16)
            return carry

        lax.fori_loop(0, 9, body, 0)

    add_core(0, 0, left_cols)
    add_core(1, 1, left_cols)
    a_y = RingSum(
        copies, y, at.at_y(1), at.at_y(3),
        lambda j, h: chip.at[j // 2, rows(576 * (j % 2) + 288 * h, 288), left_cols],
        [a_bufs.at[0], a_bufs.at[1]], [a_bufs.at[2], a_bufs.at[3]], [a_bufs.at[4], a_bufs.at[5]],
    )
    a_y.start()
    add_core(2, 0, right_cols)
    add_core(3, 1, right_cols)
    b_z = RingSum(
        copies, z, at.at_z(1), at.at_z(3),
        lambda j, h: chip.at[h, rows(288 * j, 288), right_cols],
        [b_bufs.at[0], b_bufs.at[1]], [b_bufs.at[2], b_bufs.at[3]], [b_bufs.at[4], b_bufs.at[5]],
    )
    b_z.start()

    own.wait()
    for k, index in home:
        landed(index, back.at[(y + 4 - k) % 4, quarter])
    outer = RingGather(
        copies, x, at.at_x(1), at.at_x(3),
        lambda j: back.at[:, rows(64 * j, 64)],
        lambda j, h: back.at[pl.ds(2 * h, 2), rows(64 * j, 64)],
    )
    outer.start()
    for k, index in small_x:
        landed(index, got.at[k - 1])
    normed = lax.broadcasted_iota(jnp.int32, small.shape, 1) < 4
    others = got[0] + got[1] + got[2]
    small_out[...] = small[...] + jnp.where(normed, others, 0.0)
    small_z = [(k, send(small_out, got.at[2 + k], at.at_z(k))) for k in (1, 3, 2)]

    a_y.relay()
    b_z.relay()
    outer.relay()
    a_y.finish(lambda h: a_one.at[pl.ds(288 * h, 288)])

    def uneven(ref, start, h):
        return ref.at[rows(start + 80 * h, 80 - 16 * h)]

    a_rows = 1152 * c + 576 * low
    a_z = RingSum(
        copies, z, at.at_z(1), at.at_z(3),
        lambda j, h: uneven(a_one, 144 * j, h),
        [a_tail.at[0], a_tail2.at[0]], [a_tail.at[1], a_tail2.at[1]], [a_tail.at[2], a_tail2.at[2]],
    )
    a_z.start()
    b_z.finish(lambda h: b_one.at[h])
    b_rows = 1152 * c + 288 * z
    b_y = RingSum(
        copies, y, at.at_y(1), at.at_y(3),
        lambda j, h: b_one.at[j // 2, rows(144 * (j % 2) + 80 * h, 80 - 16 * h)],
        [b_tail.at[0], b_tail2.at[0]], [b_tail.at[1], b_tail2.at[1]], [b_tail.at[2], b_tail2.at[2]],
    )
    b_y.start()

    for k, index in small_z:
        landed(index, got.at[2 + k])
    for k, index in small_z:
        copies.started[index].wait_send()
    small_out[...] = small_out[...] + (got[3] + got[4] + got[5])
    small_y = [(k, send(small_out, got.at[5 + k], at.at_y(k))) for k in (1, 3, 2)]

    a_z.relay()
    b_y.relay()
    a_out, b_out = out.at[:, left_cols], out.at[:, right_cols]
    a_z.finish(lambda h: uneven(a_out, a_rows + 144 * z, h))
    a_gather = RingGather(
        copies, z, at.at_z(1), at.at_z(3),
        lambda j: a_out.at[rows(a_rows + 144 * j, 144)],
        lambda j, h: uneven(a_out, a_rows + 144 * j, h),
    )
    a_gather.start()
    b_y.finish(lambda h: uneven(b_out, b_rows + 144 * low, h))
    view = b_out.at[rows(b_rows + 144 * low, 144)]
    b_beside = send(view, view, at.beside())

    for k, index in small_y:
        landed(index, got.at[5 + k])
    for k, index in small_y:
        copies.started[index].wait_send()
    small_out[...] = small_out[...] + (got[6] + got[7] + got[8])
    small_c = send(small_out, got.at[9], at.sibling())

    landed(b_beside, b_out.at[rows(b_rows + 144 * (1 - low), 144)])
    b_gather = RingGather(
        copies, z, at.at_z(1), at.at_z(3),
        lambda j: b_out.at[rows(1152 * c + 288 * j, 288)],
        lambda j, h: b_out.at[rows(1152 * c + 288 * j + 144 * h, 144)],
    )
    b_gather.start()
    a_gather.relay()
    a_gather.finish()
    view = a_out.at[rows(a_rows, 576)]
    a_beside = send(view, view, at.beside())
    a_half = send(view, view, at.sibling())
    b_gather.relay()
    landed(small_c, got.at[9])
    copies.started[small_c].wait_send()
    small_out[...] = small_out[...] + got[9]
    outer.finish()
    landed(a_beside, a_out.at[rows(1152 * c + 576 * (1 - low), 576)])
    view = a_out.at[rows(1152 * c + 576 * (1 - low), 576)]
    a_other = send(view, view, at.sibling())
    b_gather.finish()
    view = b_out.at[mine]
    b_all = send(view, view, at.sibling())
    landed(a_half, a_out.at[rows(1152 * (1 - c) + 576 * low, 576)])
    landed(a_other, a_out.at[rows(1152 * (1 - c) + 576 * (1 - low), 576)])
    landed(b_all, b_out.at[theirs])
    waited = {index for _, index in small_z} | {index for _, index in small_y} | {small_c}
    for index, copy in enumerate(copies.started):
        if index not in waited:
            copy.wait_send()


FINAL_COPIES = 64


def final(grads, small, slices):
    vmem = pl.BlockSpec(memory_space=pltpu.VMEM)
    return pl.pallas_call(
        final_kernel,
        out_shape=[
            jax.ShapeDtypeStruct((GRAD_ROWS, WIDTH), bf16),
            jax.ShapeDtypeStruct((2, 8, WIDTH), f32),
            jax.ShapeDtypeStruct((4, BLOCK, WIDTH), bf16),
        ],
        in_specs=[vmem] * 3,
        out_specs=[vmem] * 3,
        scratch_shapes=[
            pltpu.VMEM((2, 1152, WIDTH), bf16),
            pltpu.VMEM((576, 384), bf16),
            pltpu.VMEM((2, 288, 384), bf16),
            pltpu.VMEM((6, 288, 384), bf16),
            pltpu.VMEM((6, 288, 384), bf16),
            pltpu.VMEM((3, 80, 384), bf16),
            pltpu.VMEM((3, 64, 384), bf16),
            pltpu.VMEM((3, 80, 384), bf16),
            pltpu.VMEM((3, 64, 384), bf16),
            pltpu.VMEM((10, 2, 8, WIDTH), f32),
            pltpu.SemaphoreType.DMA((FINAL_COPIES,)),
            pltpu.SemaphoreType.DMA((FINAL_COPIES,)),
            pltpu.SemaphoreType.DMA,
        ],
        compiler_params=pltpu.CompilerParams(
            collective_id=3, has_side_effects=True, vmem_limit_bytes=VMEM_LIMIT
        ),
        name="final",
    )(grads, small, slices)


def normed_of(flat):
    middle = jnp.mean(flat, axis=-1, keepdims=True)
    centred = flat - middle
    inverse = lax.rsqrt(jnp.mean(centred * centred, axis=-1, keepdims=True) + EPS)
    return centred * inverse, inverse


def norm_back(scaled, normed, inverse):
    inner = scaled - jnp.mean(scaled, axis=-1, keepdims=True)
    inner = inner - normed * jnp.mean(scaled * normed, axis=-1, keepdims=True)
    return inner * inverse


def rotate(vector, cosine, sine):
    portion = vector[..., :ROT]
    half = ROT // 2
    turned = jnp.concatenate([-portion[..., half:], portion[..., :half]], axis=-1)
    return jnp.concatenate([portion * cosine + turned * sine, vector[..., ROT:]], axis=-1)


def unrotate(grad, cosine, sine):
    portion = grad[..., :ROT]
    half = ROT // 2
    moved = portion * sine
    back = jnp.concatenate([moved[..., half:], -moved[..., :half]], axis=-1)
    return jnp.concatenate([portion * cosine + back, grad[..., ROT:]], axis=-1)


def swapped(value):
    return lax.ppermute(value, "dp", [(n, n ^ 1) for n in range(16)])


def interleaved(own, other):
    return jnp.concatenate([own[:BLOCK], other[:BLOCK], own[BLOCK:], other[BLOCK:]], axis=0)


def gelu_parts(hidden):
    return jax.nn.gelu(hidden, approximate=False)


SPANS = ((0, BLOCK, 2 * BLOCK), (BLOCK, 2 * BLOCK, 4 * BLOCK))


def forward_layer(flat, w, geometry):
    allowed, cosine, sine = geometry
    scale = HEAD_DIM ** (-0.5)
    normed, inverse = normed_of(flat)
    first = (normed * w["g1"] + w["s1"]).astype(bf16)
    second = (normed * w["g2"] + w["s2"]).astype(bf16)
    packed = jnp.dot(first, w["qkv"], preferred_element_type=f32) + w["qkv_bias"]
    packed = packed.reshape(2 * BLOCK, HEADS, 3, HEAD_DIM)
    query = rotate(packed[:, :, 0], cosine, sine).astype(bf16)
    key = rotate(packed[:, :, 1], cosine, sine).astype(bf16)
    value = packed[:, :, 2].astype(bf16)
    both = jnp.concatenate([key.reshape(-1, INNER), value.reshape(-1, INNER)], axis=1)
    other = swapped(both)
    hidden = jnp.dot(second, w["up"], preferred_element_type=f32) + w["up_bias"]
    active = gelu_parts(hidden).astype(bf16)
    both_all = interleaved(both, other)
    keys = both_all[:, :INNER].reshape(-1, HEADS, HEAD_DIM)
    values = both_all[:, INNER:].reshape(-1, HEADS, HEAD_DIM)
    mixed, logs = [], []
    for (lo, hi, span), allow in zip(SPANS, allowed):
        score = (
            jnp.einsum("qhd,khd->hqk", query[lo:hi], keys[:span], preferred_element_type=f32) * scale
        )
        score = jnp.where(allow[None], score, MASKED)
        top = jnp.max(score, axis=-1, keepdims=True)
        expo = jnp.exp(score - top)
        total = jnp.sum(expo, axis=-1, keepdims=True)
        weights = (expo / total).astype(bf16)
        mixed.append(
            jnp.einsum("hqk,khd->qhd", weights, values[:span], preferred_element_type=f32)
        )
        logs.append(top + jnp.log(total))
    mixed = jnp.concatenate(mixed, axis=0).reshape(2 * BLOCK, INNER).astype(bf16)
    partial = jnp.dot(mixed, w["dense"], preferred_element_type=f32)
    partial = partial + jnp.dot(active, w["down"], preferred_element_type=f32)
    partial = partial.astype(bf16).reshape(2, BLOCK, WIDTH)
    kept = (normed, inverse, first, second, query, keys, values, logs, mixed, hidden, active)
    return partial, kept


def backward_layer(grad_low, w, geometry, kept):
    allowed, cosine, sine = geometry
    scale = HEAD_DIM ** (-0.5)
    normed, inverse, first, second, query, keys, values, logs, mixed, hidden, active = kept
    d_mixed = jnp.einsum("rn,kn->rk", grad_low, w["dense"], preferred_element_type=f32)
    d_mixed = d_mixed.astype(bf16).reshape(2 * BLOCK, HEADS, HEAD_DIM)
    d_query, d_keys, d_values = [], [], []
    for (lo, hi, span), allow, log_total in zip(SPANS, allowed, logs):
        q, dm = query[lo:hi], d_mixed[lo:hi]
        score = jnp.einsum("qhd,khd->hqk", q, keys[:span], preferred_element_type=f32) * scale
        prob = jnp.exp(jnp.where(allow[None], score, MASKED) - log_total)
        prob_low = prob.astype(bf16)
        d_prob = jnp.einsum("qhd,khd->hqk", dm, values[:span], preferred_element_type=f32)
        d_score = prob * (d_prob - jnp.sum(prob * d_prob, axis=-1, keepdims=True))
        d_score = d_score.astype(bf16)
        d_query.append(
            jnp.einsum("hqk,khd->qhd", d_score, keys[:span], preferred_element_type=f32) * scale
        )
        d_keys.append(jnp.einsum("hqk,qhd->khd", d_score, q, preferred_element_type=f32) * scale)
        d_values.append(jnp.einsum("hqk,qhd->khd", prob_low, dm, preferred_element_type=f32))
    d_query = jnp.concatenate(d_query, axis=0)
    halves = []
    for short, long in (d_keys, d_values):
        halves.append(jnp.concatenate([long[: 2 * BLOCK] + short, long[2 * BLOCK :]], axis=0))
    d_both = jnp.concatenate([half.reshape(-1, INNER) for half in halves], axis=1)
    d_both = d_both.reshape(2, 2, BLOCK, 2 * INNER)
    got = swapped(d_both[:, 1].astype(bf16))
    d_active = jnp.einsum("rn,kn->rk", grad_low, w["down"], preferred_element_type=f32)
    d_hidden = jax.vjp(gelu_parts, hidden)[1](d_active)[0]
    d_hidden = d_hidden.astype(bf16)
    d_second = jnp.einsum("rn,kn->rk", d_hidden, w["up"], preferred_element_type=f32)
    d_up = jnp.einsum("rk,rn->kn", second, d_hidden, preferred_element_type=bf16)
    d_dense = jnp.einsum("rk,rn->kn", mixed, grad_low, preferred_element_type=bf16)
    d_down = jnp.einsum("rk,rn->kn", active, grad_low, preferred_element_type=bf16)
    d_both = (d_both[:, 0] + got.astype(f32)).reshape(2 * BLOCK, 2, HEADS, HEAD_DIM)
    d_query = unrotate(d_query, cosine, sine)
    d_key = unrotate(d_both[:, 0], cosine, sine)
    d_packed = jnp.stack([d_query, d_key, d_both[:, 1]], axis=2)
    d_packed = d_packed.reshape(2 * BLOCK, 3 * INNER).astype(bf16)
    d_first = jnp.einsum("rn,kn->rk", d_packed, w["qkv"], preferred_element_type=f32)
    d_qkv = jnp.einsum("rn,rk->nk", d_packed, first, preferred_element_type=bf16)
    scaled = d_first * w["g1"] + d_second * w["g2"]
    scaled = scaled.astype(bf16).reshape(2, BLOCK, WIDTH)
    small = jnp.stack(
        [
            jnp.sum(d_first * normed, axis=0),
            jnp.sum(d_first, axis=0),
            jnp.sum(d_second * normed, axis=0),
            jnp.sum(d_second, axis=0),
            jnp.sum(grad_low.astype(f32), axis=0),
            jnp.sum(d_hidden.astype(f32), axis=0),
            jnp.pad(jnp.sum(d_packed.astype(f32), axis=0), (0, WIDTH - 3 * INNER)),
            jnp.zeros((WIDTH,), f32),
        ]
    )
    grads = jnp.concatenate([d_qkv, d_dense, d_up, d_down], axis=0)
    return scaled, grads, small


def geometry_of(segment_ids):
    at = Place()
    seq = lax.dynamic_slice(segment_ids, (at.y, at.z, 0), (1, 1, SEQ))[0, 0]
    spots = jnp.arange(SEQ, dtype=jnp.int32)
    own = [at.c * BLOCK, (2 + at.c) * BLOCK]
    other = [(1 - at.c) * BLOCK, (3 - at.c) * BLOCK]
    order = [own[0], other[0], own[1], other[1]]
    labels = jnp.concatenate([lax.dynamic_slice(seq, (s,), (BLOCK,)) for s in order])
    places = jnp.concatenate([s + jnp.arange(BLOCK, dtype=jnp.int32) for s in order])
    mine = jnp.concatenate([labels[:BLOCK], labels[2 * BLOCK : 3 * BLOCK]])
    my_places = jnp.concatenate([places[:BLOCK], places[2 * BLOCK : 3 * BLOCK]])
    before = jnp.sum((seq[None, :] < mine[:, None]).astype(jnp.int32), axis=1)
    allowed = []
    for lo, hi, span in SPANS:
        allowed.append(
            (labels[None, :span] == mine[lo:hi, None]) & (places[None, :span] <= my_places[lo:hi, None])
        )
    half = ROT // 2
    freqs = 10000.0 ** (-(2.0 * jnp.arange(half, dtype=f32)) / ROT)
    angles = (my_places - before).astype(f32)[:, None] * freqs
    angles = jnp.concatenate([angles, angles], axis=-1)[:, None, :]
    return allowed, jnp.cos(angles), jnp.sin(angles)


def local(
    boundary,
    segment_ids,
    attn_gain,
    attn_shift,
    mlp_gain,
    mlp_shift,
    qkv_weight,
    qkv_bias,
    dense_weight,
    dense_bias,
    up_weight,
    up_bias,
    down_weight,
    down_bias,
):
    at = Place()
    small = jnp.concatenate(
        [
            attn_gain,
            attn_shift,
            mlp_gain,
            mlp_shift,
            jnp.pad(qkv_bias, ((0, 0), (0, WIDTH - 3 * INNER))),
            up_bias,
            dense_bias + down_bias,
            jnp.zeros((1, WIDTH), f32),
        ]
    )
    xg, wq, wd, wu, wn, smalls = spread(
        boundary[0].astype(bf16), qkv_weight[0], dense_weight[0], up_weight[0], down_weight[0], small
    )
    layers = []
    for n in range(2):
        s = smalls[n]
        layers.append(
            dict(
                g1=s[0], s1=s[1], g2=s[2], s2=s[3], qkv_bias=s[4, : 3 * INNER], up_bias=s[5], extra=s[6],
                qkv=wq[n], dense=wd[n], up=wu[n], down=wn[n],
            )
        )
    geometry = geometry_of(segment_ids)
    flat = xg[0].reshape(2 * BLOCK, WIDTH).astype(f32)
    partial, kept_zero = forward_layer(flat, layers[0], geometry)
    branch = total_over_tensor(partial).reshape(2 * BLOCK, WIDTH).astype(f32)
    middle = flat + (branch + layers[0]["extra"])
    partial_one, kept_one = forward_layer(middle, layers[1], geometry)

    grad = xg[1].reshape(2 * BLOCK, WIDTH)
    scaled, grads_one, small_one = backward_layer(grad, layers[1], geometry, kept_one)
    scaled = total_over_tensor(scaled).reshape(2 * BLOCK, WIDTH).astype(f32)
    grad_zero = grad.astype(f32) + norm_back(scaled, kept_one[0], kept_one[1])
    scaled, grads_zero, small_zero = backward_layer(
        grad_zero.astype(bf16), layers[0], geometry, kept_zero
    )
    sums = pieces_over_tensor(scaled, partial_one).astype(f32)

    def quarter(value):
        value = value.reshape(2, BLOCK, value.shape[-1])
        return lax.dynamic_slice_in_dim(value, 64 * at.x, 64, 1)

    grad_in = quarter(grad_zero) + norm_back(sums[0], quarter(kept_zero[0]), quarter(kept_zero[1]))
    result = quarter(middle) + (sums[1] + layers[1]["extra"])
    slices = jnp.stack([grad_in, result]).astype(bf16)
    total, small_total, back = final(
        jnp.stack([grads_zero, grads_one]), jnp.stack([small_zero, small_one]), slices
    )
    mine = lax.dynamic_index_in_dim(small_total, at.p, 0, keepdims=False)
    total = total.astype(f32)
    d_qkv = total[: 3 * INNER].T
    d_dense = total[3 * INNER : 4 * INNER]
    d_up = total[4 * INNER : 4 * INNER + WIDTH]
    d_down = total[4 * INNER + WIDTH :]
    return (
        back.astype(f32)[None],
        mine[0:1],
        mine[1:2],
        mine[2:3],
        mine[3:4],
        d_qkv[None],
        mine[6:7, : 3 * INNER],
        d_dense[None],
        mine[4:5],
        d_up[None],
        mine[5:6],
        d_down[None],
        mine[4:5],
    )


def solution(mesh):
    in_specs = (
        P("pipe", None, "dp", None),
        P(),
        P("pipe", None),
        P("pipe", None),
        P("pipe", None),
        P("pipe", None),
        P("pipe", None, "tensor"),
        P("pipe", "tensor"),
        P("pipe", "tensor", None),
        P("pipe", None),
        P("pipe", None, "tensor"),
        P("pipe", "tensor"),
        P("pipe", "tensor", None),
        P("pipe", None),
    )
    out_specs = (
        P("pipe", None, "dp", None),
        P("pipe", None),
        P("pipe", None),
        P("pipe", None),
        P("pipe", None),
        P("pipe", None, "tensor"),
        P("pipe", "tensor"),
        P("pipe", "tensor", None),
        P("pipe", None),
        P("pipe", None, "tensor"),
        P("pipe", "tensor"),
        P("pipe", "tensor", None),
        P("pipe", None),
    )
    return jax.shard_map(local, mesh=mesh, in_specs=in_specs, out_specs=out_specs, check_vma=False)
```

time: 843 us -> 458 us (0.54)
  waiting for transfers between devices: 360 us -> 0.01 us
  Pallas kernels: 0 us -> 258 us
  starting transfers between devices: 166 us -> 7.61 us
  matrix products: 131 us -> 69 us
  blocking collectives: 52.4 us -> 0 us
  local copies, waits for them, and re-layouts: 16.6 us -> 59.6 us
  other arithmetic: 85 us -> 55.9 us
  between operations: 20 us -> 2.93 us
    psum x7 -> x0, waiting for transfers between devices: 308 us -> none  [the longest x4 167 us: local(): lax.psum(partial_out.astype(jnp.bfloat16), 'tensor').astype(jnp.float32)]
    pallas_call x0 -> x5, Pallas kernels: none -> 258 us  [the longest x1 130 us: spread(): pl.pallas_call(spread_kernel, out_shape=[jax.ShapeDtypeStruct(s, bf16) fo...]
    ppermute x53 -> x4, starting transfers between devices: 166 us -> 7.61 us  [swapped(): return lax.ppermute(value, 'dp', [(n, n ^ 1) for n in range(16)])]
    dot_general x95 -> x48, matrix products: 131 us -> 69 us  [the longest x2 17.2 us: forward_layer(): hidden = jnp.dot(second, w['up'], preferred_element_type=f32) + w['up_bias']]
    psum x1 -> x0, blocking collectives: 52.4 us -> none  [local(): lax.psum(inner_total[0].astype(jnp.bfloat16), 'dp').astype(jnp.float32)]
    ppermute x53 -> x4, waiting for transfers between devices: 50.9 us -> 0.01 us  [swapped(): return lax.ppermute(value, 'dp', [(n, n ^ 1) for n in range(16)])]
    reduce_sum x31 -> x15, other arithmetic: 34.4 us -> 13.9 us  [the longest x2 3.7 us: norm_back(): inner = scaled - jnp.mean(scaled, axis=-1, keepdims=True)]
    unnamed x533 -> x288, local copies, waits for them, and re-layouts: 8.69 us -> 22.3 us
  transfers between devices with their start and end apart: 60 -> 4, of which waited for: 28 -> 0; matrix products, arithmetic and copies ran while one was open for 17% -> 8% of each run, Pallas kernels for 0% -> 0%
where the time goes in v1:
time: 458 us; the launch traced here: 453 us
  Pallas kernels  258 us (56%)
  matrix products  69 us (15%)
  local copies, waits for them, and re-layouts  59.6 us (13%)
  other arithmetic  55.9 us (12%)
  starting transfers between devices  7.61 us (2%)
    pallas_call x1, Pallas kernels, spread(): pl.pallas_call(spread_kernel, out_shape=[jax.ShapeDtypeStruct(s, bf16) fo...  130 us
    pallas_call x1, Pallas kernels, final(): pl.pallas_call(final_kernel, out_shape=[jax.ShapeDtypeStruct((GRAD_ROWS,...  69 us
    pallas_call x2, Pallas kernels, total_over_tensor(): pl.pallas_call(total_kernel, out_shape=jax.ShapeDtypeStruct((2, BLOCK, WI...  40.4 us
    unnamed x288, local copies, waits for them, and re-layouts  22.3 us
    pallas_call x1, Pallas kernels, pieces_over_tensor(): pl.pallas_call(pieces_kernel, out_shape=jax.ShapeDtypeStruct((2, 2, 64, W...  18.7 us
    dot_general x2, matrix products, forward_layer(): hidden = jnp.dot(second, w['up'], preferred_element_type=f32) + w['up_bias']  17.2 us
  transfers between devices with their start and end apart: 4, of which 0 were waited for; matrix products, arithmetic and copies ran while one was open for 8% of the time, Pallas kernels for 0%

profile of v1, /device:TPU:1, one launch (start us, length us, event | category | flops | bytes accessed | tf_op | source)
XLA Modules:
  0.0 452.7 jit_solution(13425294590759841579)
XLA Ops:
  0.8 2.2 copy.69
  3.0 3.2 convert_bitcast_fusion.2.block
  7.1 129.6 %spread.1 = (bf16[2,2,256,768]{3,2,1,0:T(8,128)(2,1)}, bf16[2,768,576]{2,1,0:T(8,128)(2,1)}, bf16[2,192,768]{2,1,0:T(8,128)(2,1)}, bf16[2,768,768]{2,1,0:T(8,128...) custom-call(bf16[4,256,768]{2,1,0:T(8,128)(2,1)} %convert_bitcast_fusion.2.block, bf16[768,576]{1,0:T(8,128)(2,1)} %bitcast.409, ...), custom_call_target="tpu_custom_call" | custom-call | tf_op jit(solution)/shard_map/spread/pallas_call | solution.py:273
  137.6 1.8 slice_reduce_fusion.1
  151.3 2.0 convert_bitcast_fusion
  155.2 6.5 %multiply_convert_fusion.5 = (bf16[512,768]{1,0:T(8,128)(2,1)}, f32[512,768]{1,0:T(8,128)}, f32[512,768]{1,0:T(8,128)}) fusion(f32[768]{0:T(1024)S(1)} %get-tuple-element.50, bf16[512,768]{1,0:T(8,128)(2,1)S(1)} %bitcast.458, bf16[2,768,768]{2,1,0:T(8,128)(2,1)} %get-tuple-element.26), kind=kOutput, calls=%fused_computation.107 | convolution fusion | flops 629932032 | bytes 5901312 | tf_op jit(solution)/shard_map/dot_general | solution.py:646
  174.2 20.2 %total.2 = bf16[2,256,768]{2,1,0:T(8,128)(2,1)} custom-call(bf16[2,256,768]{2,1,0:T(8,128)(2,1)} %bitcast.452), custom_call_target="tpu_custom_call" | custom-call | tf_op jit(solution)/shard_map/total/pallas_call | solution.py:344
  201.5 2.2 collective-permute-start.1
  203.7 10.6 %multiply_convert_fusion.2 = (bf16[512,768]{1,0:T(8,128)(2,1)S(1)}, f32[512,768]{1,0:T(8,128)S(1)}, f32[512,768]{1,0:T(8,128)S(1)}) fusion(f32[768]{0:T(1024)S(1)} %copy-done.114, bf16[512,768]{1,0:T(8,128)(2,1)S(1)} %bitcast.459, bf16[2,768,768]{2,1,0:T(8,128)(2,1)S(1)} %copy-done.126), kind=kOutput, calls=%fused_computation.74 | convolution fusion | flops 629932032 | bytes 5902336 | tf_op jit(solution)/shard_map/dot_general | solution.py:646
  214.4 2.1 convert_reduce_fusion.3
  217.7 1.8 fusion.222
  236.7 2.7 concatenate.201
  239.5 2.1 pad_maximum_fusion.3
  241.5 2.7 concatenate.199
  247.6 3.0 add_convert_fusion
  251.9 2.7 reshape.984
  261.3 3.4 fusion.198
  264.7 20.1 %total.3 = bf16[2,256,768]{2,1,0:T(8,128)(2,1)} custom-call(bf16[2,256,768]{2,1,0:T(8,128)(2,1)} %bitcast.451), custom_call_target="tpu_custom_call" | custom-call | tf_op jit(solution)/shard_map/total/pallas_call | solution.py:344
  284.9 3.6 convert_reduce_fusion.8
  304.4 3.3 fusion.111
  308.9 1.8 fusion.220
  311.4 2.1 convert_reduce_fusion.4
  318.1 4.2 collective-permute-start.3
  323.0 3.5 maximum_bitcast_fusion.1
  333.7 3.6 fusion.34
  339.6 18.7 %pieces.1 = bf16[2,2,64,768]{3,2,1,0:T(8,128)(2,1)} custom-call(bf16[2,256,768]{2,1,0:T(8,128)(2,1)} %bitcast.460, bf16[2,256,768]{2,1,0:T(8,128)(2,1)} %bitcast.455), custom_call_target="tpu_custom_call" | custom-call | tf_op jit(solution)/shard_map/pieces/pallas_call | solution.py:377
  364.5 1.8 fusion.151
  369.1 3.4 pad_maximum_fusion.grads
  372.6 69.0 %final.1 = (bf16[2304,768]{1,0:T(8,128)(2,1)}, f32[2,8,768]{2,1,0:T(8,128)}, bf16[4,256,768]{2,1,0:T(8,128)(2,1)}) custom-call(bf16[2,2304,768]{2,1,0:T(8,128)(2,1)} %pad_maximum_fusion.grads, f32[2,8,768]{2,1,0:T(8,128)} %pad_maximum_fusion.26.small, bf16[2,2,64,768]{3,2,1,0:T(8,128)(2,1)} %pad_maximum_fusion.11.slices), custom_call_target="tpu_custom_call" | custom-call | tf_op jit(solution)/shard_map/final/pallas_call | solution.py:559
  441.6 2.5 convert_element_type.382
  446.3 2.5 slice_bitcast_fusion
  450.0 1.9 bitcast_convert_fusion
  (490 shorter events, 108.8 us)
Async XLA Ops:
  136.7 7.4 %copy-start = (bf16[2,2,256,768]{3,2,1,0:T(8,128)(2,1)S(1)}, bf16[2,2,256,768]{3,2,1,0:T(8,128)(2,1)}, u32[]{:S(2)}) copy-start(bf16[2,2,256,768]{3,2,1,0:T(8,128)(2,1)} %get-tuple-element.22) | copy-start | bytes 4718596
  139.4 6.1 %copy-start.81 = (f32[768]{0:T(1024)}, f32[768]{0:T(1024)S(1)}, u32[]{:S(2)}) copy-start(f32[768]{0:T(1024)S(1)} %get-tuple-element.51) | copy-start | bytes 9220
  139.4 6.1 %copy-start.83 = (f32[768]{0:T(1024)}, f32[768]{0:T(1024)S(1)}, u32[]{:S(2)}) copy-start(f32[768]{0:T(1024)S(1)} %get-tuple-element.52) | copy-start | bytes 9220
  139.4 6.1 %copy-start.85 = (f32[768]{0:T(1024)}, f32[768]{0:T(1024)S(1)}, u32[]{:S(2)}) copy-start(f32[768]{0:T(1024)S(1)} %get-tuple-element.54) | copy-start | bytes 9220
  141.3 4.2 copy-start.27
  150.2 13.5 %collective-permute-start = (bf16[512,384]{0,1:T(8,128)(2,1)}, bf16[512,384]{0,1:T(8,128)(2,1)}, u32[]{:S(2)}, u32[]{:S(2)}) collective-permute-start(bf16[512,384]{0,1:T(8,128)(2,1)} %pad_maximum_fusion.9), channel_id=1, source_target_pairs={{0,4},{4,0},{8,12},{12,8},{16,20},{20,16},{24,28},{28,24},{32,36},... | collective-permute-start | bytes 1179656 | tf_op jit(solution)/shard_map/ppermute | solution.py:619
  153.3 8.5 %copy-start.11 = (bf16[1,2,256,768]{3,2,1,0:T(8,128)(2,1)}, bf16[1,2,256,768]{3,2,1,0:T(8,128)(2,1)S(1)}, u32[]{:S(2)}) copy-start(bf16[1,2,256,768]{3,2,1,0:T(8,128)(2,1)S(1)} %get-tuple-element.79) | copy-start | bytes 2359300
  153.4 11.5 %copy-start.44 = (pred[256,512]{1,0:T(8,128)(4,1)}, pred[256,512]{1,0:T(8,128)(4,1)S(1)}, u32[]{:S(2)}) copy-start(pred[256,512]{1,0:T(8,128)(4,1)S(1)} %compare_and_fusion.1) | copy-start | bytes 393220
  155.2 7.3 %copy-start.105 = (f32[1,2,2,128]{3,2,1,0:T(2,128)S(1)}, f32[1,2,2,128]{3,2,1,0:T(2,128)}, u32[]{:S(2)}) copy-start(f32[1,2,2,128]{3,2,1,0:T(2,128)} %get-tuple-element.152) | copy-start | bytes 6148
  155.2 7.8 %copy-start.106 = (f32[1,2,2,128]{3,2,1,0:T(2,128)S(1)}, f32[1,2,2,128]{3,2,1,0:T(2,128)}, u32[]{:S(2)}) copy-start(f32[1,2,2,128]{3,2,1,0:T(2,128)} %get-tuple-element.154) | copy-start | bytes 6148
  164.9 5.3 %copy-start.34 = (bf16[1024,192]{0,1:T(8,128)(2,1)}, bf16[1024,192]{0,1:T(8,128)(2,1)S(1)}, u32[]{:S(2)}) copy-start(bf16[1024,192]{0,1:T(8,128)(2,1)S(1)} %get-tuple-element.89) | copy-start | bytes 1179652
  172.5 21.9 %copy-start.68 = (f32[768]{0:T(1024)S(1)}, f32[768]{0:T(1024)}, u32[]{:S(2)}) copy-start(f32[768]{0:T(1024)} %get-tuple-element.49) | copy-start | bytes 9220
  174.2 20.2 %copy-start.1 = (bf16[2,2,256,768]{3,2,1,0:T(8,128)(2,1)S(1)}, bf16[2,2,256,768]{3,2,1,0:T(8,128)(2,1)}, u32[]{:S(2)}) copy-start(bf16[2,2,256,768]{3,2,1,0:T(8,128)(2,1)} %get-tuple-element.22) | copy-start | bytes 4718596
  196.5 20.5 %copy-start.77 = (f32[2,256]{1,0:T(2,128)}, f32[2,256]{1,0:T(2,128)S(1)}, u32[]{:S(2)}) copy-start(f32[2,256]{1,0:T(2,128)S(1)} %get-tuple-element.159) | copy-start | bytes 6148
  199.0 4.7 %copy-start.114 = (f32[768]{0:T(1024)S(1)}, f32[768]{0:T(1024)}, u32[]{:S(2)}) copy-start(f32[768]{0:T(1024)} %get-tuple-element.44) | copy-start | bytes 9220
  199.0 4.7 %copy-start.126 = (bf16[2,768,768]{2,1,0:T(8,128)(2,1)S(1)}, bf16[2,768,768]{2,1,0:T(8,128)(2,1)}, u32[]{:S(2)}) copy-start(bf16[2,768,768]{2,1,0:T(8,128)(2,1)} %get-tuple-element.26) | copy-start | bytes 7077892
  201.5 18.1 %collective-permute-start.1 = (bf16[512,384]{0,1:T(8,128)(2,1)S(1)}, bf16[512,384]{0,1:T(8,128)(2,1)S(1)}, u32[]{:S(2)}, u32[]{:S(2)}) collective-permute-start(bf16[512,384]{0,1:T(8,128)(2,1)S(1)} %pad_maximum_fusion.10), channel_id=1, source_target_pairs={{0,4},{4,0},{8,12},{12,8},{16,20},{20,16},{24,28},{28,24},{32,36},... | collective-permute-start | bytes 1179656 | tf_op jit(solution)/shard_map/ppermute | solution.py:619
  203.7 10.7 %copy-start.12 = (bf16[1,2,256,768]{3,2,1,0:T(8,128)(2,1)S(1)}, bf16[1,2,256,768]{3,2,1,0:T(8,128)(2,1)}, u32[]{:S(2)}) copy-start(bf16[1,2,256,768]{3,2,1,0:T(8,128)(2,1)} %copy-done.11) | copy-start | bytes 2359300
  203.7 10.7 %copy-start.129 = (bf16[2,768,768]{2,1,0:T(8,128)(2,1)S(1)}, bf16[2,768,768]{2,1,0:T(8,128)(2,1)}, u32[]{:S(2)}) copy-start(bf16[2,768,768]{2,1,0:T(8,128)(2,1)} %get-tuple-element.27) | copy-start | bytes 7077892
  246.8 3.8 collective-permute-start.2
  251.9 4.9 %copy-start.52 = (f32[512,16]{0,1:T(8,128)S(1)}, f32[512,16]{0,1:T(8,128)}, u32[]{:S(2)}) copy-start(f32[512,16]{0,1:T(8,128)} %copy-done.50) | copy-start | bytes 98308
  264.7 20.2 %copy-start.73 = (f32[2,256]{1,0:T(2,128)S(1)}, f32[2,256]{1,0:T(2,128)}, u32[]{:S(2)}) copy-start(f32[2,256]{1,0:T(2,128)} %copy-done.72) | copy-start | bytes 6148
  264.7 20.2 %copy-start.78 = (f32[2,256]{1,0:T(2,128)S(1)}, f32[2,256]{1,0:T(2,128)}, u32[]{:S(2)}) copy-start(f32[2,256]{1,0:T(2,128)} %copy-done.77) | copy-start | bytes 6148
  284.9 4.8 %copy-start.8 = (bf16[2,256,768]{2,1,0:T(8,128)(2,1)S(1)}, bf16[2,256,768]{2,1,0:T(8,128)(2,1)}, u32[]{:S(2)}) copy-start(bf16[2,256,768]{2,1,0:T(8,128)(2,1)} %total.3) | copy-start | bytes 2359300
  316.2 6.1 %copy-start.75 = (f32[1,768]{1,0:T(1,128)S(1)}, f32[1,768]{1,0:T(1,128)}, u32[]{:S(2)}) copy-start(f32[1,768]{1,0:T(1,128)} %copy-done.74) | copy-start | bytes 9220
  316.2 6.1 %copy-start.96 = (f32[1,768]{1,0:T(1,128)S(1)}, f32[1,768]{1,0:T(1,128)}, u32[]{:S(2)}) copy-start(f32[1,768]{1,0:T(1,128)} %stack.124) | copy-start | bytes 9220
  316.2 6.1 %copy-start.97 = (f32[1,768]{1,0:T(1,128)S(1)}, f32[1,768]{1,0:T(1,128)}, u32[]{:S(2)}) copy-start(f32[1,768]{1,0:T(1,128)} %stack.125) | copy-start | bytes 9220
  316.2 6.8 %copy-start.41 = (bf16[192,768]{1,0:T(8,128)(2,1)S(1)}, bf16[192,768]{1,0:T(8,128)(2,1)}, u32[]{:S(2)}) copy-start(bf16[192,768]{1,0:T(8,128)(2,1)} %fusion.152) | copy-start | bytes 884740
  318.1 8.4 %collective-permute-start.3 = (bf16[2,256,384]{1,0,2:T(2,128)(2,1)S(1)}, bf16[2,256,384]{1,0,2:T(2,128)(2,1)}, u32[]{:S(2)}, u32[]{:S(2)}) collective-permute-start(bf16[2,256,384]{1,0,2:T(2,128)(2,1)S(1)} %fusion.119), channel_id=1, source_target_pairs={{0,4},{4,0},{8,12},{12,8},{16,20},{20,16},{24,28},{28,24},{32,36},... | collective-permute-start | bytes 1179656 | tf_op jit(solution)/shard_map/ppermute | solution.py:619
  339.6 20.0 %copy-start.14 = (f32[2,256,768]{2,1,0:T(8,128)S(1)}, f32[2,256,768]{2,1,0:T(8,128)}, u32[]{:S(2)}) copy-start(f32[2,256,768]{2,1,0:T(8,128)} %get-tuple-element.78) | copy-start | bytes 4718596
  339.6 20.0 %copy-start.101 = (f32[2,64]{1,0:T(2,128)S(1)}, f32[2,64]{1,0:T(2,128)}, u32[]{:S(2)}) copy-start(f32[2,64]{1,0:T(2,128)} %get-tuple-element.190) | copy-start | bytes 1540
  339.6 20.0 %copy-start.102 = (f32[2,64]{1,0:T(2,128)S(1)}, f32[2,64]{1,0:T(2,128)}, u32[]{:S(2)}) copy-start(f32[2,64]{1,0:T(2,128)} %get-tuple-element.191) | copy-start | bytes 1540
  (114 other events, 228.4 us)

commit v2 on v1

v2 whole, which is shorter than its diff:
```python
import functools

import jax
import jax.numpy as jnp
from jax import lax
from jax.experimental import pallas as pl
from jax.experimental.pallas import tpu as pltpu
from jax.sharding import PartitionSpec as P

MESH = pl.DeviceIdType.MESH
HEAD_DIM = 64
ROT = 16
EPS = 1e-05
MASKED = -1e30
WIDTH = 768
SEQ = 1024
BLOCK = 256
HEADS = 3
INNER = HEADS * HEAD_DIM
GRAD_ROWS = 2304
bf16 = jnp.bfloat16
f32 = jnp.float32
VMEM_LIMIT = 56 * 1024 * 1024


class Place:
    def __init__(self):
        self.p = lax.axis_index("pipe")
        self.d = lax.axis_index("dp")
        self.x = lax.axis_index("tensor")
        self.z = self.d // 4
        self.low = (self.d // 2) % 2
        self.c = self.d % 2
        self.y = 2 * self.p + self.low

    def at_x(self, steps):
        return (self.p, self.d, (self.x + steps) % 4)

    def at_y(self, steps):
        y = (self.y + steps) % 4
        return (y // 2, self.z * 4 + (y % 2) * 2 + self.c, self.x)

    def at_z(self, steps):
        return (self.p, ((self.z + steps) % 4) * 4 + self.d % 4, self.x)

    def sibling(self):
        return (self.p, self.d + 1 - 2 * self.c, self.x)

    def partner(self):
        return (1 - self.p, self.z * 4 + (1 - self.low) * 2 + self.c, self.x)

    def beside(self):
        return (self.p, self.z * 4 + (1 - self.low) * 2 + self.c, self.x)


def greet(devices):
    barrier = pltpu.get_barrier_semaphore()
    for device in devices:
        pl.semaphore_signal(barrier, inc=1, device_id=device, device_id_type=MESH)
    pl.semaphore_wait(barrier, len(devices))


class Copies:
    def __init__(self, send_sems, recv_sems, somebody):
        self.send_sems, self.recv_sems = send_sems, recv_sems
        self.somebody = somebody
        self.count = 0
        self.started = []

    def send(self, src, dst, device):
        k = self.count
        self.count += 1
        copy = pltpu.make_async_remote_copy(
            src_ref=src,
            dst_ref=dst,
            send_sem=self.send_sems.at[k],
            recv_sem=self.recv_sems.at[k],
            device_id=device,
            device_id_type=MESH,
        )
        copy.start()
        self.started.append(copy)
        return k

    def landed(self, k, dst):
        pltpu.make_async_remote_copy(
            src_ref=dst,
            dst_ref=dst,
            send_sem=self.send_sems.at[k],
            recv_sem=self.recv_sems.at[k],
            device_id=self.somebody,
            device_id_type=MESH,
        ).wait_recv()

    def drain(self):
        for copy in self.started:
            copy.wait_send()


class RingSum:
    def __init__(self, copies, me, right, left, chunk, relay, direct, final):
        self.copies, self.me, self.right, self.left = copies, me, right, left
        self.chunk, self.relay_in, self.direct, self.final = chunk, relay, direct, final

    def start(self):
        me, send = self.me, self.copies.send
        far, after, before = (me + 2) % 4, (me + 1) % 4, (me + 3) % 4
        self.k = [
            send(self.chunk(far, 0), self.relay_in[0], self.right),
            send(self.chunk(far, 1), self.relay_in[1], self.left),
            send(self.chunk(after, 1), self.direct[1], self.right),
            send(self.chunk(before, 0), self.direct[0], self.left),
        ]

    def relay(self):
        me, copies = self.me, self.copies
        after, before = (me + 1) % 4, (me + 3) % 4
        copies.landed(self.k[0], self.relay_in[0])
        add_into(self.relay_in[0], self.chunk(after, 0))
        k0 = copies.send(self.relay_in[0], self.final[0], self.right)
        copies.landed(self.k[1], self.relay_in[1])
        add_into(self.relay_in[1], self.chunk(before, 1))
        k1 = copies.send(self.relay_in[1], self.final[1], self.left)
        self.k += [k0, k1]

    def finish(self, out):
        copies = self.copies
        copies.landed(self.k[3], self.direct[0])
        copies.landed(self.k[4], self.final[0])
        store_sum(out(0), self.chunk(self.me, 0), self.direct[0], self.final[0])
        copies.landed(self.k[2], self.direct[1])
        copies.landed(self.k[5], self.final[1])
        store_sum(out(1), self.chunk(self.me, 1), self.direct[1], self.final[1])


class RingGather:
    def __init__(self, copies, me, right, left, piece, halves):
        self.copies, self.me, self.right, self.left = copies, me, right, left
        self.piece, self.halves = piece, halves

    def start(self):
        mine = self.piece(self.me)
        self.k = [
            self.copies.send(mine, mine, self.right),
            self.copies.send(mine, mine, self.left),
        ]

    def relay(self):
        before, after = (self.me + 3) % 4, (self.me + 1) % 4
        self.copies.landed(self.k[0], self.piece(before))
        view = self.halves(before, 0)
        k0 = self.copies.send(view, view, self.right)
        self.copies.landed(self.k[1], self.piece(after))
        view = self.halves(after, 1)
        k1 = self.copies.send(view, view, self.left)
        self.k += [k0, k1]

    def finish(self):
        far = (self.me + 2) % 4
        self.copies.landed(self.k[2], self.halves(far, 0))
        self.copies.landed(self.k[3], self.halves(far, 1))


def add_into(ref, other):
    ref[...] = (ref[...].astype(f32) + other[...].astype(f32)).astype(ref.dtype)


def store_sum(out, *parts):
    total = parts[0][...].astype(f32)
    for part in parts[1:]:
        total = total + part[...].astype(f32)
    out[...] = total.astype(out.dtype)


def rows(start, size, step=16):
    return pl.ds(pl.multiple_of(start, step), size)


def spread_kernel(
    block, wq, wd, wu, wn, small, xg, oq, od, ou, on, osm,
    hold_x, hold_s, hold_q, hold_d, hold_u, hold_n, send_sems, recv_sems, local_sems,
):
    at = Place()
    p, x, y, z, c = at.p, at.x, at.y, at.z, at.c
    greet(
        [at.at_x(1), at.at_x(3), at.at_y(1), at.at_y(2), at.at_y(3), at.at_z(1), at.at_z(3), at.sibling()]
    )
    copies = Copies(send_sems, recv_sems, at.at_x(1))
    weights = [(wq, oq), (wd, od), (wu, ou), (wn, on)]

    def piece(ref, zz, cc):
        if ref.shape[-2] == WIDTH:
            return ref.at[rows(192 * zz + 96 * cc, 96)]
        each = ref.shape[-2] // 4
        return ref.at[rows(each * zz, each), pl.ds(pl.multiple_of(384 * cc, 128), 384)]

    def half(ref, zz, cc, h):
        if ref.shape[-2] == WIDTH:
            return ref.at[rows(192 * zz + 96 * cc + 48 * h, 48)]
        each = ref.shape[-2] // 4
        more = (each // 2 + 15) // 16 * 16
        size = each - more if h else more
        return ref.at[rows(each * zz + more * h, size), pl.ds(pl.multiple_of(384 * cc, 128), 384)]

    quarter = rows(64 * x, 64)
    first = [
        copies.send(block.at[(y + k) % 4, quarter], xg.at[p, at.low, quarter], at.at_y(k)) for k in (1, 3, 2)
    ]
    sent = [
        copies.send(piece(src, z, c), piece(dst.at[p], z, c), at.partner()) for src, dst in weights
    ]
    sent_small = copies.send(small, osm.at[p], at.partner())
    held = [hold_x, hold_s, hold_q, hold_d, hold_u, hold_n]
    kept = [(block.at[y], xg.at[p, at.low]), (small, osm.at[p])] + [(s, d.at[p]) for s, d in weights]
    inward = [
        pltpu.make_async_copy(src, hold, local_sems.at[n]) for n, ((src, _), hold) in enumerate(zip(kept, held))
    ]
    for copy in inward:
        copy.start()
    outward = []
    for n, ((_, dst), hold) in enumerate(zip(kept, held)):
        inward[n].wait()
        copy = pltpu.make_async_copy(hold, dst, local_sems.at[n + 6])
        copy.start()
        outward.append(copy)
    gathers = []
    for k, index in zip((1, 3, 2), first):
        source = (y + 4 - k) % 4
        slot = xg.at[source // 2, source % 2]
        copies.landed(index, slot.at[quarter])
        gather = RingGather(
            copies,
            x,
            at.at_x(1),
            at.at_x(3),
            lambda j, slot=slot: slot.at[rows(64 * j, 64)],
            lambda j, h, slot=slot: slot.at[rows(64 * j + 32 * h, 32)],
        )
        gather.start()
        gathers.append(gather)
    others = [dst.at[1 - p] for _, dst in weights]
    rings, shared = [], []
    for other, index in zip(others, sent):
        copies.landed(index, piece(other, z, c))
        ring = RingGather(
            copies,
            z,
            at.at_z(1),
            at.at_z(3),
            lambda j, other=other: piece(other, j, c),
            lambda j, h, other=other: half(other, j, c, h),
        )
        ring.start()
        rings.append(ring)
        mine = piece(other, z, c)
        shared.append((copies.send(mine, mine, at.sibling()), piece(other, z, 1 - c)))
    for gather in gathers:
        gather.relay()
    for other, ring in zip(others, rings):
        ring.relay()
        for j in ((z + 3) % 4, (z + 1) % 4):
            mine = piece(other, j, c)
            shared.append((copies.send(mine, mine, at.sibling()), piece(other, j, 1 - c)))
    for gather in gathers:
        gather.finish()
    for other, ring in zip(others, rings):
        ring.finish()
        j = (z + 2) % 4
        mine = piece(other, j, c)
        shared.append((copies.send(mine, mine, at.sibling()), piece(other, j, 1 - c)))
    copies.landed(sent_small, osm.at[1 - p])
    for index, view in shared:
        copies.landed(index, view)
    for copy in outward:
        copy.wait()
    copies.drain()


SPREAD_COPIES = 3 + 4 + 1 + 12 + 16 + 16


def spread(block, wq, wd, wu, wn, small):
    any_space = pl.BlockSpec(memory_space=pl.ANY)
    shapes = [(2, 2, BLOCK, WIDTH)] + [(2,) + w.shape for w in (wq, wd, wu, wn)]
    return pl.pallas_call(
        spread_kernel,
        out_shape=[jax.ShapeDtypeStruct(s, bf16) for s in shapes]
        + [jax.ShapeDtypeStruct((2,) + small.shape, f32)],
        in_specs=[any_space] * 6,
        out_specs=[any_space] * 6,
        scratch_shapes=[
            pltpu.VMEM((BLOCK, WIDTH), bf16),
            pltpu.VMEM(small.shape, f32),
        ]
        + [pltpu.VMEM(w.shape, bf16) for w in (wq, wd, wu, wn)]
        + [
            pltpu.SemaphoreType.DMA((SPREAD_COPIES,)),
            pltpu.SemaphoreType.DMA((SPREAD_COPIES,)),
            pltpu.SemaphoreType.DMA((12,)),
        ],
        compiler_params=pltpu.CompilerParams(
            collective_id=0, has_side_effects=True, vmem_limit_bytes=VMEM_LIMIT
        ),
        name="spread",
    )(block, wq, wd, wu, wn, small)


def x_sums(at, copies, parts, bufs):
    sums = []
    for n, part in enumerate(parts):
        sums.append(
            RingSum(
                copies,
                at.x,
                at.at_x(1),
                at.at_x(3),
                lambda j, h, part=part: part.at[h, rows(64 * j, 64)],
                [bufs.at[n, 0], bufs.at[n, 1]],
                [bufs.at[n, 2], bufs.at[n, 3]],
                [bufs.at[n, 4], bufs.at[n, 5]],
            )
        )
    return sums


SPLITS = 2


def total_kernel(part, out, bufs, send_sems, recv_sems):
    at = Place()
    greet([at.at_x(1), at.at_x(3)])
    copies = Copies(send_sems, recv_sems, at.at_x(1))
    wide = WIDTH // SPLITS
    cols = [pl.ds(n * wide, wide) for n in range(SPLITS)]
    sums = x_sums(at, copies, [part.at[:, :, col] for col in cols], bufs)
    for ring in sums:
        ring.start()
    for ring in sums:
        ring.relay()
    gathers = []
    for ring, col in zip(sums, cols):
        ring.finish(lambda h, col=col: out.at[h, rows(64 * at.x, 64), col])
        gather = RingGather(
            copies,
            at.x,
            at.at_x(1),
            at.at_x(3),
            lambda j, col=col: out.at[:, rows(64 * j, 64), col],
            lambda j, h, col=col: out.at[h, rows(64 * j, 64), col],
        )
        gather.start()
        gathers.append(gather)
    for gather in gathers:
        gather.relay()
    for gather in gathers:
        gather.finish()
    copies.drain()


def total_over_tensor(part):
    vmem = pl.BlockSpec(memory_space=pltpu.VMEM)
    count = SPLITS * 10
    return pl.pallas_call(
        total_kernel,
        out_shape=jax.ShapeDtypeStruct((2, BLOCK, WIDTH), bf16),
        in_specs=[vmem],
        out_specs=vmem,
        scratch_shapes=[
            pltpu.VMEM((SPLITS, 6, 64, WIDTH // SPLITS), bf16),
            pltpu.SemaphoreType.DMA((count,)),
            pltpu.SemaphoreType.DMA((count,)),
        ],
        compiler_params=pltpu.CompilerParams(
            collective_id=1, has_side_effects=True, vmem_limit_bytes=VMEM_LIMIT
        ),
        name="total",
    )(part)


def final_kernel(
    f_zero, e_zero, f_one, e_one, sf_zero, se_zero, sf_one, se_one,
    scaled, branch, grad, normed, inverse, middle, params, out, small_out, back,
    chip, own_half, a_one, b_one, a_bufs, b_bufs, a_tail, a_tail2, b_tail, b_tail2, got, first_small, x_bufs, x_sum,
    slices, send_sems, recv_sems, local_sem, half_sems,
):
    at = Place()
    x, y, z, c, low = at.x, at.y, at.z, at.c, at.low
    greet(
        [at.at_x(k) for k in (1, 2, 3)]
        + [at.at_y(k) for k in (1, 2, 3)]
        + [at.at_z(k) for k in (1, 2, 3)]
        + [at.sibling()]
    )
    copies = Copies(send_sems, recv_sems, at.at_x(1))
    send, landed = copies.send, copies.landed
    left_cols, right_cols = pl.ds(0, 384), pl.ds(384, 384)
    quarter = rows(64 * x, 64)
    mine, theirs = rows(1152 * c, 1152), rows(1152 * (1 - c), 1152)

    layers = ((f_zero, e_zero), (f_one, e_one))
    parts = [(0, 288, 0), (1, 864, 288)]
    core, halves = {}, []
    for cols in (left_cols, right_cols):
        for layer in range(2):
            for which, size, place in parts:
                src = layers[layer][which].at[rows(size * (1 - c), size), cols]
                index = send(src, chip.at[layer, pl.ds(place, size), cols], at.sibling())
                core[cols is right_cols, layer, which] = index
    for layer in range(2):
        for which, size, place in parts:
            copy = pltpu.make_async_copy(
                layers[layer][which].at[rows(size * c, size)],
                own_half.at[layer, pl.ds(place, size)],
                half_sems.at[2 * layer + which],
            )
            copy.start()
            halves.append(copy)
    last = x_sums(at, copies, [scaled, branch], x_bufs)
    for ring in last:
        ring.start()
    for layer, refs in enumerate(((sf_zero, se_zero), (sf_one, se_one))):
        for which, ref in enumerate(refs):
            first_small[layer, pl.ds(8 * which, 8)] = ref[...]
    small_x = [(k, send(first_small, got.at[k - 1], at.at_x(k))) for k in (1, 3, 2)]
    for copy in halves:
        copy.wait()

    def add_core(cols):
        for layer in range(2):
            for which, size, place in parts:
                landed(core[cols is right_cols, layer, which], chip.at[layer, pl.ds(place, size), cols])

        def body(i, carry):
            here = rows(i * 128, 128)
            for layer in range(2):
                chip[layer, here, cols] = (
                    chip[layer, here, cols].astype(f32) + own_half[layer, here, cols].astype(f32)
                ).astype(bf16)
            return carry

        lax.fori_loop(0, 9, body, 0)

    add_core(left_cols)
    a_y = RingSum(
        copies, y, at.at_y(1), at.at_y(3),
        lambda j, h: chip.at[j // 2, rows(576 * (j % 2) + 288 * h, 288), left_cols],
        [a_bufs.at[0], a_bufs.at[1]], [a_bufs.at[2], a_bufs.at[3]], [a_bufs.at[4], a_bufs.at[5]],
    )
    a_y.start()
    add_core(right_cols)
    b_z = RingSum(
        copies, z, at.at_z(1), at.at_z(3),
        lambda j, h: chip.at[h, rows(288 * j, 288), right_cols],
        [b_bufs.at[0], b_bufs.at[1]], [b_bufs.at[2], b_bufs.at[3]], [b_bufs.at[4], b_bufs.at[5]],
    )
    b_z.start()

    for ring in last:
        ring.relay()
    for n, ring in enumerate(last):
        ring.finish(lambda h, n=n: x_sum.at[n, h])
    for h in range(2):
        here = rows(256 * h + 64 * x, 64)
        value = grad[here] + norm_back(x_sum[0, h], normed[here], inverse[here, 0:1])
        slices[0, h] = value.astype(bf16)
        slices[1, h] = (middle[here] + (x_sum[1, h] + params[1, 8:9])).astype(bf16)
    home = []
    for k in (1, 3, 2):
        j = (y + k) % 4
        home.append((k, send(slices.at[j // 2, j % 2], back.at[y, quarter], at.at_y(k))))
    own = pltpu.make_async_copy(slices.at[y // 2, y % 2], back.at[y, quarter], local_sem)
    own.start()
    for k, index in small_x:
        landed(index, got.at[k - 1])
    of_norms = lax.broadcasted_iota(jnp.int32, first_small.shape, 1) % 8 < 2
    others = got[0] + got[1] + got[2]
    small_out[...] = first_small[...] + jnp.where(of_norms, others, 0.0)
    small_z = [(k, send(small_out, got.at[2 + k], at.at_z(k))) for k in (1, 3, 2)]

    a_y.relay()
    b_z.relay()
    own.wait()
    for k, index in home:
        landed(index, back.at[(y + 4 - k) % 4, quarter])
    outer = RingGather(
        copies, x, at.at_x(1), at.at_x(3),
        lambda j: back.at[:, rows(64 * j, 64)],
        lambda j, h: back.at[pl.ds(2 * h, 2), rows(64 * j, 64)],
    )
    outer.start()
    a_y.finish(lambda h: a_one.at[pl.ds(288 * h, 288)])

    def uneven(ref, start, h):
        return ref.at[rows(start + 80 * h, 80 - 16 * h)]

    a_rows = 1152 * c + 576 * low
    a_z = RingSum(
        copies, z, at.at_z(1), at.at_z(3),
        lambda j, h: uneven(a_one, 144 * j, h),
        [a_tail.at[0], a_tail2.at[0]], [a_tail.at[1], a_tail2.at[1]], [a_tail.at[2], a_tail2.at[2]],
    )
    a_z.start()
    b_z.finish(lambda h: b_one.at[h])
    b_rows = 1152 * c + 288 * z
    b_y = RingSum(
        copies, y, at.at_y(1), at.at_y(3),
        lambda j, h: b_one.at[j // 2, rows(144 * (j % 2) + 80 * h, 80 - 16 * h)],
        [b_tail.at[0], b_tail2.at[0]], [b_tail.at[1], b_tail2.at[1]], [b_tail.at[2], b_tail2.at[2]],
    )
    b_y.start()

    for k, index in small_z:
        landed(index, got.at[2 + k])
    for k, index in small_z:
        copies.started[index].wait_send()
    small_out[...] = small_out[...] + (got[3] + got[4] + got[5])
    small_y = [(k, send(small_out, got.at[5 + k], at.at_y(k))) for k in (1, 3, 2)]

    a_z.relay()
    b_y.relay()
    outer.relay()
    a_out, b_out = out.at[:, left_cols], out.at[:, right_cols]
    a_z.finish(lambda h: uneven(a_out, a_rows + 144 * z, h))
    a_gather = RingGather(
        copies, z, at.at_z(1), at.at_z(3),
        lambda j: a_out.at[rows(a_rows + 144 * j, 144)],
        lambda j, h: uneven(a_out, a_rows + 144 * j, h),
    )
    a_gather.start()
    b_y.finish(lambda h: uneven(b_out, b_rows + 144 * low, h))
    view = b_out.at[rows(b_rows + 144 * low, 144)]
    b_beside = send(view, view, at.beside())

    for k, index in small_y:
        landed(index, got.at[5 + k])
    for k, index in small_y:
        copies.started[index].wait_send()
    small_out[...] = small_out[...] + (got[6] + got[7] + got[8])
    small_c = send(small_out, got.at[9], at.sibling())

    landed(b_beside, b_out.at[rows(b_rows + 144 * (1 - low), 144)])
    b_gather = RingGather(
        copies, z, at.at_z(1), at.at_z(3),
        lambda j: b_out.at[rows(1152 * c + 288 * j, 288)],
        lambda j, h: b_out.at[rows(1152 * c + 288 * j + 144 * h, 144)],
    )
    b_gather.start()
    a_gather.relay()
    a_gather.finish()
    view = a_out.at[rows(a_rows, 576)]
    a_beside = send(view, view, at.beside())
    a_half = send(view, view, at.sibling())
    b_gather.relay()
    landed(small_c, got.at[9])
    copies.started[small_c].wait_send()
    small_out[...] = small_out[...] + got[9]
    outer.finish()
    landed(a_beside, a_out.at[rows(1152 * c + 576 * (1 - low), 576)])
    view = a_out.at[rows(1152 * c + 576 * (1 - low), 576)]
    a_other = send(view, view, at.sibling())
    b_gather.finish()
    view = b_out.at[mine]
    b_all = send(view, view, at.sibling())
    landed(a_half, a_out.at[rows(1152 * (1 - c) + 576 * low, 576)])
    landed(a_other, a_out.at[rows(1152 * (1 - c) + 576 * (1 - low), 576)])
    landed(b_all, b_out.at[theirs])
    waited = {index for _, index in small_z} | {index for _, index in small_y} | {small_c}
    for index, copy in enumerate(copies.started):
        if index not in waited:
            copy.wait_send()


FINAL_COPIES = 80


def final(grads, small, last):
    vmem = pl.BlockSpec(memory_space=pltpu.VMEM)
    return pl.pallas_call(
        final_kernel,
        out_shape=[
            jax.ShapeDtypeStruct((GRAD_ROWS, WIDTH), bf16),
            jax.ShapeDtypeStruct((2, 16, WIDTH), f32),
            jax.ShapeDtypeStruct((4, BLOCK, WIDTH), bf16),
        ],
        in_specs=[pl.BlockSpec(memory_space=pl.ANY)] * 4 + [vmem] * 11,
        out_specs=[vmem] * 3,
        scratch_shapes=[
            pltpu.VMEM((2, 1152, WIDTH), bf16),
            pltpu.VMEM((2, 1152, WIDTH), bf16),
            pltpu.VMEM((576, 384), bf16),
            pltpu.VMEM((2, 288, 384), bf16),
            pltpu.VMEM((6, 288, 384), bf16),
            pltpu.VMEM((6, 288, 384), bf16),
            pltpu.VMEM((3, 80, 384), bf16),
            pltpu.VMEM((3, 64, 384), bf16),
            pltpu.VMEM((3, 80, 384), bf16),
            pltpu.VMEM((3, 64, 384), bf16),
            pltpu.VMEM((10, 2, 16, WIDTH), f32),
            pltpu.VMEM((2, 16, WIDTH), f32),
            pltpu.VMEM((2, 6, 64, WIDTH), bf16),
            pltpu.VMEM((2, 2, 64, WIDTH), f32),
            pltpu.VMEM((2, 2, 64, WIDTH), bf16),
            pltpu.SemaphoreType.DMA((FINAL_COPIES,)),
            pltpu.SemaphoreType.DMA((FINAL_COPIES,)),
            pltpu.SemaphoreType.DMA,
            pltpu.SemaphoreType.DMA((4,)),
        ],
        compiler_params=pltpu.CompilerParams(
            collective_id=3, has_side_effects=True, vmem_limit_bytes=VMEM_LIMIT
        ),
        name="final",
    )(*grads, *small, *last)


def nn(a, b):
    return lax.dot_general(a, b, (((1,), (0,)), ((), ())), preferred_element_type=f32)


def nt(a, b):
    return lax.dot_general(a, b, (((1,), (1,)), ((), ())), preferred_element_type=f32)


def tn(a, b):
    return lax.dot_general(a, b, (((0,), (0,)), ((), ())), preferred_element_type=f32)


def turner():
    c = lax.broadcasted_iota(jnp.int32, (INNER, INNER), 0)
    r = lax.broadcasted_iota(jnp.int32, (INNER, INNER), 1)
    lane = c % HEAD_DIM
    half = ROT // 2
    minus = (lane < half) & (r == c + half)
    plus = (lane >= half) & (lane < ROT) & (r == c - half)
    return jnp.where(plus, 1.0, jnp.where(minus, -1.0, 0.0)).astype(bf16)


def head_lanes(shape, h):
    lane = lax.broadcasted_iota(jnp.int32, shape, len(shape) - 1)
    return (lane >= h * HEAD_DIM) & (lane < (h + 1) * HEAD_DIM)


def pick(value, h):
    return jnp.where(head_lanes(value.shape, h), value, jnp.zeros_like(value))


def chunk_rows(i):
    return pl.ds(pl.multiple_of(i * BLOCK, BLOCK), BLOCK)


def front_kernel(later, *refs):
    if later:
        x_ref, add_ref, wq, small, cos, sin, x_out, n_out, inv_out, first_out, second_out, q_out, kv_out, wt = refs
    else:
        x_ref, wq, small, cos, sin, n_out, inv_out, first_out, second_out, q_out, kv_out, wt = refs
    turn = turner()
    for i in range(2):
        wt[INNER * i : INNER * (i + 1)] = nn(turn, wq[0, INNER * i : INNER * (i + 1)]).astype(bf16)

    def row(i, wide=WIDTH):
        return small[0, i : i + 1, :wide]

    def body(i, carry):
        here = chunk_rows(i)
        if later:
            x = x_ref[here] + (add_ref[here].astype(f32) + row(8))
            x_out[here] = x
        else:
            x = x_ref[0, i].astype(f32)
        centred = x - jnp.mean(x, axis=-1, keepdims=True)
        inverse = lax.rsqrt(jnp.mean(centred * centred, axis=-1, keepdims=True) + EPS)
        normed = centred * inverse
        n_out[here] = normed
        inv_out[here] = jnp.broadcast_to(inverse, (BLOCK, 128))
        first = (normed * row(0) + row(1)).astype(bf16)
        first_out[here] = first
        second_out[here] = (normed * row(2) + row(3)).astype(bf16)
        cosine, sine = cos[here], sin[here]
        query = (nt(first, wq[0, :INNER]) + row(4, INNER)) * cosine
        query = query + (nt(first, wt[:INNER]) + row(9, INNER)) * sine
        q_out[here] = (query * HEAD_DIM ** (-0.5)).astype(bf16)
        key = (nt(first, wq[0, INNER : 2 * INNER]) + row(5, INNER)) * cosine
        key = key + (nt(first, wt[INNER:]) + row(10, INNER)) * sine
        kv_out[0, here] = key.astype(bf16)
        kv_out[1, here] = (nt(first, wq[0, 2 * INNER :]) + row(6, INNER)).astype(bf16)
        return carry

    lax.fori_loop(0, 2, body, 0)


def feed_kernel(second, up, small, active_out, slope_out):
    def body(i, carry):
        here = pl.ds(pl.multiple_of(i * 128, 128), 128)
        hidden = nn(second[here], up[0]) + small[0, 7:8]
        below = 0.5 + 0.5 * lax.erf(hidden * (0.5**0.5))
        active_out[here] = (hidden * below).astype(bf16)
        density = jnp.exp(-0.5 * hidden * hidden) * 0.3989422804014327
        slope_out[here] = (below + hidden * density).astype(bf16)
        return carry

    lax.fori_loop(0, 4, body, 0)


def gather_keys(own, other, keys, values):
    for n, ref in enumerate((keys, values)):
        ref[0:BLOCK] = own[n, 0:BLOCK]
        ref[BLOCK : 2 * BLOCK] = other[n, 0:BLOCK]
        ref[2 * BLOCK : 3 * BLOCK] = own[n, BLOCK : 2 * BLOCK]
        ref[3 * BLOCK : 4 * BLOCK] = other[n, BLOCK : 2 * BLOCK]


def key_places(c, shape, dim, blocks):
    i = lax.broadcasted_iota(jnp.int32, shape, dim)
    place = jnp.where(i < BLOCK, i + BLOCK * c, i - BLOCK * c)
    if blocks == 4:
        late = jnp.where(i < 3 * BLOCK, i + BLOCK * c, i - BLOCK * c)
        place = jnp.where(i < 2 * BLOCK, place, late)
    return place


SPANS = ((0, 2), (1, 4))


def mix_kernel(q, own, other, active, dense, down, starts, part_out, mixed_out, log_out, keys, values, logs, bias):
    c = lax.axis_index("dp") % 2
    gather_keys(own, other, keys, values)
    logs[...] = jnp.zeros_like(logs)
    for block, span in SPANS:
        here, n = pl.ds(block * BLOCK, BLOCK), span * BLOCK
        place = key_places(c, (BLOCK, n), 1, span)
        mine = lax.broadcasted_iota(jnp.int32, (BLOCK, n), 0) + (2 * block + c) * BLOCK
        allowed = (place <= mine) & (place >= starts[here])
        bias[:, :n] = jnp.where(allowed, 0.0, MASKED)
        query = q[here]
        mixed = jnp.zeros((BLOCK, INNER), f32)
        for h in range(HEADS):
            score = nt(pick(query, h), keys[:n]) + bias[:, :n]
            top = jnp.max(score, axis=-1, keepdims=True)
            expo = jnp.exp(score - top)
            total = jnp.sum(expo, axis=-1, keepdims=True)
            logs[here, h : h + 1] = top + jnp.log(total)
            mixed = mixed + pick(nn(expo.astype(bf16), values[:n]) * (1.0 / total), h)
        mixed = mixed.astype(bf16)
        mixed_out[here] = mixed
        part = nn(mixed, dense[0]) + nn(active[here], down[0])
        part_out[block] = part.astype(bf16)
    log_out[...] = logs[...].T


def back_mix_kernel(later, *refs):
    if later:
        (g_ref, q, own, other, mixed, log, dense, starts, dq_out, own_out, other_out,
         keys, values, inner, bias, dkeys, dvalues) = refs
        grad_ref = g_ref
    else:
        (g_ref, add_ref, n_ref, inv_ref, q, own, other, mixed, log, dense, starts, dq_out, own_out, other_out,
         grad_out, grad_ref, keys, values, inner, bias, dkeys, dvalues) = refs

        def body(i, carry):
            here = chunk_rows(i)
            grad = g_ref[0, i].astype(f32) + norm_back(add_ref[here].astype(f32), n_ref[here], inv_ref[here, 0:1])
            grad_out[here] = grad
            grad_ref[here] = grad.astype(bf16)
            return carry

        lax.fori_loop(0, 2, body, 0)
    c = lax.axis_index("dp") % 2
    gather_keys(own, other, keys, values)
    inner[...] = jnp.zeros_like(inner)
    for block, span in reversed(SPANS):
        here, n = pl.ds(block * BLOCK, BLOCK), span * BLOCK
        place = key_places(c, (n, BLOCK), 0, span)
        mine = lax.broadcasted_iota(jnp.int32, (n, BLOCK), 1) + (2 * block + c) * BLOCK
        allowed = (place <= mine) & (place >= starts[0:1, here])
        bias[:n] = jnp.where(allowed, 0.0, MASKED)
        grad = grad_ref[0, block] if later else grad_ref[here]
        d_mixed = nt(grad, dense[0]).astype(bf16)
        product = d_mixed.astype(f32) * mixed[here].astype(f32)
        for h in range(HEADS):
            inner[:, h : h + 1] = jnp.sum(pick(product, h), axis=-1, keepdims=True)
        inner_rows = inner[...].T
        query = q[here]
        d_query = jnp.zeros((BLOCK, INNER), f32)
        for h in range(HEADS):
            mine_q, mine_d = pick(query, h), pick(d_mixed, h)
            prob = jnp.exp(nt(keys[:n], mine_q) + bias[:n] - log[h : h + 1, here])
            d_prob = nt(values[:n], mine_d)
            d_score = (prob * (d_prob - inner_rows[h : h + 1])).astype(bf16)
            d_value = nn(prob.astype(bf16), mine_d)
            d_key = nn(d_score, mine_q)
            if span == 4 and h == 0:
                dvalues[...] = d_value
                dkeys[...] = d_key
            else:
                dvalues[:n] += d_value
                dkeys[:n] += d_key
            d_query = d_query + pick(tn(d_score, keys[:n]), h)
        dq_out[here] = d_query * HEAD_DIM ** (-0.5)
    for n, ref in enumerate((dkeys, dvalues)):
        own_out[n, 0:BLOCK] = ref[0:BLOCK]
        other_out[n, 0:BLOCK] = ref[BLOCK : 2 * BLOCK].astype(bf16)
        own_out[n, BLOCK : 2 * BLOCK] = ref[2 * BLOCK : 3 * BLOCK]
        other_out[n, BLOCK : 2 * BLOCK] = ref[3 * BLOCK : 4 * BLOCK].astype(bf16)


def back_feed_kernel(later, grad, down, up, small, slope, second, active, mixed, normed, e_out, grads_out, sums_out, hid):
    sums_out[...] = jnp.zeros_like(sums_out)

    def body(i, carry):
        here = chunk_rows(i)
        g = grad[0, i] if later else grad[here]
        d_hidden = (nt(g, down[0]) * slope[here].astype(f32)).astype(bf16)
        hid[here] = d_hidden
        d_second = nt(d_hidden, up[0])
        e_out[here] = d_second * small[0, 2:3]
        sums_out[0:1] += jnp.sum(d_second * normed[here], axis=0, keepdims=True)
        sums_out[1:2] += jnp.sum(d_second, axis=0, keepdims=True)
        sums_out[2:3] += jnp.sum(g.astype(f32), axis=0, keepdims=True)
        sums_out[3:4] += jnp.sum(d_hidden.astype(f32), axis=0, keepdims=True)
        return carry

    lax.fori_loop(0, 2, body, 0)
    g = grad[0].reshape(2 * BLOCK, WIDTH) if later else grad[...]
    grads_out[:INNER] = tn(mixed[...], g).astype(bf16)
    grads_out[INNER : INNER + WIDTH] = tn(second[...], hid[...]).astype(bf16)
    grads_out[INNER + WIDTH :] = tn(active[...], g).astype(bf16)


def back_front_kernel(d_query, own, got, cos, sin, wq, small, first, normed, e_in, e_out, grads_out, sums_out, packed):
    sums_out[...] = jnp.zeros_like(sums_out)
    turn = turner()

    def unrotate(value, cosine, sine):
        moved = value * sine
        high = moved.astype(bf16)
        low = (moved - high.astype(f32)).astype(bf16)
        return value * cosine + (nn(high, turn) + nn(low, turn))

    def body(i, carry):
        here = chunk_rows(i)
        cosine, sine = cos[here], sin[here]
        parts = [
            unrotate(d_query[here], cosine, sine),
            unrotate(own[0, here] + got[0, here].astype(f32), cosine, sine),
            own[1, here] + got[1, here].astype(f32),
        ]
        d_first = jnp.zeros((BLOCK, WIDTH), f32)
        for n, part in enumerate(parts):
            part = part.astype(bf16)
            packed[n, here] = part
            d_first = d_first + nn(part, wq[0, INNER * n : INNER * (n + 1)])
            sums_out[2 + n : 3 + n, :INNER] += jnp.sum(part.astype(f32), axis=0, keepdims=True)
        e_out[i] = (d_first * small[0, 0:1] + e_in[here]).astype(bf16)
        sums_out[0:1] += jnp.sum(d_first * normed[here], axis=0, keepdims=True)
        sums_out[1:2] += jnp.sum(d_first, axis=0, keepdims=True)
        return carry

    lax.fori_loop(0, 2, body, 0)
    for n in range(3):
        grads_out[INNER * n : INNER * (n + 1)] = tn(packed[n], first[...]).astype(bf16)


ROWS = 2 * BLOCK


def shape_of(*dims, dtype=f32):
    return jax.ShapeDtypeStruct(dims, dtype)


def at_layer(layer, *dims):
    return pl.BlockSpec((1,) + dims, lambda i: (layer,) + (0,) * len(dims))


def on_device(kernel, name, args, specs, outs, scratch):
    whole = pl.BlockSpec(memory_space=pltpu.VMEM)
    return pl.pallas_call(
        kernel,
        grid=(1,),
        out_shape=outs,
        in_specs=[whole if spec is None else spec for spec in specs],
        out_specs=[whole] * len(outs),
        scratch_shapes=scratch,
        compiler_params=pltpu.CompilerParams(vmem_limit_bytes=VMEM_LIMIT),
        name=name,
    )(*args)


def norm_back(scaled, normed, inverse):
    inner = scaled - jnp.mean(scaled, axis=-1, keepdims=True)
    inner = inner - normed * jnp.mean(scaled * normed, axis=-1, keepdims=True)
    return inner * inverse


def swapped(value):
    return lax.ppermute(value, "dp", [(n, n ^ 1) for n in range(16)])


def forward_layer(layer, x, add, stacks, tables):
    wq, wd, wu, wn, small = stacks
    cosine, sine, start_col, start_row = tables
    later = add is not None
    small_spec = at_layer(layer, 16, WIDTH)
    args, specs = ([x, add], [None, None]) if later else ([x], [at_layer(0, 2, BLOCK, WIDTH)])
    outs = [
        shape_of(ROWS, WIDTH), shape_of(ROWS, 128), shape_of(ROWS, WIDTH, dtype=bf16),
        shape_of(ROWS, WIDTH, dtype=bf16), shape_of(ROWS, INNER, dtype=bf16), shape_of(2, ROWS, INNER, dtype=bf16),
    ]
    if later:
        outs = [shape_of(ROWS, WIDTH)] + outs
    got = on_device(
        functools.partial(front_kernel, later), "front",
        args + [wq, small, cosine, sine], specs + [at_layer(layer, 3 * INNER, WIDTH), small_spec, None, None],
        outs, [pltpu.VMEM((2 * INNER, WIDTH), bf16)],
    )
    flat = got[0] if later else None
    normed, inverse, first, second, query, own = got[-6:]
    other = swapped(own)
    active, slope = on_device(
        feed_kernel, "feed", [second, wu, small], [None, at_layer(layer, WIDTH, WIDTH), small_spec],
        [shape_of(ROWS, WIDTH, dtype=bf16)] * 2, [],
    )
    part, mixed, log = on_device(
        mix_kernel, "mix", [query, own, other, active, wd, wn, start_col],
        [None] * 4 + [at_layer(layer, INNER, WIDTH), at_layer(layer, WIDTH, WIDTH), None],
        [shape_of(2, BLOCK, WIDTH, dtype=bf16), shape_of(ROWS, INNER, dtype=bf16), shape_of(128, ROWS)],
        [pltpu.VMEM((SEQ, INNER), bf16)] * 2 + [pltpu.VMEM((ROWS, 128), f32), pltpu.VMEM((BLOCK, SEQ), f32)],
    )
    return flat, part, (normed, inverse, first, second, query, own, other, active, slope, mixed, log)


def backward_layer(layer, xg, extra, stacks, tables, kept):
    wq, wd, wu, wn, small = stacks
    cosine, sine, start_col, start_row = tables
    normed, inverse, first, second, query, own, other, active, slope, mixed, log = kept
    later = extra is None
    small_spec = at_layer(layer, 16, WIDTH)
    grad_spec = at_layer(1, 2, BLOCK, WIDTH)
    args, specs = [xg], [grad_spec]
    outs = [shape_of(ROWS, INNER), shape_of(2, ROWS, INNER), shape_of(2, ROWS, INNER, dtype=bf16)]
    if not later:
        args, specs = args + list(extra), specs + [None] * 3
        outs = outs + [shape_of(ROWS, WIDTH), shape_of(ROWS, WIDTH, dtype=bf16)]
    got = on_device(
        functools.partial(back_mix_kernel, later), "back_mix",
        args + [query, own, other, mixed, log, wd, start_row],
        specs + [None] * 5 + [at_layer(layer, INNER, WIDTH), None],
        outs,
        [pltpu.VMEM((SEQ, INNER), bf16)] * 2
        + [pltpu.VMEM((BLOCK, 128), f32), pltpu.VMEM((SEQ, BLOCK), f32)]
        + [pltpu.VMEM((SEQ, INNER), f32)] * 2,
    )
    d_query, d_own, d_other = got[:3]
    grad, low, low_spec = (None, xg, grad_spec) if later else (got[3], got[4], None)
    arrived = swapped(d_other)
    e_two, grads_two, sums_two = on_device(
        functools.partial(back_feed_kernel, later), "back_feed",
        [low, wn, wu, small, slope, second, active, mixed, normed],
        [low_spec, at_layer(layer, WIDTH, WIDTH), at_layer(layer, WIDTH, WIDTH), small_spec] + [None] * 5,
        [shape_of(ROWS, WIDTH), shape_of(INNER + 2 * WIDTH, WIDTH, dtype=bf16), shape_of(8, WIDTH)],
        [pltpu.VMEM((ROWS, WIDTH), bf16)],
    )
    e, grads_one, sums_one = on_device(
        back_front_kernel, "back_front",
        [d_query, d_own, arrived, cosine, sine, wq, small, first, normed, e_two],
        [None] * 5 + [at_layer(layer, 3 * INNER, WIDTH), small_spec] + [None] * 3,
        [shape_of(2, BLOCK, WIDTH, dtype=bf16), shape_of(3 * INNER, WIDTH, dtype=bf16), shape_of(8, WIDTH)],
        [pltpu.VMEM((3, ROWS, INNER), bf16)],
    )
    return grad, e, grads_one, grads_two, sums_one, sums_two


def tables_of(segment_ids):
    at = Place()
    seq = lax.dynamic_slice(segment_ids, (at.y, at.z, 0), (1, 1, SEQ))[0, 0]
    blocks = seq.reshape(2, 2, BLOCK)
    mine = lax.dynamic_index_in_dim(blocks, at.c, 1, keepdims=False).reshape(ROWS)
    start = jnp.sum((seq[None, :] < mine[:, None]).astype(jnp.int32), axis=1)
    i = jnp.arange(ROWS, dtype=jnp.int32)
    place = i + BLOCK * (i // BLOCK + at.c) - start
    half = ROT // 2
    freqs = 10000.0 ** (-(2.0 * jnp.arange(half, dtype=f32)) / ROT)
    angles = place.astype(f32)[:, None] * freqs
    cosine, sine = jnp.cos(angles), jnp.sin(angles)
    rest = HEAD_DIM - ROT
    cosine = jnp.concatenate([cosine, cosine, jnp.ones((ROWS, rest), f32)], axis=1)
    sine = jnp.concatenate([sine, sine, jnp.zeros((ROWS, rest), f32)], axis=1)
    return jnp.tile(cosine, (1, HEADS)), jnp.tile(sine, (1, HEADS)), start[:, None], start[None, :]


def by_kind(value):
    return value.reshape(value.shape[0], HEADS, 3, HEAD_DIM).transpose(2, 1, 3, 0).reshape(3 * INNER, -1)


def local(
    boundary,
    segment_ids,
    attn_gain,
    attn_shift,
    mlp_gain,
    mlp_shift,
    qkv_weight,
    qkv_bias,
    dense_weight,
    dense_bias,
    up_weight,
    up_bias,
    down_weight,
    down_bias,
):
    bias = qkv_bias.reshape(HEADS, 3, HEAD_DIM).transpose(1, 0, 2)
    half = ROT // 2
    turned = jnp.concatenate(
        [-bias[:2, :, half:ROT], bias[:2, :, :half], jnp.zeros((2, HEADS, HEAD_DIM - ROT), f32)], axis=2
    )
    bias = jnp.concatenate([bias, turned]).reshape(5, INNER)
    bias = jnp.pad(bias, ((0, 0), (0, WIDTH - INNER)))
    small = jnp.concatenate(
        [
            attn_gain, attn_shift, mlp_gain, mlp_shift, bias[:3], up_bias, dense_bias + down_bias, bias[3:],
            jnp.zeros((5, WIDTH), f32),
        ]
    )
    xg, *stacks = spread(
        boundary[0].astype(bf16), by_kind(qkv_weight[0]), dense_weight[0], up_weight[0], down_weight[0], small
    )
    tables = tables_of(segment_ids)
    _, part_zero, kept_zero = forward_layer(0, xg, None, stacks, tables)
    branch = total_over_tensor(part_zero).reshape(ROWS, WIDTH)
    flat = xg[0].reshape(ROWS, WIDTH).astype(f32)
    small_one = stacks[4]
    small_one = small_one.at[1, 8].set(stacks[4][0, 8])
    middle, part_one, kept_one = forward_layer(1, flat, branch, stacks[:4] + [small_one], tables)

    _, e_one, grads_one, grads_two, sums_one, sums_two = backward_layer(1, xg, None, stacks, tables, kept_one)
    e_one = total_over_tensor(e_one).reshape(ROWS, WIDTH)
    grad, e_zero, grads_three, grads_four, sums_three, sums_four = backward_layer(
        0, xg, (e_one, kept_one[0], kept_one[1]), stacks, tables, kept_zero
    )
    total, small_total, back = final(
        [grads_three, grads_four, grads_one, grads_two],
        [sums_three, sums_four, sums_one, sums_two],
        [e_zero, part_one, grad, kept_zero[0], kept_zero[1], middle, stacks[4]],
    )
    mine = lax.dynamic_index_in_dim(small_total, lax.axis_index("pipe"), 0, keepdims=False)
    total = total.astype(f32).reshape(2, GRAD_ROWS // 2, WIDTH)
    d_qkv = jnp.concatenate([total[0, :288], total[1, :288]])
    d_qkv = d_qkv.reshape(3, HEADS, HEAD_DIM, WIDTH).transpose(3, 1, 0, 2).reshape(1, WIDTH, 3 * INNER)
    d_bias = mine[2:5, :INNER].reshape(3, HEADS, HEAD_DIM).transpose(1, 0, 2).reshape(1, 3 * INNER)
    d_up = jnp.concatenate([total[0, 480:], total[1, 288:384]])
    return (
        back.astype(f32)[None],
        mine[0:1],
        mine[1:2],
        mine[8:9],
        mine[9:10],
        d_qkv,
        d_bias,
        total[0, 288:480][None],
        mine[10:11],
        d_up[None],
        mine[11:12],
        total[1, 384:][None],
        mine[10:11],
    )


def solution(mesh):
    in_specs = (
        P("pipe", None, "dp", None),
        P(),
        P("pipe", None),
        P("pipe", None),
        P("pipe", None),
        P("pipe", None),
        P("pipe", None, "tensor"),
        P("pipe", "tensor"),
        P("pipe", "tensor", None),
        P("pipe", None),
        P("pipe", None, "tensor"),
        P("pipe", "tensor"),
        P("pipe", "tensor", None),
        P("pipe", None),
    )
    out_specs = (
        P("pipe", None, "dp", None),
        P("pipe", None),
        P("pipe", None),
        P("pipe", None),
        P("pipe", None),
        P("pipe", None, "tensor"),
        P("pipe", "tensor"),
        P("pipe", "tensor", None),
        P("pipe", None),
        P("pipe", None, "tensor"),
        P("pipe", "tensor"),
        P("pipe", "tensor", None),
        P("pipe", None),
    )
    return jax.shard_map(local, mesh=mesh, in_specs=in_specs, out_specs=out_specs, check_vma=False)
```

time: 458 us -> 265 us (0.58); the launches traced: 453 us -> 265 us
  matrix products: 69 us -> 0 us
  other arithmetic: 55.9 us -> 11 us
  local copies, waits for them, and re-layouts: 59.6 us -> 20.9 us
  Pallas kernels: 258 us -> 224 us
    pallas_call x1, Pallas kernels: 130 us -> 37.6 us  [spread(): pl.pallas_call(spread_kernel, out_shape=[jax.ShapeDtypeStruct(s, bf16) fo...]
    dot_general x48 -> x0, matrix products: 69 us -> none  [the longest x2 17.2 us: forward_layer(): hidden = jnp.dot(second, w['up'], preferred_element_type=f32) + w['up_bias']]
    pallas_call x1 -> x12, Pallas kernels: 18.7 us -> 78 us  [on_device(): pl.pallas_call(kernel, grid=(1,), out_shape=outs, in_specs=[whole if spec...]
    unnamed x288 -> x46, local copies, waits for them, and re-layouts: 22.3 us -> 6.38 us
    reduce_sum x15 -> x1, other arithmetic: 13.9 us -> 0.36 us  [tables_of(): start = jnp.sum((seq[None, :] < mine[:, None]).astype(jnp.int32), axis=1)]
    another operation x16 -> x0, other arithmetic: 12.8 us -> none  [the longest x3 7.3 us: local(): jnp.stack([grads_zero, grads_one])]
    convert_element_type x10 -> x2, other arithmetic: 10.2 us -> 1.31 us  [the longest x1 1.3 us: local(): flat = xg[0].reshape(ROWS, WIDTH).astype(f32)]
    concatenate x7 -> x4, local copies, waits for them, and re-layouts: 8.47 us -> 1.5 us  [the longest x1 1.27 us: local(): jnp.concatenate([attn_gain, attn_shift, mlp_gain, mlp_shift, bias[:3], up...]
  transfers between devices with their start and end apart: 4 -> 4, of which waited for: 0 -> 0; matrix products, arithmetic and copies ran while one was open for 8% -> 1% of each run, Pallas kernels for 0% -> 9%
where the time goes in v2:
time: 265 us
  Pallas kernels  224 us (85%)
  local copies, waits for them, and re-layouts  20.9 us (8%)
  other arithmetic  11 us (4%)
  starting transfers between devices  7.44 us (3%)
    pallas_call x12, Pallas kernels, on_device(): pl.pallas_call(kernel, grid=(1,), out_shape=outs, in_specs=[whole if spec...  78 us
    pallas_call x1, Pallas kernels, final(): pl.pallas_call(final_kernel, out_shape=[jax.ShapeDtypeStruct((GRAD_ROWS,...  71 us
    pallas_call x2, Pallas kernels, total_over_tensor(): pl.pallas_call(total_kernel, out_shape=jax.ShapeDtypeStruct((2, BLOCK, WI...  37.7 us
    pallas_call x1, Pallas kernels, spread(): pl.pallas_call(spread_kernel, out_shape=[jax.ShapeDtypeStruct(s, bf16) fo...  37.6 us
    ppermute x4, starting transfers between devices, swapped(): return lax.ppermute(value, 'dp', [(n, n ^ 1) for n in range(16)])  7.44 us
    unnamed x46, local copies, waits for them, and re-layouts  6.38 us
  transfers between devices with their start and end apart: 4, of which 0 were waited for; matrix products, arithmetic and copies ran while one was open for 1% of the time, Pallas kernels for 9%

profile of v2, /device:TPU:1, one launch (start us, length us, event | category | flops | bytes accessed | tf_op | source)
XLA Modules:
  0.0 264.8 jit_solution(574227479373774710)
XLA Ops:
  3.1 1.4 fusion.8
  6.0 1.0 copy.59.refs_3_.refs_4_.cos
  7.0 0.9 tile.20
  7.9 1.0 copy.60.refs_4_.refs_5_.sin
  9.0 1.3 convert_bitcast_fusion.block
  10.3 1.0 copy.57
  11.4 1.3 concatenate.26.small
  12.6 37.6 %spread.1 = (bf16[2,2,256,768]{3,2,1,0:T(8,128)(2,1)}, bf16[2,576,768]{2,1,0:T(8,128)(2,1)}, bf16[2,192,768]{2,1,0:T(8,128)(2,1)}, bf16[2,768,768]{2,1,0:T(8,128...) custom-call(bf16[4,256,768]{2,1,0:T(8,128)(2,1)} %convert_bitcast_fusion.block, bf16[576,768]{1,0:T(8,128)(2,1)} %bitcast.61, ...), custom_call_target="tpu_custom_call" | custom-call | tf_op jit(solution)/shard_map/spread/pallas_call | solution.py:285
  50.3 5.4 %front.2 = (f32[512,768]{1,0:T(8,128)}, f32[512,128]{1,0:T(8,128)}, bf16[512,768]{1,0:T(8,128)(2,1)}, bf16[512,768]{1,0:T(8,128)(2,1)}, bf16[512,192]{1,0:T(8,128)(2,1)}, /*index=5*/bf16[2,512,192]{2,1,0:T(8,128)(2,1)}) custom-call(bf16[2,2,256,768]{3,2,1,0:T(8,128)(2,1)} %get-tuple-element.77.refs_0_.grad, ...), custom_call_target="tpu_custom_call" | custom-call | tf_op jit(solution)/shard_map/front/pallas_call | solution.py:875
  56.7 4.3 %feed.2 = (bf16[512,768]{1,0:T(8,128)(2,1)}, bf16[512,768]{1,0:T(8,128)(2,1)}) custom-call(bf16[512,768]{1,0:T(8,128)(2,1)} %get-tuple-element.82.second, bf16[2,768,768]{2,1,0:T(8,128)(2,1)} %get-tuple-element.83.up, f32[2,16,768]{2,1,0:T(8,128)} %get-tuple-element.79.refs_2_.small.params), custom_call_target="tpu_custom_call" | custom-call | tf_op jit(solution)/shard_map/feed/pallas_call | solution.py:875
  61.1 1.3 bitcast_convert_fusion.1.refs_0_
  63.2 6.0 %mix.2 = (bf16[2,256,768]{2,1,0:T(8,128)(2,1)}, bf16[512,192]{1,0:T(8,128)(2,1)}, f32[128,512]{1,0:T(8,128)}) custom-call(bf16[512,192]{1,0:T(8,128)(2,1)} %get-tuple-element.80.q.refs_4_, bf16[2,512,192]{2,1,0:T(8,128)(2,1)} %get-tuple-element.81.own.refs_5_, bf16[2,512,192]{2,1,0:T(8,128)(2,1)} %copy-done.4, bf16[512,768]{1,0:T(8,128)(2,1)} %get-tuple-element.84.active, ...), custom_call_target="tpu_custom_call" | custom-call | tf_op jit(solution)/shard_map/mix/pallas_call | solution.py:875
  69.2 18.4 %total.2 = bf16[2,256,768]{2,1,0:T(8,128)(2,1)} custom-call(bf16[2,256,768]{2,1,0:T(8,128)(2,1)} %get-tuple-element.87.part), custom_call_target="tpu_custom_call" | custom-call | tf_op jit(solution)/shard_map/total/pallas_call | solution.py:363
  87.6 6.3 %front.3 = (f32[512,768]{1,0:T(8,128)}, f32[512,768]{1,0:T(8,128)}, f32[512,128]{1,0:T(8,128)}, bf16[512,768]{1,0:T(8,128)(2,1)}, bf16[512,768]{1,0:T(8,128)(2,1...) custom-call(f32[512,768]{1,0:T(8,128)} %bitcast_convert_fusion.1.refs_0_, bf16[512,768]{1,0:T(8,128)(2,1)} %bitcast.63, ...), custom_call_target="tpu_custom_call" | custom-call | tf_op jit(solution)/shard_map/front/pallas_call | solution.py:875
  93.9 3.4 %collective-permute-start.1 = (bf16[2,512,192]{2,1,0:T(8,128)(2,1)}, bf16[2,512,192]{2,1,0:T(8,128)(2,1)S(1)}, u32[]{:S(2)}, u32[]{:S(2)}) collective-permute-start(bf16[2,512,192]{2,1,0:T(8,128)(2,1)} %get-tuple-element.89.own.refs_2_), channel_id=1, source_target_pairs={{0,4},{4,0},{8,12},{12,8},{16,20},{20,16},{24,28},{28,24},{32,36},... | collective-permute-start | bytes 1179656 | tf_op jit(solution)/shard_map/ppermute | solution.py:894
  97.4 4.2 %feed.3 = (bf16[512,768]{1,0:T(8,128)(2,1)}, bf16[512,768]{1,0:T(8,128)(2,1)}) custom-call(bf16[512,768]{1,0:T(8,128)(2,1)} %get-tuple-element.90.second, bf16[2,768,768]{2,1,0:T(8,128)(2,1)} %get-tuple-element.83.up, f32[2,16,768]{2,1,0:T(8,128)} %copy-done.7), custom_call_target="tpu_custom_call" | custom-call | tf_op jit(solution)/shard_map/feed/pallas_call | solution.py:875
  102.4 6.0 %mix.3 = (bf16[2,256,768]{2,1,0:T(8,128)(2,1)}, bf16[512,192]{1,0:T(8,128)(2,1)}, f32[128,512]{1,0:T(8,128)}) custom-call(bf16[512,192]{1,0:T(8,128)(2,1)} %get-tuple-element.88.q.refs_1_, bf16[2,512,192]{2,1,0:T(8,128)(2,1)} %get-tuple-element.89.own.refs_2_, bf16[2,512,192]{2,1,0:T(8,128)(2,1)} %copy-done.5, bf16[512,768]{1,0:T(8,128)(2,1)} %get-tuple-element.91.active, ...), custom_call_target="tpu_custom_call" | custom-call | tf_op jit(solution)/shard_map/mix/pallas_call | solution.py:875
  108.5 7.2 %back_mix.2 = (f32[512,192]{1,0:T(8,128)}, f32[2,512,192]{2,1,0:T(8,128)}, bf16[2,512,192]{2,1,0:T(8,128)(2,1)}) custom-call(bf16[2,2,256,768]{3,2,1,0:T(8,128)(2,1)} %get-tuple-element.77.refs_0_.grad, bf16[512,192]{1,0:T(8,128)(2,1)} %get-tuple-element.88.q.refs_1_, bf16[2,512,192]{2,1,0:T(8,128)(2,1)} %get-tuple-element.89.own.refs_2_, ...), custom_call_target="tpu_custom_call" | custom-call | tf_op jit(solution)/shard_map/back_mix/pallas_call | solution.py:875
  115.7 8.1 %back_feed.2 = (f32[512,768]{1,0:T(8,128)}, bf16[1728,768]{1,0:T(8,128)(2,1)}, f32[8,768]{1,0:T(8,128)}) custom-call(bf16[2,2,256,768]{3,2,1,0:T(8,128)(2,1)} %get-tuple-element.77.refs_0_.grad, bf16[2,768,768]{2,1,0:T(8,128)(2,1)} %get-tuple-element.86.down, bf16[2,768,768]{2,1,0:T(8,128)(2,1)} %get-tuple-element.83.up, ...), custom_call_target="tpu_custom_call" | custom-call | tf_op jit(solution)/shard_map/back_feed/pallas_call | solution.py:875
  124.6 6.8 %back_front.2 = (bf16[2,256,768]{2,1,0:T(8,128)(2,1)}, bf16[576,768]{1,0:T(8,128)(2,1)}, f32[8,768]{1,0:T(8,128)}) custom-call(f32[512,192]{1,0:T(8,128)} %get-tuple-element.94.d_query, f32[2,512,192]{2,1,0:T(8,128)} %get-tuple-element.95.own, bf16[2,512,192]{2,1,0:T(8,128)(2,1)} %copy-done.10, f32[512,192]{1,0:T(8,128)} %copy.59.refs_3_.refs_4_.cos, ...), custom_call_target="tpu_custom_call" | custom-call | tf_op jit(solution)/shard_map/back_front/pallas_call | solution.py:875
  131.4 19.3 %total.3 = bf16[2,256,768]{2,1,0:T(8,128)(2,1)} custom-call(bf16[2,256,768]{2,1,0:T(8,128)(2,1)} %get-tuple-element.101.part), custom_call_target="tpu_custom_call" | custom-call | tf_op jit(solution)/shard_map/total/pallas_call | solution.py:363
  150.7 8.7 %back_mix.3 = (f32[512,192]{1,0:T(8,128)}, f32[2,512,192]{2,1,0:T(8,128)}, bf16[2,512,192]{2,1,0:T(8,128)(2,1)}, f32[512,768]{1,0:T(8,128)}, bf16[512,768]{1,0:T(8,128)(2,1)}) custom-call(bf16[2,2,256,768]{3,2,1,0:T(8,128)(2,1)} %get-tuple-element.77.refs_0_.grad, bf16[512,768]{1,0:T(8,128)(2,1)} %bitcast.62, f32[512,768]{1,0:T(8,128)} %get-tuple-element.98.normed.refs_2_, ...), custom_call_target="tpu_custom_call" | custom-call | tf_op jit(solution)/shard_map/back_mix/pallas_call | solution.py:875
  159.4 3.9 %collective-permute-start.3 = (bf16[2,512,192]{2,1,0:T(8,128)(2,1)}, bf16[2,512,192]{2,1,0:T(8,128)(2,1)S(1)}, u32[]{:S(2)}, u32[]{:S(2)}) collective-permute-start(bf16[2,512,192]{2,1,0:T(8,128)(2,1)} %get-tuple-element.107), channel_id=1, source_target_pairs={{0,4},{4,0},{8,12},{12,8},{16,20},{20,16},{24,28},{28,24},{32,36},... | collective-permute-start | bytes 1179656 | tf_op jit(solution)/shard_map/ppermute | solution.py:894
  163.3 8.2 %back_feed.3 = (f32[512,768]{1,0:T(8,128)}, bf16[1728,768]{1,0:T(8,128)(2,1)}, f32[8,768]{1,0:T(8,128)}) custom-call(bf16[512,768]{1,0:T(8,128)(2,1)} %get-tuple-element.110.grad, bf16[2,768,768]{2,1,0:T(8,128)(2,1)} %get-tuple-element.86.down, bf16[2,768,768]{2,1,0:T(8,128)(2,1)} %get-tuple-element.83.up, ...), custom_call_target="tpu_custom_call" | custom-call | tf_op jit(solution)/shard_map/back_feed/pallas_call | solution.py:875
  172.3 6.7 %back_front.3 = (bf16[2,256,768]{2,1,0:T(8,128)(2,1)}, bf16[576,768]{1,0:T(8,128)(2,1)}, f32[8,768]{1,0:T(8,128)}) custom-call(f32[512,192]{1,0:T(8,128)} %get-tuple-element.105.d_query, f32[2,512,192]{2,1,0:T(8,128)} %get-tuple-element.106.own, bf16[2,512,192]{2,1,0:T(8,128)(2,1)} %copy-done.9, f32[512,192]{1,0:T(8,128)} %copy.59.refs_3_.refs_4_.cos, ...), custom_call_target="tpu_custom_call" | custom-call | tf_op jit(solution)/shard_map/back_front/pallas_call | solution.py:875
  179.0 71.0 %final.1 = (bf16[2304,768]{1,0:T(8,128)(2,1)}, f32[2,16,768]{2,1,0:T(8,128)}, bf16[4,256,768]{2,1,0:T(8,128)(2,1)}) custom-call(bf16[576,768]{1,0:T(8,128)(2,1)} %get-tuple-element.113.f_zero, bf16[1728,768]{1,0:T(8,128)(2,1)} %get-tuple-element.114.e_zero, bf16[576,768]{1,0:T(8,128)(2,1)} %get-tuple-element.115.f_one, ...), custom_call_target="tpu_custom_call" | custom-call | tf_op jit(solution)/shard_map/final/pallas_call | solution.py:578
  250.1 2.5 convert.3
  252.9 1.8 copy-done.1
  254.8 1.6 slice.131
  257.3 1.3 copy.69
  259.4 1.9 bitcast_convert_fusion
  262.7 1.6 maximum_bitcast_fusion
  (91 shorter events, 12.0 us)
Async XLA Ops:
  0.6 8.3 %copy-start.3 = (f32[1,4,256,768]{3,2,1,0:T(8,128)S(1)}, f32[1,4,256,768]{3,2,1,0:T(8,128)}, u32[]{:S(2)}) copy-start(f32[1,4,256,768]{3,2,1,0:T(8,128)} %param.16) | copy-start | bytes 9437188
  4.9 51.0 %copy-start.11 = (s32[512]{0:T(512)}, s32[512]{0:T(512)S(1)}, u32[]{:S(2)}) copy-start(s32[512]{0:T(512)S(1)} %convert_reduce_fusion) | copy-start | bytes 6148
  8.9 1.4 copy-start.8
  8.9 2.4 copy-start.20
  8.9 2.4 copy-start.21
  8.9 2.4 copy-start.13
  9.0 2.4 copy-start.15
  9.0 2.4 copy-start.16
  9.0 2.4 copy-start.17
  9.0 2.4 copy-start.18
  9.0 2.4 copy-start.19
  50.3 5.5 %copy-start.2 = (f32[2,16,768]{2,1,0:T(8,128)S(1)}, f32[2,16,768]{2,1,0:T(8,128)}, u32[]{:S(2)}) copy-start(f32[2,16,768]{2,1,0:T(8,128)} %get-tuple-element.79.refs_2_.small.params) | copy-start | bytes 294916
  50.3 5.5 %copy-start = (bf16[2,2,256,768]{3,2,1,0:T(8,128)(2,1)S(1)}, bf16[2,2,256,768]{3,2,1,0:T(8,128)(2,1)}, u32[]{:S(2)}) copy-start(bf16[2,2,256,768]{3,2,1,0:T(8,128)(2,1)} %get-tuple-element.77.refs_0_.grad) | copy-start | bytes 4718596
  55.7 6.7 %collective-permute-start = (bf16[2,512,192]{2,1,0:T(8,128)(2,1)}, bf16[2,512,192]{2,1,0:T(8,128)(2,1)S(1)}, u32[]{:S(2)}, u32[]{:S(2)}) collective-permute-start(bf16[2,512,192]{2,1,0:T(8,128)(2,1)} %get-tuple-element.81.own.refs_5_), channel_id=1, source_target_pairs={{0,4},{4,0},{8,12},{12,8},{16,20},{20,16},{24,28},{28,24},{32,36},... | collective-permute-start | bytes 1179656 | tf_op jit(solution)/shard_map/ppermute | solution.py:894
  61.1 8.1 %copy-start.7 = (f32[2,16,768]{2,1,0:T(8,128)}, f32[2,16,768]{2,1,0:T(8,128)S(1)}, u32[]{:S(2)}) copy-start(f32[2,16,768]{2,1,0:T(8,128)S(1)} %scatter.4.refs_3_.small) | copy-start | bytes 294916
  62.4 0.8 copy-start.4
  93.9 7.7 %collective-permute-start.1 = (bf16[2,512,192]{2,1,0:T(8,128)(2,1)}, bf16[2,512,192]{2,1,0:T(8,128)(2,1)S(1)}, u32[]{:S(2)}, u32[]{:S(2)}) collective-permute-start(bf16[2,512,192]{2,1,0:T(8,128)(2,1)} %get-tuple-element.89.own.refs_2_), channel_id=1, source_target_pairs={{0,4},{4,0},{8,12},{12,8},{16,20},{20,16},{24,28},{28,24},{32,36},... | collective-permute-start | bytes 1179656 | tf_op jit(solution)/shard_map/ppermute | solution.py:894
  101.6 0.8 copy-start.5
  115.7 8.1 %collective-permute-start.2 = (bf16[2,512,192]{2,1,0:T(8,128)(2,1)}, bf16[2,512,192]{2,1,0:T(8,128)(2,1)S(1)}, u32[]{:S(2)}, u32[]{:S(2)}) collective-permute-start(bf16[2,512,192]{2,1,0:T(8,128)(2,1)} %get-tuple-element.96), channel_id=1, source_target_pairs={{0,4},{4,0},{8,12},{12,8},{16,20},{20,16},{24,28},{28,24},{32,36},... | collective-permute-start | bytes 1179656 | tf_op jit(solution)/shard_map/ppermute | solution.py:894
  123.8 0.8 copy-start.10
  159.4 12.1 %collective-permute-start.3 = (bf16[2,512,192]{2,1,0:T(8,128)(2,1)}, bf16[2,512,192]{2,1,0:T(8,128)(2,1)S(1)}, u32[]{:S(2)}, u32[]{:S(2)}) collective-permute-start(bf16[2,512,192]{2,1,0:T(8,128)(2,1)} %get-tuple-element.107), channel_id=1, source_target_pairs={{0,4},{4,0},{8,12},{12,8},{16,20},{20,16},{24,28},{28,24},{32,36},... | collective-permute-start | bytes 1179656 | tf_op jit(solution)/shard_map/ppermute | solution.py:894
  171.5 0.8 copy-start.9
  252.8 2.0 copy-start.1
  257.3 2.0 copy-start.6
  259.4 1.9 copy-start.12
  262.7 1.6 copy-start.14

commit v3 on v2

v3 whole, which is shorter than its diff:
```python
import functools
import types

import jax
import jax.numpy as jnp
from jax import lax
from jax.experimental import pallas as pl
from jax.experimental.pallas import tpu as pltpu
from jax.sharding import PartitionSpec as P

MESH = pl.DeviceIdType.MESH
HEAD_DIM = 64
ROT = 16
EPS = 1e-05
MASKED = -1e30
WIDTH = 768
SEQ = 1024
BLOCK = 256
HEADS = 3
INNER = HEADS * HEAD_DIM
GRAD_ROWS = 2304
bf16 = jnp.bfloat16
f32 = jnp.float32
VMEM_LIMIT = 56 * 1024 * 1024


class Place:
    def __init__(self):
        self.p = lax.axis_index("pipe")
        self.d = lax.axis_index("dp")
        self.x = lax.axis_index("tensor")
        self.z = self.d // 4
        self.low = (self.d // 2) % 2
        self.c = self.d % 2
        self.y = 2 * self.p + self.low

    def at_x(self, steps):
        return (self.p, self.d, (self.x + steps) % 4)

    def at_y(self, steps):
        y = (self.y + steps) % 4
        return (y // 2, self.z * 4 + (y % 2) * 2 + self.c, self.x)

    def at_z(self, steps):
        return (self.p, ((self.z + steps) % 4) * 4 + self.d % 4, self.x)

    def sibling(self):
        return (self.p, self.d + 1 - 2 * self.c, self.x)

    def partner(self):
        return (1 - self.p, self.z * 4 + (1 - self.low) * 2 + self.c, self.x)

    def beside(self):
        return (self.p, self.z * 4 + (1 - self.low) * 2 + self.c, self.x)


def greet(devices):
    barrier = pltpu.get_barrier_semaphore()
    for device in devices:
        pl.semaphore_signal(barrier, inc=1, device_id=device, device_id_type=MESH)
    pl.semaphore_wait(barrier, len(devices))


class Copies:
    def __init__(self, send_sems, recv_sems, somebody):
        self.send_sems, self.recv_sems = send_sems, recv_sems
        self.somebody = somebody
        self.count = 0
        self.started = []

    def send(self, src, dst, device):
        k = self.count
        self.count += 1
        copy = pltpu.make_async_remote_copy(
            src_ref=src,
            dst_ref=dst,
            send_sem=self.send_sems.at[k],
            recv_sem=self.recv_sems.at[k],
            device_id=device,
            device_id_type=MESH,
        )
        copy.start()
        self.started.append(copy)
        return k

    def landed(self, k, dst):
        pltpu.make_async_remote_copy(
            src_ref=dst,
            dst_ref=dst,
            send_sem=self.send_sems.at[k],
            recv_sem=self.recv_sems.at[k],
            device_id=self.somebody,
            device_id_type=MESH,
        ).wait_recv()

    def drain(self):
        for copy in self.started:
            copy.wait_send()


class RingSum:
    def __init__(self, copies, me, right, left, chunk, relay, direct, final):
        self.copies, self.me, self.right, self.left = copies, me, right, left
        self.chunk, self.relay_in, self.direct, self.final = chunk, relay, direct, final

    def start(self):
        me, send = self.me, self.copies.send
        far, after, before = (me + 2) % 4, (me + 1) % 4, (me + 3) % 4
        self.k = [
            send(self.chunk(far, 0), self.relay_in[0], self.right),
            send(self.chunk(far, 1), self.relay_in[1], self.left),
            send(self.chunk(after, 1), self.direct[1], self.right),
            send(self.chunk(before, 0), self.direct[0], self.left),
        ]

    def relay(self):
        me, copies = self.me, self.copies
        after, before = (me + 1) % 4, (me + 3) % 4
        copies.landed(self.k[0], self.relay_in[0])
        add_into(self.relay_in[0], self.chunk(after, 0))
        k0 = copies.send(self.relay_in[0], self.final[0], self.right)
        copies.landed(self.k[1], self.relay_in[1])
        add_into(self.relay_in[1], self.chunk(before, 1))
        k1 = copies.send(self.relay_in[1], self.final[1], self.left)
        self.k += [k0, k1]

    def finish(self, out):
        copies = self.copies
        copies.landed(self.k[3], self.direct[0])
        copies.landed(self.k[4], self.final[0])
        store_sum(out(0), self.chunk(self.me, 0), self.direct[0], self.final[0])
        copies.landed(self.k[2], self.direct[1])
        copies.landed(self.k[5], self.final[1])
        store_sum(out(1), self.chunk(self.me, 1), self.direct[1], self.final[1])


class RingGather:
    def __init__(self, copies, me, right, left, piece, halves):
        self.copies, self.me, self.right, self.left = copies, me, right, left
        self.piece, self.halves = piece, halves

    def start(self):
        mine = self.piece(self.me)
        self.k = [
            self.copies.send(mine, mine, self.right),
            self.copies.send(mine, mine, self.left),
        ]

    def relay(self):
        before, after = (self.me + 3) % 4, (self.me + 1) % 4
        self.copies.landed(self.k[0], self.piece(before))
        view = self.halves(before, 0)
        k0 = self.copies.send(view, view, self.right)
        self.copies.landed(self.k[1], self.piece(after))
        view = self.halves(after, 1)
        k1 = self.copies.send(view, view, self.left)
        self.k += [k0, k1]

    def finish(self):
        far = (self.me + 2) % 4
        self.copies.landed(self.k[2], self.halves(far, 0))
        self.copies.landed(self.k[3], self.halves(far, 1))


class DirectSum:
    def __init__(self, copies, me, to, chunk, bufs):
        self.copies, self.me, self.to, self.chunk, self.bufs = copies, me, to, chunk, bufs

    def start(self):
        self.k = [
            self.copies.send(self.chunk((self.me + k) % 4), self.bufs[k - 1], self.to(k)) for k in (1, 3, 2)
        ]

    def finish(self, out):
        for index, k in zip(self.k, (1, 3, 2)):
            self.copies.landed(index, self.bufs[k - 1])
        store_sum(out, self.chunk(self.me), *self.bufs)


class DirectGather:
    def __init__(self, copies, me, to, piece):
        self.copies, self.me, self.to, self.piece = copies, me, to, piece

    def start(self):
        mine = self.piece(self.me)
        self.k = [self.copies.send(mine, mine, self.to(k)) for k in (1, 3, 2)]

    def finish(self):
        for index, k in zip(self.k, (1, 3, 2)):
            self.copies.landed(index, self.piece((self.me + 4 - k) % 4))


def add_into(ref, other):
    ref[...] = (ref[...].astype(f32) + other[...].astype(f32)).astype(ref.dtype)


def store_sum(out, *parts):
    total = parts[0][...].astype(f32)
    for part in parts[1:]:
        total = total + part[...].astype(f32)
    out[...] = total.astype(out.dtype)


def rows(start, size, step=16):
    return pl.ds(pl.multiple_of(start, step), size)


def spread_kernel(
    block, wq, wd, wu, wn, small, xg, oq, od, ou, on, osm,
    hold_x, hold_s, hold_q, hold_d, hold_u, hold_n, send_sems, recv_sems, local_sems,
):
    at = Place()
    p, x, y, z, c = at.p, at.x, at.y, at.z, at.c
    greet(
        [at.at_x(1), at.at_x(3), at.at_y(1), at.at_y(2), at.at_y(3), at.at_z(1), at.at_z(3), at.sibling()]
    )
    copies = Copies(send_sems, recv_sems, at.at_x(1))
    weights = [(wq, oq), (wd, od), (wu, ou), (wn, on)]

    def piece(ref, zz, cc):
        if ref.shape[-2] == WIDTH:
            return ref.at[rows(192 * zz + 96 * cc, 96)]
        each = ref.shape[-2] // 4
        return ref.at[rows(each * zz, each), pl.ds(pl.multiple_of(384 * cc, 128), 384)]

    def half(ref, zz, cc, h):
        if ref.shape[-2] == WIDTH:
            return ref.at[rows(192 * zz + 96 * cc + 48 * h, 48)]
        each = ref.shape[-2] // 4
        more = (each // 2 + 15) // 16 * 16
        size = each - more if h else more
        return ref.at[rows(each * zz + more * h, size), pl.ds(pl.multiple_of(384 * cc, 128), 384)]

    quarter = rows(64 * x, 64)
    first = [
        copies.send(block.at[(y + k) % 4, quarter], xg.at[p, at.low, quarter], at.at_y(k)) for k in (1, 3, 2)
    ]
    sent = [
        copies.send(piece(src, z, c), piece(dst.at[p], z, c), at.partner()) for src, dst in weights
    ]
    sent_small = copies.send(small, osm.at[p], at.partner())
    held = [hold_x, hold_s, hold_q, hold_d, hold_u, hold_n]
    kept = [(block.at[y], xg.at[p, at.low]), (small, osm.at[p])] + [(s, d.at[p]) for s, d in weights]
    inward = [
        pltpu.make_async_copy(src, hold, local_sems.at[n]) for n, ((src, _), hold) in enumerate(zip(kept, held))
    ]
    for copy in inward:
        copy.start()
    outward = []
    for n, ((_, dst), hold) in enumerate(zip(kept, held)):
        inward[n].wait()
        copy = pltpu.make_async_copy(hold, dst, local_sems.at[n + 6])
        copy.start()
        outward.append(copy)
    gathers = []
    for k, index in zip((1, 3, 2), first):
        source = (y + 4 - k) % 4
        slot = xg.at[source // 2, source % 2]
        copies.landed(index, slot.at[quarter])
        gather = RingGather(
            copies,
            x,
            at.at_x(1),
            at.at_x(3),
            lambda j, slot=slot: slot.at[rows(64 * j, 64)],
            lambda j, h, slot=slot: slot.at[rows(64 * j + 32 * h, 32)],
        )
        gather.start()
        gathers.append(gather)
    others = [dst.at[1 - p] for _, dst in weights]
    rings, shared = [], []
    for other, index in zip(others, sent):
        copies.landed(index, piece(other, z, c))
        ring = RingGather(
            copies,
            z,
            at.at_z(1),
            at.at_z(3),
            lambda j, other=other: piece(other, j, c),
            lambda j, h, other=other: half(other, j, c, h),
        )
        ring.start()
        rings.append(ring)
        mine = piece(other, z, c)
        shared.append((copies.send(mine, mine, at.sibling()), piece(other, z, 1 - c)))
    for gather in gathers:
        gather.relay()
    for other, ring in zip(others, rings):
        ring.relay()
        for j in ((z + 3) % 4, (z + 1) % 4):
            mine = piece(other, j, c)
            shared.append((copies.send(mine, mine, at.sibling()), piece(other, j, 1 - c)))
    for gather in gathers:
        gather.finish()
    for other, ring in zip(others, rings):
        ring.finish()
        j = (z + 2) % 4
        mine = piece(other, j, c)
        shared.append((copies.send(mine, mine, at.sibling()), piece(other, j, 1 - c)))
    copies.landed(sent_small, osm.at[1 - p])
    for index, view in shared:
        copies.landed(index, view)
    for copy in outward:
        copy.wait()
    copies.drain()


SPREAD_COPIES = 3 + 4 + 1 + 12 + 16 + 16


def spread(block, wq, wd, wu, wn, small):
    any_space = pl.BlockSpec(memory_space=pl.ANY)
    shapes = [(2, 2, BLOCK, WIDTH)] + [(2,) + w.shape for w in (wq, wd, wu, wn)]
    return pl.pallas_call(
        spread_kernel,
        out_shape=[jax.ShapeDtypeStruct(s, bf16) for s in shapes]
        + [jax.ShapeDtypeStruct((2,) + small.shape, f32)],
        in_specs=[any_space] * 6,
        out_specs=[any_space] * 6,
        scratch_shapes=[
            pltpu.VMEM((BLOCK, WIDTH), bf16),
            pltpu.VMEM(small.shape, f32),
        ]
        + [pltpu.VMEM(w.shape, bf16) for w in (wq, wd, wu, wn)]
        + [
            pltpu.SemaphoreType.DMA((SPREAD_COPIES,)),
            pltpu.SemaphoreType.DMA((SPREAD_COPIES,)),
            pltpu.SemaphoreType.DMA((12,)),
        ],
        compiler_params=pltpu.CompilerParams(
            collective_id=0, has_side_effects=True, vmem_limit_bytes=VMEM_LIMIT
        ),
        name="spread",
    )(block, wq, wd, wu, wn, small)


PAIRS = 3
LANES = 128


class Flow:
    def __init__(self, at, copies, chip, own_half, out, cols):
        self.at, self.copies, self.cols = at, copies, cols
        self.chip, self.own_half, self.out = chip.at[:, :, cols], own_half.at[:, :, cols], out.at[:, cols]
        self.base, self.other_base = 1152 * at.c, 1152 * (1 - at.c)

    def send_core(self, layers):
        self.core = []
        for layer in range(2):
            for which, size, place in PARTS:
                src = layers[layer][which].at[rows(size * (1 - self.at.c), size), self.cols]
                dst = self.chip.at[layer, pl.ds(place, size)]
                self.core.append((self.copies.send(src, dst, self.at.sibling()), dst))

    def add_core(self):
        for index, dst in self.core:
            self.copies.landed(index, dst)
        chip, own_half = self.chip, self.own_half

        def body(i, carry):
            here = rows(i * 192, 192)
            for layer in range(2):
                chip[layer, here] = (chip[layer, here].astype(f32) + own_half[layer, here].astype(f32)).astype(bf16)
            return carry

        lax.fori_loop(0, 6, body, 0)

    def to_sibling(self, start, size):
        view = self.out.at[rows(self.base + start, size)]
        index = self.copies.send(view, view, self.at.sibling())
        return index, start, size

    def from_sibling(self, sent):
        index, start, size = sent
        self.copies.landed(index, self.out.at[rows(self.other_base + start, size)])


class FlowYZ(Flow):
    def begin(self, bufs, one, tail):
        at, chip = self.at, self.chip
        self.add_core()
        self.one, self.tail = one, tail
        self.ring = RingSum(
            self.copies, at.y, at.at_y(1), at.at_y(3),
            lambda j, h: chip.at[j // 2, rows(576 * (j % 2) + 288 * h, 288)],
            [bufs.at[0], bufs.at[1]], [bufs.at[2], bufs.at[3]], [bufs.at[4], bufs.at[5]],
        )
        self.ring.start()

    def relay(self):
        self.ring.relay()

    def second(self):
        at, one, tail = self.at, self.one, self.tail
        self.ring.finish(lambda h: one.at[pl.ds(288 * h, 288)])
        self.sum = DirectSum(
            self.copies, at.z, at.at_z, lambda j: one.at[rows(144 * j, 144)], [tail.at[n] for n in range(3)]
        )
        self.sum.start()

    def back(self):
        at, out = self.at, self.out
        start = self.base + 576 * at.low
        self.sum.finish(out.at[rows(start + 144 * at.z, 144)])
        self.gather = DirectGather(self.copies, at.z, at.at_z, lambda j: out.at[rows(start + 144 * j, 144)])
        self.gather.start()

    def beside(self):
        at, out = self.at, self.out
        self.gather.finish()
        view = out.at[rows(self.base + 576 * at.low, 576)]
        self.next = self.copies.send(view, view, at.beside())
        self.half = self.to_sibling(576 * at.low, 576)

    def share(self):
        at, out = self.at, self.out
        self.copies.landed(self.next, out.at[rows(self.base + 576 * (1 - at.low), 576)])
        self.rest = self.to_sibling(576 * (1 - at.low), 576)

    def share_rest(self):
        pass

    def end(self):
        self.from_sibling(self.half)
        self.from_sibling(self.rest)


class FlowZY(Flow):
    def begin(self, bufs, one, tail):
        at, chip = self.at, self.chip
        self.add_core()
        self.one, self.tail = one, tail
        self.ring = RingSum(
            self.copies, at.z, at.at_z(1), at.at_z(3),
            lambda j, h: chip.at[h, rows(288 * j, 288)],
            [bufs.at[0], bufs.at[1]], [bufs.at[2], bufs.at[3]], [bufs.at[4], bufs.at[5]],
        )
        self.ring.start()

    def relay(self):
        self.ring.relay()

    def second(self):
        at, one, tail = self.at, self.one, self.tail
        self.ring.finish(lambda h: one.at[pl.ds(288 * h, 288)])
        self.sum = DirectSum(
            self.copies, at.y, at.at_y, lambda j: one.at[rows(144 * j, 144)], [tail.at[n] for n in range(3)]
        )
        self.sum.start()

    def back(self):
        at, out = self.at, self.out
        view = out.at[rows(self.base + 288 * at.z + 144 * at.low, 144)]
        self.sum.finish(view)
        self.next = self.copies.send(view, view, at.beside())

    def beside(self):
        at, out = self.at, self.out
        self.copies.landed(self.next, out.at[rows(self.base + 288 * at.z + 144 * (1 - at.low), 144)])
        self.gather = RingGather(
            self.copies, at.z, at.at_z(1), at.at_z(3),
            lambda j: out.at[rows(self.base + 288 * j, 288)],
            lambda j, h: out.at[rows(self.base + 288 * j + 144 * h, 144)],
        )
        self.gather.start()

    def share(self):
        self.gather.relay()

    def share_rest(self):
        self.gather.finish()
        self.all = self.to_sibling(0, 1152)

    def end(self):
        self.from_sibling(self.all)


PARTS = ((0, 288, 0), (1, 864, 288))


def final_kernel(
    f_zero, e_zero, f_one, e_one, sf_zero, se_zero, sf_one, se_one,
    scaled, branch, grad, normed, inverse, middle, params, out, small_out, back,
    chip, own_half, ones, bufs, tails, got, first_small, grad_rows, normed_rows, inverse_rows, middle_rows,
    slices, send_sems, recv_sems, local_sem, half_sems, tail_sems,
):
    at = Place()
    x, y, c = at.x, at.y, at.c
    tail_loads = []
    for source, target in ((grad, grad_rows), (normed, normed_rows), (inverse, inverse_rows), (middle, middle_rows)):
        for h in range(2):
            copy = pltpu.make_async_copy(
                source.at[rows(256 * h + 64 * x, 64)], target.at[pl.ds(64 * h, 64)], tail_sems.at[len(tail_loads)]
            )
            copy.start()
            tail_loads.append(copy)
    greet(
        [at.at_x(k) for k in (1, 2, 3)]
        + [at.at_y(k) for k in (1, 2, 3)]
        + [at.at_z(k) for k in (1, 2, 3)]
        + [at.sibling()]
    )
    copies = Copies(send_sems, recv_sems, at.at_x(1))
    send, landed = copies.send, copies.landed
    quarter = rows(64 * x, 64)
    layers = ((f_zero, e_zero), (f_one, e_one))
    flows = []
    for n in range(PAIRS):
        for kind, start in ((FlowYZ, 0), (FlowZY, PAIRS * LANES)):
            flows.append(kind(at, copies, chip, own_half, out, pl.ds(start + n * LANES, LANES)))
    flows[0].send_core(layers)
    flows[1].send_core(layers)
    halves = []
    for layer in range(2):
        for which, size, place in PARTS:
            copy = pltpu.make_async_copy(
                layers[layer][which].at[rows(size * c, size)],
                own_half.at[layer, pl.ds(place, size)],
                half_sems.at[2 * layer + which],
            )
            copy.start()
            halves.append(copy)
    for copy in tail_loads:
        copy.wait()
    for h in range(2):
        here = pl.ds(64 * h, 64)
        value = grad_rows[here] + norm_back(scaled[h], normed_rows[here], inverse_rows[here, 0:1])
        slices[0, h] = value.astype(bf16)
        slices[1, h] = (middle_rows[here] + (branch[h] + params[1, 8:9])).astype(bf16)
    home = []
    for k in (1, 3, 2):
        j = (y + k) % 4
        home.append((k, send(slices.at[j // 2, j % 2], back.at[y, quarter], at.at_y(k))))
    own = pltpu.make_async_copy(slices.at[y // 2, y % 2], back.at[y, quarter], local_sem)
    own.start()
    for flow in flows[2:]:
        flow.send_core(layers)
    for layer, refs in enumerate(((sf_zero, se_zero), (sf_one, se_one))):
        for which, ref in enumerate(refs):
            first_small[layer, pl.ds(8 * which, 8)] = ref[...]
    small_x = [(k, send(first_small, got.at[k - 1], at.at_x(k))) for k in (1, 3, 2)]
    for copy in halves:
        copy.wait()

    def slot(t):
        for n in range(PAIRS):
            for m in (2 * n, 2 * n + 1):
                flow, stage = flows[m], t - n
                if stage == 0:
                    flow.begin(bufs.at[m], ones.at[m], tails.at[m])
                elif 0 < stage < 7:
                    (flow.relay, flow.second, flow.back, flow.beside, flow.share, flow.share_rest)[stage - 1]()

    slot(0)
    own.wait()
    for k, index in home:
        landed(index, back.at[(y + 4 - k) % 4, quarter])
    outer = RingGather(
        copies, x, at.at_x(1), at.at_x(3),
        lambda j: back.at[:, rows(64 * j, 64)],
        lambda j, h: back.at[pl.ds(2 * h, 2), rows(64 * j, 64)],
    )
    outer.start()
    slot(1)
    slot(2)
    outer.relay()
    for k, index in small_x:
        landed(index, got.at[k - 1])
    of_norms = lax.broadcasted_iota(jnp.int32, first_small.shape, 1) % 8 < 2
    others = got[0] + got[1] + got[2]
    small_out[...] = first_small[...] + jnp.where(of_norms, others, 0.0)
    small_z = [(k, send(small_out, got.at[2 + k], at.at_z(k))) for k in (1, 3, 2)]
    slot(3)
    for k, index in small_z:
        landed(index, got.at[2 + k])
    for k, index in small_z:
        copies.started[index].wait_send()
    small_out[...] = small_out[...] + (got[3] + got[4] + got[5])
    small_y = [(k, send(small_out, got.at[5 + k], at.at_y(k))) for k in (1, 3, 2)]
    slot(4)
    slot(5)
    for k, index in small_y:
        landed(index, got.at[5 + k])
    for k, index in small_y:
        copies.started[index].wait_send()
    small_out[...] = small_out[...] + (got[6] + got[7] + got[8])
    small_c = send(small_out, got.at[9], at.sibling())
    slot(6)
    landed(small_c, got.at[9])
    copies.started[small_c].wait_send()
    small_out[...] = small_out[...] + got[9]
    slot(7)
    slot(8)
    outer.finish()
    for flow in flows:
        flow.end()
    waited = {index for _, index in small_z} | {index for _, index in small_y} | {small_c}
    for index, copy in enumerate(copies.started):
        if index not in waited:
            copy.wait_send()


FINAL_COPIES = 160


def final(grads, small, last):
    vmem = pl.BlockSpec(memory_space=pltpu.VMEM)
    return pl.pallas_call(
        final_kernel,
        out_shape=[
            jax.ShapeDtypeStruct((GRAD_ROWS, WIDTH), bf16),
            jax.ShapeDtypeStruct((2, 16, WIDTH), f32),
            jax.ShapeDtypeStruct((4, BLOCK, WIDTH), bf16),
        ],
        in_specs=[pl.BlockSpec(memory_space=pl.ANY)] * 4 + [vmem] * 6 + [pl.BlockSpec(memory_space=pl.ANY)] * 4 + [vmem],
        out_specs=[vmem] * 3,
        scratch_shapes=[
            pltpu.VMEM((2, 1152, WIDTH), bf16),
            pltpu.VMEM((2, 1152, WIDTH), bf16),
            pltpu.VMEM((2 * PAIRS, 576, LANES), bf16),
            pltpu.VMEM((2 * PAIRS, 6, 288, LANES), bf16),
            pltpu.VMEM((2 * PAIRS, 3, 144, LANES), bf16),
            pltpu.VMEM((10, 2, 16, WIDTH), f32),
            pltpu.VMEM((2, 16, WIDTH), f32),
            pltpu.VMEM((128, WIDTH), f32),
            pltpu.VMEM((128, WIDTH), f32),
            pltpu.VMEM((128, 128), f32),
            pltpu.VMEM((128, WIDTH), f32),
            pltpu.VMEM((2, 2, 64, WIDTH), bf16),
            pltpu.SemaphoreType.DMA((FINAL_COPIES,)),
            pltpu.SemaphoreType.DMA((FINAL_COPIES,)),
            pltpu.SemaphoreType.DMA,
            pltpu.SemaphoreType.DMA((4,)),
            pltpu.SemaphoreType.DMA((8,)),
        ],
        compiler_params=pltpu.CompilerParams(
            collective_id=3, has_side_effects=True, vmem_limit_bytes=VMEM_LIMIT
        ),
        name="final",
    )(*grads, *small, *last)


def nn(a, b):
    return lax.dot_general(a, b, (((1,), (0,)), ((), ())), preferred_element_type=f32)


def nt(a, b):
    return lax.dot_general(a, b, (((1,), (1,)), ((), ())), preferred_element_type=f32)


def tn(a, b):
    return lax.dot_general(a, b, (((0,), (0,)), ((), ())), preferred_element_type=f32)


def turner():
    c = lax.broadcasted_iota(jnp.int32, (INNER, INNER), 0)
    r = lax.broadcasted_iota(jnp.int32, (INNER, INNER), 1)
    lane = c % HEAD_DIM
    half = ROT // 2
    minus = (lane < half) & (r == c + half)
    plus = (lane >= half) & (lane < ROT) & (r == c - half)
    return jnp.where(plus, 1.0, jnp.where(minus, -1.0, 0.0)).astype(bf16)


def head_lanes(shape, h):
    lane = lax.broadcasted_iota(jnp.int32, shape, len(shape) - 1)
    return (lane >= h * HEAD_DIM) & (lane < (h + 1) * HEAD_DIM)


def pick(value, h):
    return jnp.where(head_lanes(value.shape, h), value, jnp.zeros_like(value))


def chunk_rows(i):
    return pl.ds(pl.multiple_of(i * BLOCK, BLOCK), BLOCK)


def gather_keys(own, other, keys, values):
    for n, ref in enumerate((keys, values)):
        ref[0:BLOCK] = own[n, 0:BLOCK]
        ref[BLOCK : 2 * BLOCK] = other[n, 0:BLOCK]
        ref[2 * BLOCK : 3 * BLOCK] = own[n, BLOCK : 2 * BLOCK]
        ref[3 * BLOCK : 4 * BLOCK] = other[n, BLOCK : 2 * BLOCK]


def key_places(c, shape, dim, blocks):
    i = lax.broadcasted_iota(jnp.int32, shape, dim)
    place = jnp.where(i < BLOCK, i + BLOCK * c, i - BLOCK * c)
    if blocks == 4:
        late = jnp.where(i < 3 * BLOCK, i + BLOCK * c, i - BLOCK * c)
        place = jnp.where(i < 2 * BLOCK, place, late)
    return place


SPANS = ((0, 2), (1, 4))


ROWS = 2 * BLOCK


def shape_of(*dims, dtype=f32):
    return jax.ShapeDtypeStruct(dims, dtype)


def at_layer(layer, *dims):
    return pl.BlockSpec((1,) + dims, lambda i: (layer,) + (0,) * len(dims))


def on_device(kernel, name, args, specs, outs, scratch):
    whole = pl.BlockSpec(memory_space=pltpu.VMEM)
    return pl.pallas_call(
        kernel,
        grid=(1,),
        out_shape=outs,
        in_specs=[whole if spec is None else spec for spec in specs],
        out_specs=[whole] * len(outs),
        scratch_shapes=scratch,
        compiler_params=pltpu.CompilerParams(vmem_limit_bytes=VMEM_LIMIT),
        name=name,
    )(*args)


def norm_back(scaled, normed, inverse):
    inner = scaled - jnp.mean(scaled, axis=-1, keepdims=True)
    inner = inner - normed * jnp.mean(scaled * normed, axis=-1, keepdims=True)
    return inner * inverse


class Env:
    def __init__(self, refs, ins, outs, scratch):
        refs = list(refs)
        sources = {name: refs.pop(0) for name in ins}
        self.targets = {name: refs.pop(0) for name in outs}
        self.v = types.SimpleNamespace(**{name: refs.pop(0) for name in list(ins) + list(outs) + list(scratch)})
        self.send_sems, self.recv_sems, load_sems, self.store_sems = refs
        self.held = [getattr(self.v, name) for name in ins]
        self.kept = [getattr(self.v, name) for name in outs]
        self.targets = list(self.targets.values())
        self.loads, self.stores = [], []
        for n, name in enumerate(ins):
            source, index = sources[name], ins[name][1]
            source = source if index is None else source.at[index]
            copy = pltpu.make_async_copy(source, self.held[n], load_sems.at[n])
            copy.start()
            self.loads.append(copy)

    def need(self, *refs):
        for ref in refs:
            n = [held is ref for held in self.held].index(True)
            if self.loads[n] is not None:
                self.loads[n].wait()
                self.loads[n] = None

    def done(self, *refs):
        for ref in refs:
            n = [kept is ref for kept in self.kept].index(True)
            copy = pltpu.make_async_copy(ref, self.targets[n], self.store_sems.at[n])
            copy.start()
            self.stores.append(copy)

    def close(self):
        assert not any(self.loads) and len(self.stores) == len(self.kept)
        for copy in self.stores:
            copy.wait()


def fused(body, name, ins, outs, scratch, copies, collective_id):
    def kernel(*refs):
        env = Env(refs, ins, outs, scratch)
        body(env)
        env.close()

    any_space = pl.BlockSpec(memory_space=pl.ANY)
    arrays = [array for array, _ in ins.values()]
    held = [pltpu.VMEM(array.shape if index is None else array.shape[1:], array.dtype) for array, index in ins.values()]
    kept = [pltpu.VMEM(s.shape, s.dtype) for s in list(outs.values()) + list(scratch.values())]
    got = pl.pallas_call(
        kernel,
        out_shape=list(outs.values()),
        in_specs=[any_space] * len(ins),
        out_specs=[any_space] * len(outs),
        scratch_shapes=held
        + kept
        + [
            pltpu.SemaphoreType.DMA((copies,)),
            pltpu.SemaphoreType.DMA((copies,)),
            pltpu.SemaphoreType.DMA((len(ins),)),
            pltpu.SemaphoreType.DMA((len(outs),)),
        ],
        compiler_params=pltpu.CompilerParams(
            collective_id=collective_id, has_side_effects=True, vmem_limit_bytes=VMEM_LIMIT
        ),
        name=name,
    )(*arrays)
    return types.SimpleNamespace(**dict(zip(outs, got)))


def block_sum(at, copies, part, bufs, block):
    return RingSum(
        copies, at.x, at.at_x(1), at.at_x(3),
        lambda j, h: part.at[block, rows(64 * j, 64), pl.ds(384 * h, 384)],
        [bufs.at[block, 0], bufs.at[block, 1]], [bufs.at[block, 2], bufs.at[block, 3]],
        [bufs.at[block, 4], bufs.at[block, 5]],
    )


def block_gather(at, copies, out, block):
    return RingGather(
        copies, at.x, at.at_x(1), at.at_x(3),
        lambda j: out.at[block, rows(64 * j, 64)],
        lambda j, h: out.at[block, rows(64 * j, 64), pl.ds(384 * h, 384)],
    )


def sum_out(at, out, block):
    return lambda h: out.at[block, rows(64 * at.x, 64), pl.ds(384 * h, 384)]


def piece_out(out, block):
    return lambda h: out.at[block, :, pl.ds(384 * h, 384)]


def forward_body(later, env):
    at, v = Place(), env.v
    greet([at.sibling()] if later else [at.sibling(), at.at_x(1), at.at_x(3)])
    copies = Copies(env.send_sems, env.recv_sems, at.sibling())
    wq, wt, small = v.wq, v.wt, v.small
    env.need(v.wq, v.small)
    turn = turner()
    for i in range(2):
        wt[INNER * i : INNER * (i + 1)] = nn(turn, wq[INNER * i : INNER * (i + 1)]).astype(bf16)

    def row(i, wide=WIDTH):
        return small[i : i + 1, :wide]

    env.need(v.x, v.cos, v.sin)
    if later:
        env.need(v.add, v.before)

    def front(i, carry):
        here = chunk_rows(i)
        x = v.x[i].astype(f32)
        if later:
            x = x + (v.add[i].astype(f32) + v.before[8:9])
            v.middle[here] = x
        centred = x - jnp.mean(x, axis=-1, keepdims=True)
        inverse = lax.rsqrt(jnp.mean(centred * centred, axis=-1, keepdims=True) + EPS)
        normed = centred * inverse
        v.normed[here] = normed
        v.inverse[here] = jnp.broadcast_to(inverse, (BLOCK, 128))
        first = (normed * row(0) + row(1)).astype(bf16)
        v.first[here] = first
        v.second[here] = (normed * row(2) + row(3)).astype(bf16)
        cosine, sine = v.cos[here], v.sin[here]
        query = (nt(first, wq[:INNER]) + row(4, INNER)) * cosine
        query = query + (nt(first, wt[:INNER]) + row(9, INNER)) * sine
        v.query[here] = (query * HEAD_DIM ** (-0.5)).astype(bf16)
        key = (nt(first, wq[INNER : 2 * INNER]) + row(5, INNER)) * cosine
        key = key + (nt(first, wt[INNER:]) + row(10, INNER)) * sine
        v.own[0, here] = key.astype(bf16)
        v.own[1, here] = (nt(first, wq[2 * INNER :]) + row(6, INNER)).astype(bf16)
        return carry

    lax.fori_loop(0, 2, front, 0)
    swap = copies.send(v.own, v.other, at.sibling())
    env.done(v.normed, v.inverse, v.first, v.second, v.query, v.own)
    if later:
        env.done(v.middle)
    env.need(v.up)

    def feed(i, carry):
        here = pl.ds(pl.multiple_of(i * 128, 128), 128)
        hidden = nn(v.second[here], v.up[...]) + row(7)
        below = 0.5 + 0.5 * lax.erf(hidden * (0.5**0.5))
        v.active[here] = (hidden * below).astype(bf16)
        density = jnp.exp(-0.5 * hidden * hidden) * 0.3989422804014327
        v.slope[here] = (below + hidden * density).astype(bf16)
        return carry

    lax.fori_loop(0, 4, feed, 0)
    env.done(v.active, v.slope)
    copies.landed(swap, v.other)
    env.done(v.other)
    keys, values, bias, logs = v.keys, v.values, v.bias, v.logs
    gather_keys(v.own, v.other, keys, values)
    logs[...] = jnp.zeros_like(logs)
    env.need(v.dense, v.down, v.starts)
    sums = {}
    for block, span in reversed(SPANS):
        here, n = pl.ds(block * BLOCK, BLOCK), span * BLOCK
        place = key_places(at.c, (BLOCK, n), 1, span)
        mine = lax.broadcasted_iota(jnp.int32, (BLOCK, n), 0) + (2 * block + at.c) * BLOCK
        allowed = (place <= mine) & (place >= v.starts[here])
        bias[:, :n] = jnp.where(allowed, 0.0, MASKED)
        query = v.query[here]
        mixed = jnp.zeros((BLOCK, INNER), f32)
        for h in range(HEADS):
            score = nt(pick(query, h), keys[:n]) + bias[:, :n]
            top = jnp.max(score, axis=-1, keepdims=True)
            expo = jnp.exp(score - top)
            total = jnp.sum(expo, axis=-1, keepdims=True)
            logs[here, h : h + 1] = top + jnp.log(total)
            mixed = mixed + pick(nn(expo.astype(bf16), values[:n]) * (1.0 / total), h)
        mixed = mixed.astype(bf16)
        v.mixed[here] = mixed
        v.part[block] = (nn(mixed, v.dense[...]) + nn(v.active[here], v.down[...])).astype(bf16)
        if not later:
            sums[block] = block_sum(at, copies, v.part, v.bufs, block)
            sums[block].start()
    v.log[...] = logs[...].T
    env.done(v.mixed, v.log)
    if later:
        env.done(v.part)
    else:
        reduce_and_gather(at, copies, sums, v.total, ())
        env.done(v.total)
    copies.drain()


def reduce_and_gather(at, copies, sums, out, between):
    between = list(between)

    def work():
        if between:
            between.pop(0)()

    work()
    sums[1].relay()
    work()
    sums[0].relay()
    work()
    gathers = {}
    for block in (1, 0):
        sums[block].finish(sum_out(at, out, block))
        gathers[block] = block_gather(at, copies, out, block)
        gathers[block].start()
        work()
    for block in (1, 0):
        gathers[block].relay()
        work()
    for block in (1, 0):
        gathers[block].finish()


def backward_body(later, env):
    at, v = Place(), env.v
    greet([at.sibling(), at.at_x(1), at.at_x(3)])
    copies = Copies(env.send_sems, env.recv_sems, at.sibling())
    extra = []
    if later:
        env.need(v.part)
        extra = [block_sum(at, copies, v.part, v.part_bufs, block) for block in (1, 0)]
        for ring in extra:
            ring.start()
        env.need(v.g)
        low = v.g
    else:
        env.need(v.g, v.add, v.n_one, v.inv_one)
        low = v.low

        def incoming(i, carry):
            here = chunk_rows(i)
            grad = v.g[i].astype(f32) + norm_back(
                v.add[i].astype(f32), v.n_one[here], v.inv_one[here, 0:1]
            )
            v.grad[here] = grad
            low[i] = grad.astype(bf16)
            return carry

        lax.fori_loop(0, 2, incoming, 0)
        env.done(v.grad)
    keys, values, bias, inner = v.keys, v.values, v.bias, v.inner
    env.need(v.own, v.other, v.query, v.mixed, v.log, v.dense, v.starts)
    gather_keys(v.own, v.other, keys, values)
    inner[...] = jnp.zeros_like(inner)
    dkeys, dvalues, log = v.dkeys, v.dvalues, v.log
    for block, span in reversed(SPANS):
        here, n = pl.ds(block * BLOCK, BLOCK), span * BLOCK
        place = key_places(at.c, (n, BLOCK), 0, span)
        mine = lax.broadcasted_iota(jnp.int32, (n, BLOCK), 1) + (2 * block + at.c) * BLOCK
        allowed = (place <= mine) & (place >= v.starts[0:1, here])
        bias[:n] = jnp.where(allowed, 0.0, MASKED)
        d_mixed = nt(low[block], v.dense[...]).astype(bf16)
        product = d_mixed.astype(f32) * v.mixed[here].astype(f32)
        for h in range(HEADS):
            inner[:, h : h + 1] = jnp.sum(pick(product, h), axis=-1, keepdims=True)
        inner_rows = inner[...].T
        query = v.query[here]
        d_query = jnp.zeros((BLOCK, INNER), f32)
        for h in range(HEADS):
            mine_q, mine_d = pick(query, h), pick(d_mixed, h)
            prob = jnp.exp(nt(keys[:n], mine_q) + bias[:n] - log[h : h + 1, here])
            d_prob = nt(values[:n], mine_d)
            d_score = (prob * (d_prob - inner_rows[h : h + 1])).astype(bf16)
            d_value = nn(prob.astype(bf16), mine_d)
            d_key = nn(d_score, mine_q)
            if span == 4 and h == 0:
                dvalues[...] = d_value
                dkeys[...] = d_key
            else:
                dvalues[:n] += d_value
                dkeys[:n] += d_key
            d_query = d_query + pick(tn(d_score, keys[:n]), h)
        v.d_query[here] = d_query * HEAD_DIM ** (-0.5)
    for n, ref in enumerate((dkeys, dvalues)):
        v.d_other[n, 0:BLOCK] = ref[BLOCK : 2 * BLOCK].astype(bf16)
        v.d_other[n, BLOCK : 2 * BLOCK] = ref[3 * BLOCK : 4 * BLOCK].astype(bf16)
    swap = copies.send(v.d_other, v.got, at.sibling())
    for ring in extra:
        ring.relay()

    small, hid, normed = v.small, v.hid, v.normed
    sums_one, sums_two = v.sums_one, v.sums_two
    sums_one[...] = jnp.zeros_like(sums_one)
    sums_two[...] = jnp.zeros_like(sums_two)
    env.need(v.down, v.up, v.small, v.slope, v.normed)

    def feed(i, carry):
        here = chunk_rows(i)
        g = low[i]
        d_hidden = (nt(g, v.down[...]) * v.slope[here].astype(f32)).astype(bf16)
        hid[here] = d_hidden
        d_second = nt(d_hidden, v.up[...])
        v.e_two[here] = d_second * small[2:3]
        sums_two[0:1] += jnp.sum(d_second * normed[here], axis=0, keepdims=True)
        sums_two[1:2] += jnp.sum(d_second, axis=0, keepdims=True)
        sums_two[2:3] += jnp.sum(g.astype(f32), axis=0, keepdims=True)
        sums_two[3:4] += jnp.sum(d_hidden.astype(f32), axis=0, keepdims=True)
        return carry

    lax.fori_loop(0, 2, feed, 0)
    env.done(v.sums_two)
    for ring, block in zip(extra, (1, 0)):
        ring.finish(piece_out(v.part_sum, block))
    if later:
        env.done(v.part_sum)

    env.need(v.cos, v.sin, v.wq, v.first, v.second, v.active)
    turn = turner()
    wq, packed, got = v.wq, v.packed, v.got

    def unrotate(value, cosine, sine):
        moved = value * sine
        high = moved.astype(bf16)
        lower = (moved - high.astype(f32)).astype(bf16)
        return value * cosine + (nn(high, turn) + nn(lower, turn))

    copies.landed(swap, got)
    sums = {}
    for i in (1, 0):
        here = pl.ds(i * BLOCK, BLOCK)
        there = pl.ds(2 * i * BLOCK, BLOCK)
        cosine, sine = v.cos[here], v.sin[here]
        parts = [
            unrotate(v.d_query[here], cosine, sine),
            unrotate(dkeys[there] + got[0, here].astype(f32), cosine, sine),
            dvalues[there] + got[1, here].astype(f32),
        ]
        d_first = jnp.zeros((BLOCK, WIDTH), f32)
        for n, part in enumerate(parts):
            part = part.astype(bf16)
            packed[n, here] = part
            d_first = d_first + nn(part, wq[INNER * n : INNER * (n + 1)])
            sums_one[2 + n : 3 + n, :INNER] += jnp.sum(part.astype(f32), axis=0, keepdims=True)
        v.e[i] = (d_first * small[0:1] + v.e_two[here]).astype(bf16)
        sums[i] = block_sum(at, copies, v.e, v.bufs, i)
        sums[i].start()
        sums_one[0:1] += jnp.sum(d_first * normed[here], axis=0, keepdims=True)
        sums_one[1:2] += jnp.sum(d_first, axis=0, keepdims=True)
    env.done(v.sums_one)

    grads_one, grads_two = v.grads_one, v.grads_two

    def grad_dense():
        grads_two[:INNER] = tn(v.mixed[...], low[...].reshape(ROWS, WIDTH)).astype(bf16)

    def grad_up():
        grads_two[INNER : INNER + WIDTH] = tn(v.second[...], hid[...]).astype(bf16)

    def grad_down():
        grads_two[INNER + WIDTH :] = tn(v.active[...], low[...].reshape(ROWS, WIDTH)).astype(bf16)

    def grad_packed():
        for n in range(3):
            grads_one[INNER * n : INNER * (n + 1)] = tn(packed[n], v.first[...]).astype(bf16)

    if later:
        reduce_and_gather(at, copies, sums, v.total, (grad_dense, grad_packed, grad_up, grad_down))
        env.done(v.total)
    else:
        grad_dense()
        sums[1].relay()
        grad_packed()
        sums[0].relay()
        grad_up()
        grad_down()
        for block in (1, 0):
            sums[block].finish(piece_out(v.total, block))
        env.done(v.total)
    env.done(v.grads_one, v.grads_two)
    copies.drain()


def low_shape(*dims):
    return shape_of(*dims, dtype=bf16)


def forward_layer(layer, xg, add, stacks, tables):
    wq, wd, wu, wn, small = stacks
    cosine, sine, start_col, _ = tables
    later = add is not None
    ins = dict(wq=(wq, layer), small=(small, layer), x=(xg, 0))
    if later:
        ins.update(add=(add, None), before=(small, 0))
    ins.update(
        cos=(cosine, None), sin=(sine, None), up=(wu, layer), dense=(wd, layer), down=(wn, layer),
        starts=(start_col, None),
    )
    outs = dict(
        normed=shape_of(ROWS, WIDTH), inverse=shape_of(ROWS, 128), first=low_shape(ROWS, WIDTH),
        second=low_shape(ROWS, WIDTH), query=low_shape(ROWS, INNER), own=low_shape(2, ROWS, INNER),
        other=low_shape(2, ROWS, INNER), active=low_shape(ROWS, WIDTH), slope=low_shape(ROWS, WIDTH),
        mixed=low_shape(ROWS, INNER), log=shape_of(128, ROWS),
    )
    scratch = dict(
        wt=low_shape(2 * INNER, WIDTH), keys=low_shape(SEQ, INNER), values=low_shape(SEQ, INNER),
        logs=shape_of(ROWS, 128), bias=shape_of(BLOCK, SEQ),
    )
    if later:
        outs.update(middle=shape_of(ROWS, WIDTH), part=low_shape(2, BLOCK, WIDTH))
    else:
        outs.update(total=low_shape(2, BLOCK, WIDTH))
        scratch.update(part=low_shape(2, BLOCK, WIDTH), bufs=low_shape(2, 6, 64, 384))
    return fused(
        functools.partial(forward_body, later), "forward", ins, outs, scratch, 1 if later else 21, 5 if later else 4
    )


def backward_layer(layer, xg, add, stacks, tables, kept, kept_one):
    wq, wd, wu, wn, small = stacks
    cosine, sine, _, start_row = tables
    later = add is None
    if later:
        ins = dict(part=(kept.part, None), g=(xg, 1))
    else:
        ins = dict(
            g=(xg, 1), add=(add, None), n_one=(kept_one.normed, None), inv_one=(kept_one.inverse, None)
        )
    ins.update(
        own=(kept.own, None), other=(kept.other, None), query=(kept.query, None), mixed=(kept.mixed, None),
        log=(kept.log, None),
    )
    ins.update(dense=(wd, layer), starts=(start_row, None), down=(wn, layer), up=(wu, layer), small=(small, layer))
    ins.update(slope=(kept.slope, None), normed=(kept.normed, None))
    ins.update(cos=(cosine, None), sin=(sine, None), wq=(wq, layer))
    ins.update(first=(kept.first, None), second=(kept.second, None), active=(kept.active, None))
    outs = dict(
        grads_one=low_shape(3 * INNER, WIDTH), grads_two=low_shape(INNER + 2 * WIDTH, WIDTH),
        sums_one=shape_of(8, WIDTH), sums_two=shape_of(8, WIDTH),
    )
    scratch = dict(
        keys=low_shape(SEQ, INNER), values=low_shape(SEQ, INNER), bias=shape_of(SEQ, BLOCK),
        inner=shape_of(BLOCK, 128), dkeys=shape_of(SEQ, INNER), dvalues=shape_of(SEQ, INNER),
        d_query=shape_of(ROWS, INNER), d_other=low_shape(2, ROWS, INNER), got=low_shape(2, ROWS, INNER),
        hid=low_shape(ROWS, WIDTH), e_two=shape_of(ROWS, WIDTH), packed=low_shape(3, ROWS, INNER),
        e=low_shape(2, BLOCK, WIDTH), bufs=low_shape(2, 6, 64, 384),
    )
    if later:
        outs.update(total=low_shape(2, BLOCK, WIDTH), part_sum=shape_of(2, 64, WIDTH))
        scratch.update(part_bufs=low_shape(2, 6, 64, 384))
    else:
        outs.update(total=shape_of(2, 64, WIDTH), grad=shape_of(ROWS, WIDTH))
        scratch.update(low=low_shape(2, BLOCK, WIDTH))
    return fused(
        functools.partial(backward_body, later), "backward", ins, outs, scratch, 33 if later else 13, 6 if later else 7
    )


def prepare_kernel(
    boundary, segment_ids, gain_one, shift_one, gain_two, shift_two, wq, qkv_bias, dense_bias, up_bias, down_bias,
    block_out, wq_out, small_out, cos_out, sin_out, col_out, row_out,
):
    at = Place()
    for m in range(4):
        block_out[m] = boundary[0, m].astype(bf16)
    for kind in range(3):
        for h in range(HEADS):
            to, source = INNER * kind + HEAD_DIM * h, INNER * h + HEAD_DIM * kind
            wq_out[to : to + HEAD_DIM] = wq[source : source + HEAD_DIM]
    small_out[...] = jnp.zeros_like(small_out)
    for n, ref in enumerate((gain_one, shift_one, gain_two, shift_two)):
        small_out[n : n + 1] = ref[...]
    half = ROT // 2
    for kind in range(3):
        for h in range(HEADS):
            lanes = pl.ds(HEAD_DIM * h, HEAD_DIM)
            source = INNER * h + HEAD_DIM * kind
            piece = qkv_bias[:, source : source + HEAD_DIM]
            small_out[4 + kind : 5 + kind, lanes] = piece
            if kind < 2:
                small_out[9 + kind : 10 + kind, pl.ds(HEAD_DIM * h, half)] = -piece[:, half:ROT]
                small_out[9 + kind : 10 + kind, pl.ds(HEAD_DIM * h + half, half)] = piece[:, :half]
    small_out[7:8] = up_bias[...]
    small_out[8:9] = dense_bias[...] + down_bias[...]
    labels = segment_ids[at.y, pl.ds(at.z, 1)]
    start = jnp.zeros((1, SEQ), f32)
    for v in range(1, 5):
        count = jnp.sum((labels == v - 1).astype(f32), axis=1, keepdims=True)
        start = start + jnp.where(labels >= v, count, 0.0)
    cosine_lane = lax.broadcasted_iota(jnp.int32, (1, INNER), 1) % HEAD_DIM
    rotary = cosine_lane < ROT
    freqs = jnp.ones((1, INNER), f32)
    for n in range(1, half):
        freqs = jnp.where(cosine_lane % half == n, 10000.0 ** (-2.0 * n / ROT), freqs)
    for i in range(2):
        pieces = [start[:, BLOCK * (2 * i + k) : BLOCK * (2 * i + k + 1)] for k in range(2)]
        mine = jnp.where(at.c == 0, pieces[0], pieces[1])
        row_out[:, BLOCK * i : BLOCK * (i + 1)] = mine.astype(jnp.int32)
        column = jnp.broadcast_to(mine, (128, BLOCK)).T[:, 0:1]
        here = pl.ds(BLOCK * i, BLOCK)
        col_out[here] = column.astype(jnp.int32)
        spot = lax.broadcasted_iota(jnp.int32, (BLOCK, 1), 0) + (2 * i + at.c) * BLOCK
        angles = (spot.astype(f32) - column) * freqs
        cos_out[here] = jnp.where(rotary, jnp.cos(angles), 1.0)
        sin_out[here] = jnp.where(rotary, jnp.sin(angles), 0.0)


def finish_kernel(
    total, small, back, x_out, g1, s1, g2, s2, qkv_out, qkv_bias, dense_out, dense_bias, up_out, up_bias,
    down_out, down_bias, total_in, back_in, x_hold, qkv_hold, dense_hold, up_hold, down_hold, load_sems, store_sems,
):
    p = lax.axis_index("pipe")
    loads = [pltpu.make_async_copy(back.at[m], back_in.at[m], load_sems.at[m]) for m in range(4)]
    loads += [
        pltpu.make_async_copy(total.at[span], total_in.at[span], load_sems.at[4 + n])
        for n, span in enumerate((pl.ds(1536, 768), pl.ds(480, 672), pl.ds(1152, 384), pl.ds(0, 480)))
    ]
    for copy in loads:
        copy.start()
    stores = []

    def store(source, target):
        copy = pltpu.make_async_copy(source, target, store_sems.at[len(stores)])
        copy.start()
        stores.append(copy)

    for m in range(4):
        loads[m].wait()
        x_hold[m] = back_in[m].astype(f32)
        store(x_hold.at[m], x_out.at[0, m])
    loads[4].wait()
    down_hold[...] = total_in[1536:].astype(f32)
    store(down_hold, down_out.at[0])
    loads[5].wait()
    loads[6].wait()
    up_hold[:672] = total_in[480:1152].astype(f32)
    up_hold[672:] = total_in[1440:1536].astype(f32)
    store(up_hold, up_out.at[0])
    loads[7].wait()
    for h in range(HEADS):
        for kind in range(3):
            to, source = INNER * h + HEAD_DIM * kind, INNER * kind + HEAD_DIM * h
            qkv_bias[:, to : to + HEAD_DIM] = small[p, 2 + kind : 3 + kind, HEAD_DIM * h : HEAD_DIM * (h + 1)]
            for start in (source, source + HEAD_DIM // 2):
                place = start if start < 288 else start - 288 + 1152
                qkv_hold[to + start - source : to + start - source + HEAD_DIM // 2] = total_in[
                    place : place + HEAD_DIM // 2
                ].astype(f32)
    store(qkv_hold, qkv_out.at[0])
    dense_hold[...] = total_in[288:480].astype(f32)
    store(dense_hold, dense_out.at[0])
    for row, ref in ((0, g1), (1, s1), (8, g2), (9, s2), (10, dense_bias), (11, up_bias), (10, down_bias)):
        ref[...] = small[p, row : row + 1]
    for copy in stores:
        copy.wait()


def local(
    boundary,
    segment_ids,
    attn_gain,
    attn_shift,
    mlp_gain,
    mlp_shift,
    qkv_weight,
    qkv_bias,
    dense_weight,
    dense_bias,
    up_weight,
    up_bias,
    down_weight,
    down_bias,
):
    block, wq, small, cosine, sine, start_col, start_row = on_device(
        prepare_kernel, "prepare",
        [boundary, segment_ids, attn_gain, attn_shift, mlp_gain, mlp_shift, qkv_weight[0].T, qkv_bias, dense_bias, up_bias,
         down_bias],
        [None] * 11,
        [
            shape_of(4, BLOCK, WIDTH, dtype=bf16), shape_of(3 * INNER, WIDTH, dtype=bf16), shape_of(16, WIDTH),
            shape_of(ROWS, INNER), shape_of(ROWS, INNER), shape_of(ROWS, 1, dtype=jnp.int32),
            shape_of(1, ROWS, dtype=jnp.int32),
        ],
        [],
    )
    tables = (cosine, sine, start_col, start_row)
    xg, *stacks = spread(block, wq, dense_weight[0], up_weight[0], down_weight[0], small)
    zero = forward_layer(0, xg, None, stacks, tables)
    one = forward_layer(1, xg, zero.total, stacks, tables)
    back_one = backward_layer(1, xg, None, stacks, tables, one, one)
    back_zero = backward_layer(0, xg, back_one.total, stacks, tables, zero, one)
    total, small_total, back = final(
        [back_zero.grads_one, back_zero.grads_two, back_one.grads_one, back_one.grads_two],
        [back_zero.sums_one, back_zero.sums_two, back_one.sums_one, back_one.sums_two],
        [
            back_zero.total, back_one.part_sum, back_zero.grad, zero.normed, zero.inverse,
            one.middle, stacks[4],
        ],
    )
    vector = shape_of(1, WIDTH)
    vmem, any_space = pl.BlockSpec(memory_space=pltpu.VMEM), pl.BlockSpec(memory_space=pl.ANY)
    outs = list(
        pl.pallas_call(
            finish_kernel,
            out_shape=[shape_of(1, 4, BLOCK, WIDTH)] + [vector] * 4
            + [shape_of(1, 3 * INNER, WIDTH), shape_of(1, 3 * INNER), shape_of(1, INNER, WIDTH), vector]
            + [shape_of(1, WIDTH, WIDTH), vector] * 2,
            in_specs=[any_space, vmem, any_space],
            out_specs=[any_space] + [vmem] * 4 + [any_space, vmem] * 4,
            scratch_shapes=[
                pltpu.VMEM((GRAD_ROWS, WIDTH), bf16),
                pltpu.VMEM((4, BLOCK, WIDTH), bf16),
                pltpu.VMEM((4, BLOCK, WIDTH), f32),
                pltpu.VMEM((3 * INNER, WIDTH), f32),
                pltpu.VMEM((INNER, WIDTH), f32),
                pltpu.VMEM((WIDTH, WIDTH), f32),
                pltpu.VMEM((WIDTH, WIDTH), f32),
                pltpu.SemaphoreType.DMA((8,)),
                pltpu.SemaphoreType.DMA((8,)),
            ],
            compiler_params=pltpu.CompilerParams(vmem_limit_bytes=VMEM_LIMIT),
            name="finish",
        )(total, small_total, back)
    )
    outs[5] = outs[5].transpose(0, 2, 1)
    return tuple(outs)


def solution(mesh):
    in_specs = (
        P("pipe", None, "dp", None),
        P(),
        P("pipe", None),
        P("pipe", None),
        P("pipe", None),
        P("pipe", None),
        P("pipe", None, "tensor"),
        P("pipe", "tensor"),
        P("pipe", "tensor", None),
        P("pipe", None),
        P("pipe", None, "tensor"),
        P("pipe", "tensor"),
        P("pipe", "tensor", None),
        P("pipe", None),
    )
    out_specs = (
        P("pipe", None, "dp", None),
        P("pipe", None),
        P("pipe", None),
        P("pipe", None),
        P("pipe", None),
        P("pipe", None, "tensor"),
        P("pipe", "tensor"),
        P("pipe", "tensor", None),
        P("pipe", None),
        P("pipe", None, "tensor"),
        P("pipe", "tensor"),
        P("pipe", "tensor", None),
        P("pipe", None),
    )
    return jax.shard_map(local, mesh=mesh, in_specs=in_specs, out_specs=out_specs, check_vma=False)
```

time: 265 us -> 205 us (0.77)
  local copies, waits for them, and re-layouts: 20.9 us -> 0 us
  Pallas kernels: 224 us -> 204 us
  other arithmetic: 11 us -> 0 us
  starting transfers between devices: 7.44 us -> 0 us
    pallas_call x12 -> x1, Pallas kernels: 78 us -> 6.2 us  [on_device(): pl.pallas_call(kernel, grid=(1,), out_shape=outs, in_specs=[whole if spec...]
    pallas_call x2 -> x5, Pallas kernels: 37.7 us -> 96.8 us  [the longest x4 90.1 us: fused(): pl.pallas_call(kernel, out_shape=list(outs.values()), in_specs=[any_space...]
    pallas_call x1, Pallas kernels: 71 us -> 63.5 us  [final(): pl.pallas_call(final_kernel, out_shape=[jax.ShapeDtypeStruct((GRAD_ROWS,...]
    ppermute x4 -> x0, starting transfers between devices: 7.44 us -> none  [swapped(): return lax.ppermute(value, 'dp', [(n, n ^ 1) for n in range(16)])]
    unnamed x46 -> x0, local copies, waits for them, and re-layouts: 6.38 us -> none
    another operation x6 -> x0, local copies, waits for them, and re-layouts: 3.95 us -> none  [the longest x2 1.93 us: tables_of(): jnp.tile(sine, (1, HEADS))]
    slice x8 -> x0, local copies, waits for them, and re-layouts: 3.7 us -> none  [the longest x1 1.58 us: local(): total[1, 384:][None]]
    broadcast_in_dim x2 -> x0, other arithmetic: 3.49 us -> none  [the longest x1 1.93 us: local(): back.astype(f32)[None]]
  transfers between devices with their start and end apart: 4 -> 0, of which waited for: 0 -> 0; matrix products, arithmetic and copies ran while one was open for 1% -> 0% of each run, Pallas kernels for 9% -> 0%
where the time goes in v3:
time: 205 us
  Pallas kernels  204 us (100%)
    pallas_call x4, Pallas kernels, fused(): pl.pallas_call(kernel, out_shape=list(outs.values()), in_specs=[any_space...  90.1 us
    pallas_call x1, Pallas kernels, final(): pl.pallas_call(final_kernel, out_shape=[jax.ShapeDtypeStruct((GRAD_ROWS,...  63.5 us
    pallas_call x1, Pallas kernels, spread(): pl.pallas_call(spread_kernel, out_shape=[jax.ShapeDtypeStruct(s, bf16) fo...  37.8 us
    pallas_call x1, Pallas kernels, local(): pl.pallas_call(finish_kernel, out_shape=[shape_of(1, 4, BLOCK, WIDTH)] +...  6.73 us
    pallas_call x1, Pallas kernels, on_device(): pl.pallas_call(kernel, grid=(1,), out_shape=outs, in_specs=[whole if spec...  6.2 us

profile of v3, /device:TPU:1, one launch (start us, length us, event | category | flops | bytes accessed | tf_op | source)
XLA Modules:
  0.0 205.2 jit_solution(11859444214731707573)
XLA Ops:
  0.7 6.2 %prepare.1 = (bf16[4,256,768]{2,1,0:T(8,128)(2,1)}, bf16[576,768]{1,0:T(8,128)(2,1)}, f32[16,768]{1,0:T(8,128)}, f32[512,192]{1,0:T(8,128)}, f32[512,192]{1,0:T(...) custom-call(f32[1,4,256,768]{3,2,1,0:T(8,128)} %boundary.1, s32[4,4,1024]{2,1,0:T(4,128)} %segment_ids.1, f32[1,768]{1,0:T(1,128)} %gain_one.1, ...), custom_call_target="tpu_custom_call" | custom-call | tf_op jit(solution)/shard_map/prepare/pallas_call | solution.py:711
  6.8 37.8 %spread.1 = (bf16[2,2,256,768]{3,2,1,0:T(8,128)(2,1)}, bf16[2,576,768]{2,1,0:T(8,128)(2,1)}, bf16[2,192,768]{2,1,0:T(8,128)(2,1)}, bf16[2,768,768]{2,1,0:T(8,128...) custom-call(bf16[4,256,768]{2,1,0:T(8,128)(2,1)} %get-tuple-element.79.block, ...), custom_call_target="tpu_custom_call" | custom-call | tf_op jit(solution)/shard_map/spread/pallas_call | solution.py:314
  44.6 24.5 %forward.2 = (f32[512,768]{1,0:T(8,128)}, f32[512,128]{1,0:T(8,128)}, bf16[512,768]{1,0:T(8,128)(2,1)}, bf16[512,768]{1,0:T(8,128)(2,1)}, bf16[512,192]{1,0:T(8,...) custom-call(bf16[2,576,768]{2,1,0:T(8,128)(2,1)} %get-tuple-element., ...), custom_call_target="tpu_custom_call" | custom-call | tf_op jit(solution)/shard_map/forward/pallas_call | solution.py:777
  69.2 11.8 %forward.3 = (f32[512,768]{1,0:T(8,128)}, f32[512,128]{1,0:T(8,128)}, bf16[512,768]{1,0:T(8,128)(2,1)}, bf16[512,768]{1,0:T(8,128)(2,1)}, bf16[512,192]{1,0:T(8,...) custom-call(bf16[2,576,768]{2,1,0:T(8,128)(2,1)} %get-tuple-element., ...), custom_call_target="tpu_custom_call" | custom-call | tf_op jit(solution)/shard_map/forward/pallas_call | solution.py:777
  80.9 29.1 %backward.2 = (bf16[576,768]{1,0:T(8,128)(2,1)}, bf16[1728,768]{1,0:T(8,128)(2,1)}, f32[8,768]{1,0:T(8,128)}, f32[8,768]{1,0:T(8,128)}, bf16[2,256,768]{2,1,0:T(8,128)(2,1)}, /*index=5*/f32[2,64,768]{2,1,0:T(8,128)}) custom-call(bf16[2,256,768]{2,1,0:T(8,128)(2,1)} %get-tuple-element.92.refs_0_, ...), custom_call_target="tpu_custom_call" | custom-call | tf_op jit(solution)/shard_map/backward/pallas_call | solution.py:777
  110.0 24.7 %backward.3 = (bf16[576,768]{1,0:T(8,128)(2,1)}, bf16[1728,768]{1,0:T(8,128)(2,1)}, f32[8,768]{1,0:T(8,128)}, f32[8,768]{1,0:T(8,128)}, f32[2,64,768]{2,1,0:T(8,128)}, /*index=5*/f32[512,768]{1,0:T(8,128)}) custom-call(bf16[2,2,256,768]{3,2,1,0:T(8,128)(2,1)} %get-tuple-element.82.refs_2_.refs_1_.refs_0_, bf16[2,256,768]{2,1,0:T(8,128)(2,1)} %get-tuple-element.104.refs_1_, ...), custom_call_target="tpu_custom_call" | custom-call | tf_op jit(solution)/shard_map/backward/pallas_call | solution.py:777
  134.8 63.5 %final.1 = (bf16[2304,768]{1,0:T(8,128)(2,1)}, f32[2,16,768]{2,1,0:T(8,128)}, bf16[4,256,768]{2,1,0:T(8,128)(2,1)}) custom-call(bf16[576,768]{1,0:T(8,128)(2,1)} %get-tuple-element.116.f_zero, bf16[1728,768]{1,0:T(8,128)(2,1)} %get-tuple-element.117.e_zero, bf16[576,768]{1,0:T(8,128)(2,1)} %get-tuple-element.118.f_one, ...), custom_call_target="tpu_custom_call" | custom-call | tf_op jit(solution)/shard_map/final/pallas_call | solution.py:608
  198.3 6.7 %finish.1 = (f32[1,4,256,768]{3,2,1,0:T(8,128)}, f32[1,768]{1,0:T(1,128)}, f32[1,768]{1,0:T(1,128)}, f32[1,768]{1,0:T(1,128)}, f32[1,768]{1,0:T(1,128)}, /*index...) custom-call(bf16[2304,768]{1,0:T(8,128)(2,1)} %get-tuple-element.129, ...), custom_call_target="tpu_custom_call" | custom-call | tf_op jit(solution)/shard_map/finish/pallas_call | solution.py:1323

commit v4 on v3

--- a/solution.py
+++ b/solution.py
@@ -203,135 +203,6 @@
 
 def rows(start, size, step=16):
     return pl.ds(pl.multiple_of(start, step), size)
-
-
-def spread_kernel(
-    block, wq, wd, wu, wn, small, xg, oq, od, ou, on, osm,
-    hold_x, hold_s, hold_q, hold_d, hold_u, hold_n, send_sems, recv_sems, local_sems,
-):
-    at = Place()
-    p, x, y, z, c = at.p, at.x, at.y, at.z, at.c
-    greet(
-        [at.at_x(1), at.at_x(3), at.at_y(1), at.at_y(2), at.at_y(3), at.at_z(1), at.at_z(3), at.sibling()]
-    )
-    copies = Copies(send_sems, recv_sems, at.at_x(1))
-    weights = [(wq, oq), (wd, od), (wu, ou), (wn, on)]
-
-    def piece(ref, zz, cc):
-        if ref.shape[-2] == WIDTH:
-            return ref.at[rows(192 * zz + 96 * cc, 96)]
-        each = ref.shape[-2] // 4
-        return ref.at[rows(each * zz, each), pl.ds(pl.multiple_of(384 * cc, 128), 384)]
-
-    def half(ref, zz, cc, h):
-        if ref.shape[-2] == WIDTH:
-            return ref.at[rows(192 * zz + 96 * cc + 48 * h, 48)]
-        each = ref.shape[-2] // 4
-        more = (each // 2 + 15) // 16 * 16
-        size = each - more if h else more
-        return ref.at[rows(each * zz + more * h, size), pl.ds(pl.multiple_of(384 * cc, 128), 384)]
-
-    quarter = rows(64 * x, 64)
-    first = [
-        copies.send(block.at[(y + k) % 4, quarter], xg.at[p, at.low, quarter], at.at_y(k)) for k in (1, 3, 2)
-    ]
-    sent = [
-        copies.send(piece(src, z, c), piece(dst.at[p], z, c), at.partner()) for src, dst in weights
-    ]
-    sent_small = copies.send(small, osm.at[p], at.partner())
-    held = [hold_x, hold_s, hold_q, hold_d, hold_u, hold_n]
-    kept = [(block.at[y], xg.at[p, at.low]), (small, osm.at[p])] + [(s, d.at[p]) for s, d in weights]
-    inward = [
-        pltpu.make_async_copy(src, hold, local_sems.at[n]) for n, ((src, _), hold) in enumerate(zip(kept, held))
-    ]
-    for copy in inward:
-        copy.start()
-    outward = []
-    for n, ((_, dst), hold) in enumerate(zip(kept, held)):
-        inward[n].wait()
-        copy = pltpu.make_async_copy(hold, dst, local_sems.at[n + 6])
-        copy.start()
-        outward.append(copy)
-    gathers = []
-    for k, index in zip((1, 3, 2), first):
-        source = (y + 4 - k) % 4
-        slot = xg.at[source // 2, source % 2]
-        copies.landed(index, slot.at[quarter])
-        gather = RingGather(
-            copies,
-            x,
-            at.at_x(1),
-            at.at_x(3),
-            lambda j, slot=slot: slot.at[rows(64 * j, 64)],
-            lambda j, h, slot=slot: slot.at[rows(64 * j + 32 * h, 32)],
-        )
-        gather.start()
-        gathers.append(gather)
-    others = [dst.at[1 - p] for _, dst in weights]
-    rings, shared = [], []
-    for other, index in zip(others, sent):
-        copies.landed(index, piece(other, z, c))
-        ring = RingGather(
-            copies,
-            z,
-            at.at_z(1),
-            at.at_z(3),
-            lambda j, other=other: piece(other, j, c),
-            lambda j, h, other=other: half(other, j, c, h),
-        )
-        ring.start()
-        rings.append(ring)
-        mine = piece(other, z, c)
-        shared.append((copies.send(mine, mine, at.sibling()), piece(other, z, 1 - c)))
-    for gather in gathers:
-        gather.relay()
-    for other, ring in zip(others, rings):
-        ring.relay()
-        for j in ((z + 3) % 4, (z + 1) % 4):
-            mine = piece(other, j, c)
-            shared.append((copies.send(mine, mine, at.sibling()), piece(other, j, 1 - c)))
-    for gather in gathers:
-        gather.finish()
-    for other, ring in zip(others, rings):
-        ring.finish()
-        j = (z + 2) % 4
-        mine = piece(other, j, c)
-        shared.append((copies.send(mine, mine, at.sibling()), piece(other, j, 1 - c)))
-    copies.landed(sent_small, osm.at[1 - p])
-    for index, view in shared:
-        copies.landed(index, view)
-    for copy in outward:
-        copy.wait()
-    copies.drain()
-
-
-SPREAD_COPIES = 3 + 4 + 1 + 12 + 16 + 16
-
-
-def spread(block, wq, wd, wu, wn, small):
-    any_space = pl.BlockSpec(memory_space=pl.ANY)
-    shapes = [(2, 2, BLOCK, WIDTH)] + [(2,) + w.shape for w in (wq, wd, wu, wn)]
-    return pl.pallas_call(
-        spread_kernel,
-        out_shape=[jax.ShapeDtypeStruct(s, bf16) for s in shapes]
-        + [jax.ShapeDtypeStruct((2,) + small.shape, f32)],
-        in_specs=[any_space] * 6,
-        out_specs=[any_space] * 6,
-        scratch_shapes=[
-            pltpu.VMEM((BLOCK, WIDTH), bf16),
-            pltpu.VMEM(small.shape, f32),
-        ]
-        + [pltpu.VMEM(w.shape, bf16) for w in (wq, wd, wu, wn)]
-        + [
-            pltpu.SemaphoreType.DMA((SPREAD_COPIES,)),
-            pltpu.SemaphoreType.DMA((SPREAD_COPIES,)),
-            pltpu.SemaphoreType.DMA((12,)),
-        ],
-        compiler_params=pltpu.CompilerParams(
-            collective_id=0, has_side_effects=True, vmem_limit_bytes=VMEM_LIMIT
-        ),
-        name="spread",
-    )(block, wq, wd, wu, wn, small)
 
 
 PAIRS = 3
@@ -702,24 +573,6 @@
     return jax.ShapeDtypeStruct(dims, dtype)
 
 
-def at_layer(layer, *dims):
-    return pl.BlockSpec((1,) + dims, lambda i: (layer,) + (0,) * len(dims))
-
-
-def on_device(kernel, name, args, specs, outs, scratch):
-    whole = pl.BlockSpec(memory_space=pltpu.VMEM)
-    return pl.pallas_call(
-        kernel,
-        grid=(1,),
-        out_shape=outs,
-        in_specs=[whole if spec is None else spec for spec in specs],
-        out_specs=[whole] * len(outs),
-        scratch_shapes=scratch,
-        compiler_params=pltpu.CompilerParams(vmem_limit_bytes=VMEM_LIMIT),
-        name=name,
-    )(*args)
-
-
 def norm_back(scaled, normed, inverse):
     inner = scaled - jnp.mean(scaled, axis=-1, keepdims=True)
     inner = inner - normed * jnp.mean(scaled * normed, axis=-1, keepdims=True)
@@ -727,12 +580,13 @@
 
 
 class Env:
-    def __init__(self, refs, ins, outs, scratch):
+    def __init__(self, refs, ins, outs, scratch, raw):
         refs = list(refs)
         sources = {name: refs.pop(0) for name in ins}
+        self.raw = types.SimpleNamespace(**{name: refs.pop(0) for name in raw})
         self.targets = {name: refs.pop(0) for name in outs}
         self.v = types.SimpleNamespace(**{name: refs.pop(0) for name in list(ins) + list(outs) + list(scratch)})
-        self.send_sems, self.recv_sems, load_sems, self.store_sems = refs
+        self.send_sems, self.recv_sems, load_sems, self.store_sems, self.local_sems = refs
         self.held = [getattr(self.v, name) for name in ins]
         self.kept = [getattr(self.v, name) for name in outs]
         self.targets = list(self.targets.values())
@@ -764,20 +618,20 @@
             copy.wait()
 
 
-def fused(body, name, ins, outs, scratch, copies, collective_id):
+def fused(body, name, ins, outs, scratch, copies, collective_id, raw={}, local_copies=1):
     def kernel(*refs):
-        env = Env(refs, ins, outs, scratch)
+        env = Env(refs, ins, outs, scratch, raw)
         body(env)
         env.close()
 
     any_space = pl.BlockSpec(memory_space=pl.ANY)
-    arrays = [array for array, _ in ins.values()]
+    arrays = [array for array, _ in ins.values()] + list(raw.values())
     held = [pltpu.VMEM(array.shape if index is None else array.shape[1:], array.dtype) for array, index in ins.values()]
     kept = [pltpu.VMEM(s.shape, s.dtype) for s in list(outs.values()) + list(scratch.values())]
     got = pl.pallas_call(
         kernel,
         out_shape=list(outs.values()),
-        in_specs=[any_space] * len(ins),
+        in_specs=[any_space] * len(arrays),
         out_specs=[any_space] * len(outs),
         scratch_shapes=held
         + kept
@@ -786,6 +640,7 @@
             pltpu.SemaphoreType.DMA((copies,)),
             pltpu.SemaphoreType.DMA((len(ins),)),
             pltpu.SemaphoreType.DMA((len(outs),)),
+            pltpu.SemaphoreType.DMA((local_copies,)),
         ],
         compiler_params=pltpu.CompilerParams(
             collective_id=collective_id, has_side_effects=True, vmem_limit_bytes=VMEM_LIMIT
@@ -824,18 +679,24 @@
     at, v = Place(), env.v
     greet([at.sibling()] if later else [at.sibling(), at.at_x(1), at.at_x(3)])
     copies = Copies(env.send_sems, env.recv_sems, at.sibling())
+    forward_steps(
+        later, at, copies, v, env.done,
+        lambda: env.need(v.wq, v.small, v.x, v.cos, v.sin, v.add, v.before),
+        lambda: env.need(v.up),
+        lambda: env.need(v.dense, v.down, v.starts),
+    )
+    copies.drain()
+
+
+def forward_steps(later, at, copies, v, done, for_front, for_feed, for_mix):
+    for_front()
     wq, wt, small = v.wq, v.wt, v.small
-    env.need(v.wq, v.small)
     turn = turner()
     for i in range(2):
         wt[INNER * i : INNER * (i + 1)] = nn(turn, wq[INNER * i : INNER * (i + 1)]).astype(bf16)
 
     def row(i, wide=WIDTH):
         return small[i : i + 1, :wide]
-
-    env.need(v.x, v.cos, v.sin)
-    if later:
-        env.need(v.add, v.before)
 
     def front(i, carry):
         here = chunk_rows(i)
@@ -863,10 +724,10 @@
 
     lax.fori_loop(0, 2, front, 0)
     swap = copies.send(v.own, v.other, at.sibling())
-    env.done(v.normed, v.inverse, v.first, v.second, v.query, v.own)
+    done(v.normed, v.inverse, v.first, v.second, v.query, v.own)
     if later:
-        env.done(v.middle)
-    env.need(v.up)
+        done(v.middle)
+    for_feed()
 
     def feed(i, carry):
         here = pl.ds(pl.multiple_of(i * 128, 128), 128)
@@ -878,13 +739,13 @@
         return carry
 
     lax.fori_loop(0, 4, feed, 0)
-    env.done(v.active, v.slope)
+    done(v.active, v.slope)
     copies.landed(swap, v.other)
-    env.done(v.other)
+    done(v.other)
     keys, values, bias, logs = v.keys, v.values, v.bias, v.logs
     gather_keys(v.own, v.other, keys, values)
     logs[...] = jnp.zeros_like(logs)
-    env.need(v.dense, v.down, v.starts)
+    for_mix()
     sums = {}
     for block, span in reversed(SPANS):
         here, n = pl.ds(block * BLOCK, BLOCK), span * BLOCK
@@ -908,13 +769,12 @@
             sums[block] = block_sum(at, copies, v.part, v.bufs, block)
             sums[block].start()
     v.log[...] = logs[...].T
-    env.done(v.mixed, v.log)
+    done(v.mixed, v.log)
     if later:
-        env.done(v.part)
+        done(v.part)
     else:
         reduce_and_gather(at, copies, sums, v.total, ())
-        env.done(v.total)
-    copies.drain()
+        done(v.total)
 
 
 def reduce_and_gather(at, copies, sums, out, between):
@@ -1105,35 +965,50 @@
     return shape_of(*dims, dtype=bf16)
 
 
-def forward_layer(layer, xg, add, stacks, tables):
-    wq, wd, wu, wn, small = stacks
-    cosine, sine, start_col, _ = tables
-    later = add is not None
-    ins = dict(wq=(wq, layer), small=(small, layer), x=(xg, 0))
-    if later:
-        ins.update(add=(add, None), before=(small, 0))
-    ins.update(
-        cos=(cosine, None), sin=(sine, None), up=(wu, layer), dense=(wd, layer), down=(wn, layer),
-        starts=(start_col, None),
-    )
-    outs = dict(
+def forward_outs():
+    return dict(
         normed=shape_of(ROWS, WIDTH), inverse=shape_of(ROWS, 128), first=low_shape(ROWS, WIDTH),
         second=low_shape(ROWS, WIDTH), query=low_shape(ROWS, INNER), own=low_shape(2, ROWS, INNER),
         other=low_shape(2, ROWS, INNER), active=low_shape(ROWS, WIDTH), slope=low_shape(ROWS, WIDTH),
         mixed=low_shape(ROWS, INNER), log=shape_of(128, ROWS),
     )
-    scratch = dict(
+
+
+def forward_scratch():
+    return dict(
         wt=low_shape(2 * INNER, WIDTH), keys=low_shape(SEQ, INNER), values=low_shape(SEQ, INNER),
         logs=shape_of(ROWS, 128), bias=shape_of(BLOCK, SEQ),
     )
-    if later:
-        outs.update(middle=shape_of(ROWS, WIDTH), part=low_shape(2, BLOCK, WIDTH))
-    else:
-        outs.update(total=low_shape(2, BLOCK, WIDTH))
-        scratch.update(part=low_shape(2, BLOCK, WIDTH), bufs=low_shape(2, 6, 64, 384))
-    return fused(
-        functools.partial(forward_body, later), "forward", ins, outs, scratch, 1 if later else 21, 5 if later else 4
-    )
+
+
+def start_layer(boundary, segment_ids, vectors, wq, wd, wu, wn):
+    ins = dict(raw_q=(wq, None))
+    ins.update({name: (array, None) for name, array in vectors.items()})
+    ins.update(segment_ids=(segment_ids, None))
+    outs = dict(
+        wq=low_shape(2, 3 * INNER, WIDTH), wu=low_shape(2, WIDTH, WIDTH), wd=low_shape(2, INNER, WIDTH),
+        wn=low_shape(2, WIDTH, WIDTH), smalls=shape_of(2, 16, WIDTH), xg=low_shape(2, 2, BLOCK, WIDTH),
+        cos=shape_of(ROWS, INNER), sin=shape_of(ROWS, INNER), start_col=shape_of(ROWS, 1, dtype=jnp.int32),
+        start_row=shape_of(1, ROWS, dtype=jnp.int32), total=low_shape(2, BLOCK, WIDTH), **forward_outs(),
+    )
+    scratch = dict(
+        quarters=shape_of(4, 64, WIDTH), quarters_low=low_shape(4, 64, WIDTH), block=shape_of(BLOCK, WIDTH),
+        vectors=shape_of(16, WIDTH), part=low_shape(2, BLOCK, WIDTH), bufs=low_shape(2, 6, 64, 384),
+        **forward_scratch(),
+    )
+    raw = dict(boundary=boundary, up=wu, dense=wd, down=wn)
+    return fused(start_body, "start", ins, outs, scratch, 52 + 21, 0, raw, 5)
+
+
+def forward_layer(layer, xg, add, stacks, tables):
+    wq, wd, wu, wn, small = stacks
+    cosine, sine, start_col, _ = tables
+    ins = dict(
+        wq=(wq, layer), small=(small, layer), x=(xg, 0), add=(add, None), before=(small, 0), cos=(cosine, None),
+        sin=(sine, None), up=(wu, layer), dense=(wd, layer), down=(wn, layer), starts=(start_col, None),
+    )
+    outs = dict(middle=shape_of(ROWS, WIDTH), part=low_shape(2, BLOCK, WIDTH), **forward_outs())
+    return fused(functools.partial(forward_body, True), "forward", ins, outs, forward_scratch(), 1, 5)
 
 
 def backward_layer(layer, xg, add, stacks, tables, kept, kept_one):
@@ -1176,53 +1051,184 @@
     )
 
 
-def prepare_kernel(
-    boundary, segment_ids, gain_one, shift_one, gain_two, shift_two, wq, qkv_bias, dense_bias, up_bias, down_bias,
-    block_out, wq_out, small_out, cos_out, sin_out, col_out, row_out,
-):
-    at = Place()
-    for m in range(4):
-        block_out[m] = boundary[0, m].astype(bf16)
+def start_body(env):
+    at, v, raw = Place(), env.v, env.raw
+    p, x, y, z, c = at.p, at.x, at.y, at.z, at.c
+    quarter = rows(64 * x, 64)
+    local = []
+
+    def bring(source, target):
+        copy = pltpu.make_async_copy(source, target, env.local_sems.at[len(local)])
+        copy.start()
+        local.append(copy)
+        return copy
+
+    quarters_in = bring(raw.boundary.at[0, :, quarter], v.quarters)
+    up_in = bring(raw.up, v.wu.at[p])
+    dense_in = bring(raw.dense, v.wd.at[p])
+    down_in = bring(raw.down, v.wn.at[p])
+    block_in = bring(raw.boundary.at[0, y], v.block)
+    greet(
+        [at.at_x(1), at.at_x(3), at.at_y(1), at.at_y(2), at.at_y(3), at.at_z(1), at.at_z(3), at.sibling()]
+    )
+    copies = Copies(env.send_sems, env.recv_sems, at.at_x(1))
+
+    def piece(ref, zz, cc):
+        if ref.shape[-2] == WIDTH:
+            return ref.at[rows(192 * zz + 96 * cc, 96)]
+        each = ref.shape[-2] // 4
+        return ref.at[rows(each * zz, each), pl.ds(pl.multiple_of(384 * cc, 128), 384)]
+
+    def half(ref, zz, cc, h):
+        if ref.shape[-2] == WIDTH:
+            return ref.at[rows(192 * zz + 96 * cc + 48 * h, 48)]
+        each = ref.shape[-2] // 4
+        more = (each // 2 + 15) // 16 * 16
+        size = each - more if h else more
+        return ref.at[rows(each * zz + more * h, size), pl.ds(pl.multiple_of(384 * cc, 128), 384)]
+
+    quarters_in.wait()
+    v.quarters_low[...] = v.quarters[...].astype(bf16)
+    first = [
+        copies.send(v.quarters_low.at[(y + k) % 4], v.xg.at[p, at.low, quarter], at.at_y(k)) for k in (1, 3, 2)
+    ]
+    env.need(v.raw_q)
     for kind in range(3):
         for h in range(HEADS):
             to, source = INNER * kind + HEAD_DIM * h, INNER * h + HEAD_DIM * kind
-            wq_out[to : to + HEAD_DIM] = wq[source : source + HEAD_DIM]
-    small_out[...] = jnp.zeros_like(small_out)
-    for n, ref in enumerate((gain_one, shift_one, gain_two, shift_two)):
-        small_out[n : n + 1] = ref[...]
-    half = ROT // 2
+            v.wq[p, to : to + HEAD_DIM] = v.raw_q[source : source + HEAD_DIM]
+    stacks = [v.wq, v.wu, v.wd, v.wn]
+    sent = []
+    for stack, copy in zip(stacks, (None, up_in, dense_in, down_in)):
+        if copy is not None:
+            copy.wait()
+        sent.append(copies.send(piece(stack.at[p], z, c), piece(stack.at[p], z, c), at.partner()))
+    env.need(v.gain_one, v.shift_one, v.gain_two, v.shift_two, v.qkv_bias, v.dense_bias, v.up_bias, v.down_bias)
+    vectors = v.vectors
+    vectors[...] = jnp.zeros_like(vectors)
+    for n, ref in enumerate((v.gain_one, v.shift_one, v.gain_two, v.shift_two)):
+        vectors[n : n + 1] = ref[...]
+    turned = ROT // 2
     for kind in range(3):
         for h in range(HEADS):
-            lanes = pl.ds(HEAD_DIM * h, HEAD_DIM)
             source = INNER * h + HEAD_DIM * kind
-            piece = qkv_bias[:, source : source + HEAD_DIM]
-            small_out[4 + kind : 5 + kind, lanes] = piece
+            part = v.qkv_bias[:, source : source + HEAD_DIM]
+            vectors[4 + kind : 5 + kind, pl.ds(HEAD_DIM * h, HEAD_DIM)] = part
             if kind < 2:
-                small_out[9 + kind : 10 + kind, pl.ds(HEAD_DIM * h, half)] = -piece[:, half:ROT]
-                small_out[9 + kind : 10 + kind, pl.ds(HEAD_DIM * h + half, half)] = piece[:, :half]
-    small_out[7:8] = up_bias[...]
-    small_out[8:9] = dense_bias[...] + down_bias[...]
-    labels = segment_ids[at.y, pl.ds(at.z, 1)]
+                vectors[9 + kind : 10 + kind, pl.ds(HEAD_DIM * h, turned)] = -part[:, turned:ROT]
+                vectors[9 + kind : 10 + kind, pl.ds(HEAD_DIM * h + turned, turned)] = part[:, :turned]
+    vectors[7:8] = v.up_bias[...]
+    vectors[8:9] = v.dense_bias[...] + v.down_bias[...]
+    v.smalls[p] = vectors[...]
+    sent_small = copies.send(vectors, v.smalls.at[p], at.partner())
+    block_in.wait()
+    v.xg[p, at.low] = v.block[...].astype(bf16)
+    env.need(v.segment_ids)
+    labels = v.segment_ids[at.y, pl.ds(at.z, 1)]
     start = jnp.zeros((1, SEQ), f32)
-    for v in range(1, 5):
-        count = jnp.sum((labels == v - 1).astype(f32), axis=1, keepdims=True)
-        start = start + jnp.where(labels >= v, count, 0.0)
-    cosine_lane = lax.broadcasted_iota(jnp.int32, (1, INNER), 1) % HEAD_DIM
-    rotary = cosine_lane < ROT
+    for label in range(1, 5):
+        count = jnp.sum((labels == label - 1).astype(f32), axis=1, keepdims=True)
+        start = start + jnp.where(labels >= label, count, 0.0)
+    lane = lax.broadcasted_iota(jnp.int32, (1, INNER), 1) % HEAD_DIM
     freqs = jnp.ones((1, INNER), f32)
-    for n in range(1, half):
-        freqs = jnp.where(cosine_lane % half == n, 10000.0 ** (-2.0 * n / ROT), freqs)
+    for n in range(1, turned):
+        freqs = jnp.where(lane % turned == n, 10000.0 ** (-2.0 * n / ROT), freqs)
+    angles = []
     for i in range(2):
         pieces = [start[:, BLOCK * (2 * i + k) : BLOCK * (2 * i + k + 1)] for k in range(2)]
-        mine = jnp.where(at.c == 0, pieces[0], pieces[1])
-        row_out[:, BLOCK * i : BLOCK * (i + 1)] = mine.astype(jnp.int32)
+        mine = jnp.where(c == 0, pieces[0], pieces[1])
+        v.start_row[:, BLOCK * i : BLOCK * (i + 1)] = mine.astype(jnp.int32)
         column = jnp.broadcast_to(mine, (128, BLOCK)).T[:, 0:1]
-        here = pl.ds(BLOCK * i, BLOCK)
-        col_out[here] = column.astype(jnp.int32)
-        spot = lax.broadcasted_iota(jnp.int32, (BLOCK, 1), 0) + (2 * i + at.c) * BLOCK
-        angles = (spot.astype(f32) - column) * freqs
-        cos_out[here] = jnp.where(rotary, jnp.cos(angles), 1.0)
-        sin_out[here] = jnp.where(rotary, jnp.sin(angles), 0.0)
+        v.start_col[BLOCK * i : BLOCK * (i + 1)] = column.astype(jnp.int32)
+        spot = lax.broadcasted_iota(jnp.int32, (BLOCK, 1), 0) + (2 * i + c) * BLOCK
+        angles.append((spot.astype(f32) - column) * freqs)
+
+    def table(ref, function, rest):
+        for i in range(2):
+            ref[BLOCK * i : BLOCK * (i + 1)] = jnp.where(lane < ROT, function(angles[i]), rest)
+
+    gathers = []
+    for k, index in zip((1, 3, 2), first):
+        source = (y + 4 - k) % 4
+        slot = v.xg.at[source // 2, source % 2]
+        copies.landed(index, slot.at[quarter])
+        gather = RingGather(
+            copies, x, at.at_x(1), at.at_x(3),
+            lambda j, slot=slot: slot.at[rows(64 * j, 64)],
+            lambda j, h, slot=slot: slot.at[rows(64 * j + 32 * h, 32)],
+        )
+        gather.start()
+        gathers.append(gather)
+    others = [stack.at[1 - p] for stack in stacks]
+    rings, shared = [], []
+
+    def share(n, j):
+        mine = piece(others[n], j, c)
+        shared[n].append((copies.send(mine, mine, at.sibling()), piece(others[n], j, 1 - c)))
+
+    def begin(n):
+        other = others[n]
+        copies.landed(sent[n], piece(other, z, c))
+        ring = RingGather(
+            copies, z, at.at_z(1), at.at_z(3),
+            lambda j: piece(other, j, c), lambda j, h: half(other, j, c, h),
+        )
+        ring.start()
+        rings.append(ring)
+        shared.append([])
+        share(n, z)
+
+    def relay(n):
+        rings[n].relay()
+        share(n, (z + 3) % 4)
+        share(n, (z + 1) % 4)
+
+    def finish(n):
+        rings[n].finish()
+        share(n, (z + 2) % 4)
+
+    def arrived(n):
+        for index, view in shared[n]:
+            copies.landed(index, view)
+        env.done(stacks[n])
+
+    begin(0)
+    begin(1)
+    table(v.cos, jnp.cos, 1.0)
+    begin(2)
+    begin(3)
+    table(v.sin, jnp.sin, 0.0)
+    env.done(v.cos, v.sin, v.start_col, v.start_row)
+    for gather in gathers:
+        gather.relay()
+    relay(0)
+    relay(1)
+
+    def for_front():
+        finish(0)
+        for gather in gathers:
+            gather.finish()
+        copies.landed(sent_small, v.smalls.at[1 - p])
+        relay(2)
+        relay(3)
+        arrived(0)
+        env.done(v.xg, v.smalls)
+
+    def for_feed():
+        finish(1)
+        finish(2)
+        finish(3)
+        arrived(1)
+
+    def for_mix():
+        arrived(2)
+        arrived(3)
+
+    views = types.SimpleNamespace(**vars(v))
+    views.wq, views.up, views.dense, views.down = [stack.at[0] for stack in stacks]
+    views.small, views.x, views.starts = v.smalls.at[0], v.xg.at[0], v.start_col
+    forward_steps(False, at, copies, views, env.done, for_front, for_feed, for_mix)
+    copies.drain()
 
 
 def finish_kernel(
@@ -1291,21 +1297,15 @@
     down_weight,
     down_bias,
 ):
-    block, wq, small, cosine, sine, start_col, start_row = on_device(
-        prepare_kernel, "prepare",
-        [boundary, segment_ids, attn_gain, attn_shift, mlp_gain, mlp_shift, qkv_weight[0].T, qkv_bias, dense_bias, up_bias,
-         down_bias],
-        [None] * 11,
-        [
-            shape_of(4, BLOCK, WIDTH, dtype=bf16), shape_of(3 * INNER, WIDTH, dtype=bf16), shape_of(16, WIDTH),
-            shape_of(ROWS, INNER), shape_of(ROWS, INNER), shape_of(ROWS, 1, dtype=jnp.int32),
-            shape_of(1, ROWS, dtype=jnp.int32),
-        ],
-        [],
-    )
-    tables = (cosine, sine, start_col, start_row)
-    xg, *stacks = spread(block, wq, dense_weight[0], up_weight[0], down_weight[0], small)
-    zero = forward_layer(0, xg, None, stacks, tables)
+    vectors = dict(
+        gain_one=attn_gain, shift_one=attn_shift, gain_two=mlp_gain, shift_two=mlp_shift, qkv_bias=qkv_bias,
+        dense_bias=dense_bias, up_bias=up_bias, down_bias=down_bias,
+    )
+    zero = start_layer(
+        boundary, segment_ids, vectors, qkv_weight[0].T, dense_weight[0], up_weight[0], down_weight[0]
+    )
+    xg, stacks = zero.xg, [zero.wq, zero.wd, zero.wu, zero.wn, zero.smalls]
+    tables = (zero.cos, zero.sin, zero.start_col, zero.start_row)
     one = forward_layer(1, xg, zero.total, stacks, tables)
     back_one = backward_layer(1, xg, None, stacks, tables, one, one)
     back_zero = backward_layer(0, xg, back_one.total, stacks, tables, zero, one)

time: 205 us -> 194 us (0.946)
  Pallas kernels: 204 us -> 193 us
    pallas_call x2 -> x0, Pallas kernels: 44 us -> none  [the longest x1 37.8 us: spread(): pl.pallas_call(spread_kernel, out_shape=[jax.ShapeDtypeStruct(s, bf16) fo...]
    pallas_call x4, Pallas kernels: 90.1 us -> 124 us  [fused(): pl.pallas_call(kernel, out_shape=list(outs.values()), in_specs=[any_space...]
where the time goes in v4:
time: 194 us
  Pallas kernels  193 us (99%)
    pallas_call x4, Pallas kernels, fused(): pl.pallas_call(kernel, out_shape=list(outs.values()), in_specs=[any_space...  124 us
    pallas_call x1, Pallas kernels, final(): pl.pallas_call(final_kernel, out_shape=[jax.ShapeDtypeStruct((GRAD_ROWS,...  62 us
    pallas_call x1, Pallas kernels, local(): pl.pallas_call(finish_kernel, out_shape=[shape_of(1, 4, BLOCK, WIDTH)] +...  6.73 us

profile of v4, /device:TPU:1, one launch (start us, length us, event | category | flops | bytes accessed | tf_op | source)
XLA Modules:
  0.0 194.1 jit_solution(15447355838147926459)
XLA Ops:
  0.7 56.3 %start.1 = (bf16[2,576,768]{2,1,0:T(8,128)(2,1)}, bf16[2,768,768]{2,1,0:T(8,128)(2,1)}, bf16[2,192,768]{2,1,0:T(8,128)(2,1)}, bf16[2,768,768]{2,1,0:T(8,128)(2,1...) custom-call(bf16[576,768]{1,0:T(8,128)(2,1)} %bitcast.9, ...), custom_call_target="tpu_custom_call" | custom-call | tf_op jit(solution)/shard_map/start/pallas_call | solution.py:631
  56.9 14.8 %forward.1 = (f32[512,768]{1,0:T(8,128)}, bf16[2,256,768]{2,1,0:T(8,128)(2,1)}, f32[512,768]{1,0:T(8,128)}, f32[512,128]{1,0:T(8,128)}, bf16[512,768]{1,0:T(8,12...) custom-call(bf16[2,576,768]{2,1,0:T(8,128)(2,1)} %get-tuple-element., ...), custom_call_target="tpu_custom_call" | custom-call | tf_op jit(solution)/shard_map/forward/pallas_call | solution.py:631
  71.7 28.3 %backward.2 = (bf16[576,768]{1,0:T(8,128)(2,1)}, bf16[1728,768]{1,0:T(8,128)(2,1)}, f32[8,768]{1,0:T(8,128)}, f32[8,768]{1,0:T(8,128)}, bf16[2,256,768]{2,1,0:T(8,128)(2,1)}, /*index=5*/f32[2,64,768]{2,1,0:T(8,128)}) custom-call(bf16[2,256,768]{2,1,0:T(8,128)(2,1)} %get-tuple-element.86.refs_0_, ...), custom_call_target="tpu_custom_call" | custom-call | tf_op jit(solution)/shard_map/backward/pallas_call | solution.py:631
  100.0 25.1 %backward.3 = (bf16[576,768]{1,0:T(8,128)(2,1)}, bf16[1728,768]{1,0:T(8,128)(2,1)}, f32[8,768]{1,0:T(8,128)}, f32[8,768]{1,0:T(8,128)}, f32[2,64,768]{2,1,0:T(8,128)}, /*index=5*/f32[512,768]{1,0:T(8,128)}) custom-call(bf16[2,2,256,768]{3,2,1,0:T(8,128)(2,1)} %get-tuple-element.76.refs_2_.refs_1_.refs_0_, bf16[2,256,768]{2,1,0:T(8,128)(2,1)} %get-tuple-element.98.refs_1_, ...), custom_call_target="tpu_custom_call" | custom-call | tf_op jit(solution)/shard_map/backward/pallas_call | solution.py:631
  125.2 62.0 %final.1 = (bf16[2304,768]{1,0:T(8,128)(2,1)}, f32[2,16,768]{2,1,0:T(8,128)}, bf16[4,256,768]{2,1,0:T(8,128)(2,1)}) custom-call(bf16[576,768]{1,0:T(8,128)(2,1)} %get-tuple-element.110.f_zero, bf16[1728,768]{1,0:T(8,128)(2,1)} %get-tuple-element.111.e_zero, bf16[576,768]{1,0:T(8,128)(2,1)} %get-tuple-element.112.f_one, ...), custom_call_target="tpu_custom_call" | custom-call | tf_op jit(solution)/shard_map/final/pallas_call | solution.py:479
  187.2 6.7 %finish.1 = (f32[1,4,256,768]{3,2,1,0:T(8,128)}, f32[1,768]{1,0:T(1,128)}, f32[1,768]{1,0:T(1,128)}, f32[1,768]{1,0:T(1,128)}, f32[1,768]{1,0:T(1,128)}, /*index...) custom-call(bf16[2304,768]{1,0:T(8,128)(2,1)} %get-tuple-element.123, ...), custom_call_target="tpu_custom_call" | custom-call | tf_op jit(solution)/shard_map/finish/pallas_call | solution.py:1323

commit v5 on v4

--- a/solution.py
+++ b/solution.py
@@ -93,9 +93,15 @@
             device_id_type=MESH,
         ).wait_recv()
 
+    def sent(self, which):
+        for k in which:
+            self.started[k].wait_send()
+            self.started[k] = None
+
     def drain(self):
         for copy in self.started:
-            copy.wait_send()
+            if copy is not None:
+                copy.wait_send()
 
 
 class RingSum:
@@ -205,55 +211,57 @@
     return pl.ds(pl.multiple_of(start, step), size)
 
 
-PAIRS = 3
-LANES = 128
-
-
-class Flow:
-    def __init__(self, at, copies, chip, own_half, out, cols):
-        self.at, self.copies, self.cols = at, copies, cols
-        self.chip, self.own_half, self.out = chip.at[:, :, cols], own_half.at[:, :, cols], out.at[:, cols]
-        self.base, self.other_base = 1152 * at.c, 1152 * (1 - at.c)
-
-    def send_core(self, layers):
+GROUPS = ((0, 384, True), (640, 256, False), (384, 256, True), (896, 256, False))
+HALF_ROWS = GRAD_ROWS // 2
+F_ROWS, E_ROWS = 288, 864
+FLOW_COPIES = 80
+SLOTS = 9
+
+
+class GradFlow:
+    def __init__(self, at, copies, sources, chip, own, out, group, bufs, one, tail):
+        self.at, self.copies, self.sources = at, copies, sources
+        self.chip, self.own, self.out = chip, own, out
+        self.start, self.count, y_first = group
+        self.chunk, self.part = self.count // 4, self.count // 8
+        self.bufs, self.one, self.tail = bufs, one, tail
+        over_y, over_z = (at.y, at.at_y), (at.z, at.at_z)
+        (self.a, self.to_a), (self.b, self.to_b) = (over_y, over_z) if y_first else (over_z, over_y)
+        self.base, self.other_base = HALF_ROWS * at.c + self.start, HALF_ROWS * (1 - at.c) + self.start
+
+    def pieces(self, core):
+        first, end = self.start, self.start + self.count
+        f, e = self.sources
+        found = []
+        if first < F_ROWS:
+            found.append((f.at[rows(F_ROWS * core + first, F_ROWS - first)], pl.ds(first, F_ROWS - first)))
+            first = F_ROWS
+        found.append((e.at[rows(E_ROWS * core + first - F_ROWS, end - first)], pl.ds(first, end - first)))
+        return found
+
+    def send_core(self):
         self.core = []
-        for layer in range(2):
-            for which, size, place in PARTS:
-                src = layers[layer][which].at[rows(size * (1 - self.at.c), size), self.cols]
-                dst = self.chip.at[layer, pl.ds(place, size)]
-                self.core.append((self.copies.send(src, dst, self.at.sibling()), dst))
-
-    def add_core(self):
+        for src, place in self.pieces(1 - self.at.c):
+            dst = self.chip.at[place]
+            self.core.append((self.copies.send(src, dst, self.at.sibling()), dst))
+
+    def quarter(self, ref, start, j):
+        return ref.at[rows(start + self.part * (j // 2), self.part), pl.ds(pl.multiple_of(384 * (j % 2), 128), 384)]
+
+    def begin(self):
+        chip, own, bufs = self.chip, self.own, self.bufs
         for index, dst in self.core:
             self.copies.landed(index, dst)
-        chip, own_half = self.chip, self.own_half
 
         def body(i, carry):
-            here = rows(i * 192, 192)
-            for layer in range(2):
-                chip[layer, here] = (chip[layer, here].astype(f32) + own_half[layer, here].astype(f32)).astype(bf16)
+            here = rows(self.start + i * 128, 128)
+            chip[here] = (chip[here].astype(f32) + own[here].astype(f32)).astype(bf16)
             return carry
 
-        lax.fori_loop(0, 6, body, 0)
-
-    def to_sibling(self, start, size):
-        view = self.out.at[rows(self.base + start, size)]
-        index = self.copies.send(view, view, self.at.sibling())
-        return index, start, size
-
-    def from_sibling(self, sent):
-        index, start, size = sent
-        self.copies.landed(index, self.out.at[rows(self.other_base + start, size)])
-
-
-class FlowYZ(Flow):
-    def begin(self, bufs, one, tail):
-        at, chip = self.at, self.chip
-        self.add_core()
-        self.one, self.tail = one, tail
+        lax.fori_loop(0, self.count // 128, body, 0)
         self.ring = RingSum(
-            self.copies, at.y, at.at_y(1), at.at_y(3),
-            lambda j, h: chip.at[j // 2, rows(576 * (j % 2) + 288 * h, 288)],
+            self.copies, self.a, self.to_a(1), self.to_a(3),
+            lambda j, h: chip.at[rows(self.start + self.chunk * j + self.part * h, self.part)],
             [bufs.at[0], bufs.at[1]], [bufs.at[2], bufs.at[3]], [bufs.at[4], bufs.at[5]],
         )
         self.ring.start()
@@ -262,253 +270,79 @@
         self.ring.relay()
 
     def second(self):
-        at, one, tail = self.at, self.one, self.tail
-        self.ring.finish(lambda h: one.at[pl.ds(288 * h, 288)])
+        one, tail = self.one, self.tail
+        self.ring.finish(lambda h: one.at[pl.ds(self.part * h, self.part)])
         self.sum = DirectSum(
-            self.copies, at.z, at.at_z, lambda j: one.at[rows(144 * j, 144)], [tail.at[n] for n in range(3)]
+            self.copies, self.b, self.to_b, lambda j: self.quarter(one, 0, j), [tail.at[n] for n in range(3)]
         )
         self.sum.start()
 
     def back(self):
-        at, out = self.at, self.out
-        start = self.base + 576 * at.low
-        self.sum.finish(out.at[rows(start + 144 * at.z, 144)])
-        self.gather = DirectGather(self.copies, at.z, at.at_z, lambda j: out.at[rows(start + 144 * j, 144)])
+        start = self.base + self.chunk * self.a
+        self.sum.finish(self.quarter(self.out, start, self.b))
+        self.gather = DirectGather(self.copies, self.b, self.to_b, lambda j: self.quarter(self.out, start, j))
         self.gather.start()
 
-    def beside(self):
-        at, out = self.at, self.out
+    def whole(self):
         self.gather.finish()
-        view = out.at[rows(self.base + 576 * at.low, 576)]
-        self.next = self.copies.send(view, view, at.beside())
-        self.half = self.to_sibling(576 * at.low, 576)
-
-    def share(self):
-        at, out = self.at, self.out
-        self.copies.landed(self.next, out.at[rows(self.base + 576 * (1 - at.low), 576)])
-        self.rest = self.to_sibling(576 * (1 - at.low), 576)
-
-    def share_rest(self):
-        pass
-
-    def end(self):
-        self.from_sibling(self.half)
-        self.from_sibling(self.rest)
-
-
-class FlowZY(Flow):
-    def begin(self, bufs, one, tail):
-        at, chip = self.at, self.chip
-        self.add_core()
-        self.one, self.tail = one, tail
-        self.ring = RingSum(
-            self.copies, at.z, at.at_z(1), at.at_z(3),
-            lambda j, h: chip.at[h, rows(288 * j, 288)],
-            [bufs.at[0], bufs.at[1]], [bufs.at[2], bufs.at[3]], [bufs.at[4], bufs.at[5]],
+        out = self.out
+        self.ring = RingGather(
+            self.copies, self.a, self.to_a(1), self.to_a(3),
+            lambda j: out.at[rows(self.base + self.chunk * j, self.chunk)],
+            lambda j, h: out.at[rows(self.base + self.chunk * j + self.part * h, self.part)],
         )
         self.ring.start()
 
-    def relay(self):
-        self.ring.relay()
-
-    def second(self):
-        at, one, tail = self.at, self.one, self.tail
-        self.ring.finish(lambda h: one.at[pl.ds(288 * h, 288)])
-        self.sum = DirectSum(
-            self.copies, at.y, at.at_y, lambda j: one.at[rows(144 * j, 144)], [tail.at[n] for n in range(3)]
-        )
-        self.sum.start()
-
-    def back(self):
-        at, out = self.at, self.out
-        view = out.at[rows(self.base + 288 * at.z + 144 * at.low, 144)]
-        self.sum.finish(view)
-        self.next = self.copies.send(view, view, at.beside())
-
-    def beside(self):
-        at, out = self.at, self.out
-        self.copies.landed(self.next, out.at[rows(self.base + 288 * at.z + 144 * (1 - at.low), 144)])
-        self.gather = RingGather(
-            self.copies, at.z, at.at_z(1), at.at_z(3),
-            lambda j: out.at[rows(self.base + 288 * j, 288)],
-            lambda j, h: out.at[rows(self.base + 288 * j + 144 * h, 144)],
-        )
-        self.gather.start()
-
     def share(self):
-        self.gather.relay()
-
-    def share_rest(self):
-        self.gather.finish()
-        self.all = self.to_sibling(0, 1152)
+        self.ring.finish()
+        view = self.out.at[rows(self.base, self.count)]
+        self.shared = self.copies.send(view, view, self.at.sibling())
 
     def end(self):
-        self.from_sibling(self.all)
-
-
-PARTS = ((0, 288, 0), (1, 864, 288))
-
-
-def final_kernel(
-    f_zero, e_zero, f_one, e_one, sf_zero, se_zero, sf_one, se_one,
-    scaled, branch, grad, normed, inverse, middle, params, out, small_out, back,
-    chip, own_half, ones, bufs, tails, got, first_small, grad_rows, normed_rows, inverse_rows, middle_rows,
-    slices, send_sems, recv_sems, local_sem, half_sems, tail_sems,
-):
-    at = Place()
-    x, y, c = at.x, at.y, at.c
-    tail_loads = []
-    for source, target in ((grad, grad_rows), (normed, normed_rows), (inverse, inverse_rows), (middle, middle_rows)):
-        for h in range(2):
-            copy = pltpu.make_async_copy(
-                source.at[rows(256 * h + 64 * x, 64)], target.at[pl.ds(64 * h, 64)], tail_sems.at[len(tail_loads)]
-            )
-            copy.start()
-            tail_loads.append(copy)
-    greet(
-        [at.at_x(k) for k in (1, 2, 3)]
-        + [at.at_y(k) for k in (1, 2, 3)]
-        + [at.at_z(k) for k in (1, 2, 3)]
-        + [at.sibling()]
-    )
-    copies = Copies(send_sems, recv_sems, at.at_x(1))
-    send, landed = copies.send, copies.landed
-    quarter = rows(64 * x, 64)
-    layers = ((f_zero, e_zero), (f_one, e_one))
-    flows = []
-    for n in range(PAIRS):
-        for kind, start in ((FlowYZ, 0), (FlowZY, PAIRS * LANES)):
-            flows.append(kind(at, copies, chip, own_half, out, pl.ds(start + n * LANES, LANES)))
-    flows[0].send_core(layers)
-    flows[1].send_core(layers)
-    halves = []
-    for layer in range(2):
-        for which, size, place in PARTS:
-            copy = pltpu.make_async_copy(
-                layers[layer][which].at[rows(size * c, size)],
-                own_half.at[layer, pl.ds(place, size)],
-                half_sems.at[2 * layer + which],
-            )
-            copy.start()
-            halves.append(copy)
-    for copy in tail_loads:
-        copy.wait()
-    for h in range(2):
-        here = pl.ds(64 * h, 64)
-        value = grad_rows[here] + norm_back(scaled[h], normed_rows[here], inverse_rows[here, 0:1])
-        slices[0, h] = value.astype(bf16)
-        slices[1, h] = (middle_rows[here] + (branch[h] + params[1, 8:9])).astype(bf16)
-    home = []
-    for k in (1, 3, 2):
-        j = (y + k) % 4
-        home.append((k, send(slices.at[j // 2, j % 2], back.at[y, quarter], at.at_y(k))))
-    own = pltpu.make_async_copy(slices.at[y // 2, y % 2], back.at[y, quarter], local_sem)
-    own.start()
-    for flow in flows[2:]:
-        flow.send_core(layers)
-    for layer, refs in enumerate(((sf_zero, se_zero), (sf_one, se_one))):
-        for which, ref in enumerate(refs):
-            first_small[layer, pl.ds(8 * which, 8)] = ref[...]
-    small_x = [(k, send(first_small, got.at[k - 1], at.at_x(k))) for k in (1, 3, 2)]
-    for copy in halves:
-        copy.wait()
-
-    def slot(t):
-        for n in range(PAIRS):
-            for m in (2 * n, 2 * n + 1):
-                flow, stage = flows[m], t - n
-                if stage == 0:
-                    flow.begin(bufs.at[m], ones.at[m], tails.at[m])
-                elif 0 < stage < 7:
-                    (flow.relay, flow.second, flow.back, flow.beside, flow.share, flow.share_rest)[stage - 1]()
-
-    slot(0)
-    own.wait()
-    for k, index in home:
-        landed(index, back.at[(y + 4 - k) % 4, quarter])
-    outer = RingGather(
-        copies, x, at.at_x(1), at.at_x(3),
-        lambda j: back.at[:, rows(64 * j, 64)],
-        lambda j, h: back.at[pl.ds(2 * h, 2), rows(64 * j, 64)],
-    )
-    outer.start()
-    slot(1)
-    slot(2)
-    outer.relay()
-    for k, index in small_x:
-        landed(index, got.at[k - 1])
-    of_norms = lax.broadcasted_iota(jnp.int32, first_small.shape, 1) % 8 < 2
-    others = got[0] + got[1] + got[2]
-    small_out[...] = first_small[...] + jnp.where(of_norms, others, 0.0)
-    small_z = [(k, send(small_out, got.at[2 + k], at.at_z(k))) for k in (1, 3, 2)]
-    slot(3)
-    for k, index in small_z:
-        landed(index, got.at[2 + k])
-    for k, index in small_z:
-        copies.started[index].wait_send()
-    small_out[...] = small_out[...] + (got[3] + got[4] + got[5])
-    small_y = [(k, send(small_out, got.at[5 + k], at.at_y(k))) for k in (1, 3, 2)]
-    slot(4)
-    slot(5)
-    for k, index in small_y:
-        landed(index, got.at[5 + k])
-    for k, index in small_y:
-        copies.started[index].wait_send()
-    small_out[...] = small_out[...] + (got[6] + got[7] + got[8])
-    small_c = send(small_out, got.at[9], at.sibling())
-    slot(6)
-    landed(small_c, got.at[9])
-    copies.started[small_c].wait_send()
-    small_out[...] = small_out[...] + got[9]
-    slot(7)
-    slot(8)
-    outer.finish()
-    for flow in flows:
-        flow.end()
-    waited = {index for _, index in small_z} | {index for _, index in small_y} | {small_c}
-    for index, copy in enumerate(copies.started):
-        if index not in waited:
-            copy.wait_send()
-
-
-FINAL_COPIES = 160
-
-
-def final(grads, small, last):
-    vmem = pl.BlockSpec(memory_space=pltpu.VMEM)
-    return pl.pallas_call(
-        final_kernel,
-        out_shape=[
-            jax.ShapeDtypeStruct((GRAD_ROWS, WIDTH), bf16),
-            jax.ShapeDtypeStruct((2, 16, WIDTH), f32),
-            jax.ShapeDtypeStruct((4, BLOCK, WIDTH), bf16),
-        ],
-        in_specs=[pl.BlockSpec(memory_space=pl.ANY)] * 4 + [vmem] * 6 + [pl.BlockSpec(memory_space=pl.ANY)] * 4 + [vmem],
-        out_specs=[vmem] * 3,
-        scratch_shapes=[
-            pltpu.VMEM((2, 1152, WIDTH), bf16),
-            pltpu.VMEM((2, 1152, WIDTH), bf16),
-            pltpu.VMEM((2 * PAIRS, 576, LANES), bf16),
-            pltpu.VMEM((2 * PAIRS, 6, 288, LANES), bf16),
-            pltpu.VMEM((2 * PAIRS, 3, 144, LANES), bf16),
-            pltpu.VMEM((10, 2, 16, WIDTH), f32),
-            pltpu.VMEM((2, 16, WIDTH), f32),
-            pltpu.VMEM((128, WIDTH), f32),
-            pltpu.VMEM((128, WIDTH), f32),
-            pltpu.VMEM((128, 128), f32),
-            pltpu.VMEM((128, WIDTH), f32),
-            pltpu.VMEM((2, 2, 64, WIDTH), bf16),
-            pltpu.SemaphoreType.DMA((FINAL_COPIES,)),
-            pltpu.SemaphoreType.DMA((FINAL_COPIES,)),
-            pltpu.SemaphoreType.DMA,
-            pltpu.SemaphoreType.DMA((4,)),
-            pltpu.SemaphoreType.DMA((8,)),
-        ],
-        compiler_params=pltpu.CompilerParams(
-            collective_id=3, has_side_effects=True, vmem_limit_bytes=VMEM_LIMIT
-        ),
-        name="final",
-    )(*grads, *small, *last)
+        self.copies.landed(self.shared, self.out.at[rows(self.other_base, self.count)])
+
+
+class GradSum:
+    def __init__(self, at, copies, sources, v, out, sems):
+        bufs = ((v.bufs_a, v.one_a, v.tail_a), (v.bufs_b, v.one_b, v.tail_b), (v.bufs_c, v.one_c, v.tail_c),
+                (v.bufs_d, v.one_d, v.tail_d))
+        self.flows = [
+            GradFlow(at, copies, sources, v.chip, v.own_half, out, group, *some) for group, some in zip(GROUPS, bufs)
+        ]
+        self.halves = []
+        for flow in self.flows:
+            flow.send_core()
+            for src, place in flow.pieces(at.c):
+                copy = pltpu.make_async_copy(src, v.own_half.at[place], sems.at[len(self.halves)])
+                copy.start()
+                self.halves.append(copy)
+
+    def slot(self, t):
+        if t == 0:
+            for copy in self.halves:
+                copy.wait()
+        for n, flow in enumerate(self.flows):
+            stage = t - n // 2
+            if 0 <= stage < 8:
+                steps = (flow.begin, flow.relay, flow.second, flow.back, flow.whole, flow.relay, flow.share, flow.end)
+                steps[stage]()
+
+
+def flow_scratch():
+    shapes = dict(chip=low_shape(HALF_ROWS, WIDTH), own_half=low_shape(HALF_ROWS, WIDTH))
+    for name, (_, count, _) in zip("abcd", GROUPS):
+        shapes["bufs_" + name] = low_shape(6, count // 8, WIDTH)
+        shapes["one_" + name] = low_shape(count // 4, WIDTH)
+        shapes["tail_" + name] = low_shape(3, count // 8, 384)
+    return shapes
+
+
+def low_shape(*dims):
+    return shape_of(*dims, dtype=bf16)
+
+
+def shape_of(*dims, dtype=f32):
+    return jax.ShapeDtypeStruct(dims, dtype)
 
 
 def nn(a, b):
@@ -567,10 +401,6 @@
 
 
 ROWS = 2 * BLOCK
-
-
-def shape_of(*dims, dtype=f32):
-    return jax.ShapeDtypeStruct(dims, dtype)
 
 
 def norm_back(scaled, normed, inverse):
@@ -599,15 +429,15 @@
             self.loads.append(copy)
 
     def need(self, *refs):
-        for ref in refs:
-            n = [held is ref for held in self.held].index(True)
-            if self.loads[n] is not None:
+        for n, held in enumerate(self.held):
+            if self.loads[n] is not None and any(held is ref for ref in refs):
                 self.loads[n].wait()
                 self.loads[n] = None
 
     def done(self, *refs):
-        for ref in refs:
-            n = [kept is ref for kept in self.kept].index(True)
+        for n, ref in enumerate(self.kept):
+            if not any(ref is other for other in refs):
+                continue
             copy = pltpu.make_async_copy(ref, self.targets[n], self.store_sems.at[n])
             copy.start()
             self.stores.append(copy)
@@ -675,16 +505,30 @@
     return lambda h: out.at[block, :, pl.ds(384 * h, 384)]
 
 
-def forward_body(later, env):
+def layer_one_body(env):
     at, v = Place(), env.v
-    greet([at.sibling()] if later else [at.sibling(), at.at_x(1), at.at_x(3)])
+    greet([at.sibling(), at.at_x(1), at.at_x(3)])
     copies = Copies(env.send_sems, env.recv_sems, at.sibling())
     forward_steps(
-        later, at, copies, v, env.done,
+        True, at, copies, v, env.done,
         lambda: env.need(v.wq, v.small, v.x, v.cos, v.sin, v.add, v.before),
         lambda: env.need(v.up),
         lambda: env.need(v.dense, v.down, v.starts),
     )
+    backward_steps(True, env, at, copies)
+    copies.drain()
+
+
+def layer_zero_back_body(env):
+    at = Place()
+    greet(
+        [at.sibling()]
+        + [at.at_x(k) for k in (1, 2, 3)]
+        + [at.at_y(k) for k in (1, 2, 3)]
+        + [at.at_z(k) for k in (1, 2, 3)]
+    )
+    copies = Copies(env.send_sems, env.recv_sems, at.sibling())
+    backward_steps(False, env, at, copies)
     copies.drain()
 
 
@@ -802,11 +646,15 @@
         gathers[block].finish()
 
 
-def backward_body(later, env):
-    at, v = Place(), env.v
-    greet([at.sibling(), at.at_x(1), at.at_x(3)])
-    copies = Copies(env.send_sems, env.recv_sems, at.sibling())
+def backward_steps(later, env, at, copies):
+    v = env.v
     extra = []
+    flows = None if later else GradSum(at, copies, (env.raw.f_one, env.raw.e_one), v, v.summed_one, env.local_sems)
+
+    def slot(*which):
+        for t in which if flows else ():
+            flows.slot(t)
+
     if later:
         env.need(v.part)
         extra = [block_sum(at, copies, v.part, v.part_bufs, block) for block in (1, 0)]
@@ -828,17 +676,17 @@
             return carry
 
         lax.fori_loop(0, 2, incoming, 0)
-        env.done(v.grad)
-    keys, values, bias, inner = v.keys, v.values, v.bias, v.inner
-    env.need(v.own, v.other, v.query, v.mixed, v.log, v.dense, v.starts)
-    gather_keys(v.own, v.other, keys, values)
+    keys, values, bias, inner = v.keys, v.values, v.bias_rows, v.inner
+    env.need(v.own, v.other, v.query, v.mixed, v.log, v.dense, v.start_row)
+    if not later:
+        gather_keys(v.own, v.other, keys, values)
     inner[...] = jnp.zeros_like(inner)
     dkeys, dvalues, log = v.dkeys, v.dvalues, v.log
     for block, span in reversed(SPANS):
         here, n = pl.ds(block * BLOCK, BLOCK), span * BLOCK
         place = key_places(at.c, (n, BLOCK), 0, span)
         mine = lax.broadcasted_iota(jnp.int32, (n, BLOCK), 1) + (2 * block + at.c) * BLOCK
-        allowed = (place <= mine) & (place >= v.starts[0:1, here])
+        allowed = (place <= mine) & (place >= v.start_row[0:1, here])
         bias[:n] = jnp.where(allowed, 0.0, MASKED)
         d_mixed = nt(low[block], v.dense[...]).astype(bf16)
         product = d_mixed.astype(f32) * v.mixed[here].astype(f32)
@@ -862,6 +710,8 @@
                 dkeys[:n] += d_key
             d_query = d_query + pick(tn(d_score, keys[:n]), h)
         v.d_query[here] = d_query * HEAD_DIM ** (-0.5)
+        if block == 1:
+            slot(0)
     for n, ref in enumerate((dkeys, dvalues)):
         v.d_other[n, 0:BLOCK] = ref[BLOCK : 2 * BLOCK].astype(bf16)
         v.d_other[n, BLOCK : 2 * BLOCK] = ref[3 * BLOCK : 4 * BLOCK].astype(bf16)
@@ -889,7 +739,9 @@
         return carry
 
     lax.fori_loop(0, 2, feed, 0)
-    env.done(v.sums_two)
+    slot(1)
+    if later:
+        env.done(v.sums_two)
     for ring, block in zip(extra, (1, 0)):
         ring.finish(piece_out(v.part_sum, block))
     if later:
@@ -927,7 +779,8 @@
         sums[i].start()
         sums_one[0:1] += jnp.sum(d_first * normed[here], axis=0, keepdims=True)
         sums_one[1:2] += jnp.sum(d_first, axis=0, keepdims=True)
-    env.done(v.sums_one)
+    if later:
+        env.done(v.sums_one)
 
     grads_one, grads_two = v.grads_one, v.grads_two
 
@@ -946,23 +799,98 @@
 
     if later:
         reduce_and_gather(at, copies, sums, v.total, (grad_dense, grad_packed, grad_up, grad_down))
-        env.done(v.total)
+        env.done(v.total, v.grads_one, v.grads_two)
     else:
+        slot(2)
         grad_dense()
         sums[1].relay()
         grad_packed()
         sums[0].relay()
+        slot(3)
         grad_up()
         grad_down()
-        for block in (1, 0):
-            sums[block].finish(piece_out(v.total, block))
-        env.done(v.total)
-    env.done(v.grads_one, v.grads_two)
-    copies.drain()
-
-
-def low_shape(*dims):
-    return shape_of(*dims, dtype=bf16)
+        last_steps(env, at, copies, flows, sums)
+
+
+def last_steps(env, at, copies, flows_one, sums):
+    v, x, y = env.v, at.x, at.y
+    send, landed = copies.send, copies.landed
+    quarter = rows(64 * x, 64)
+    flows_zero = GradSum(at, copies, (v.grads_one, v.grads_two), *copied(v), env.local_sems.at[pl.ds(8, 8)])
+    for block in (1, 0):
+        sums[block].finish(piece_out(v.total, block))
+    env.need(v.part_sum, v.inverse, v.middle, v.params)
+    slices, back = v.slices, v.back
+    for h in range(2):
+        here = rows(256 * h + 64 * x, 64)
+        value = v.grad[here] + norm_back(v.total[h], v.normed[here], v.inverse[here, 0:1])
+        slices[0, h] = value.astype(bf16)
+        slices[1, h] = (v.middle[here] + (v.part_sum[h] + v.params[8:9])).astype(bf16)
+    home = []
+    for k in (1, 3, 2):
+        j = (y + k) % 4
+        home.append((k, send(slices.at[j // 2, j % 2], back.at[y, quarter], at.at_y(k))))
+    own = pltpu.make_async_copy(slices.at[y // 2, y % 2], back.at[y, quarter], env.local_sems.at[16])
+    own.start()
+    env.need(v.sf_one, v.se_one)
+    first_small, small_out, got = v.first_small, v.small_out, v.small_got
+    for layer, refs in enumerate(((v.sums_one, v.sums_two), (v.sf_one, v.se_one))):
+        for which, ref in enumerate(refs):
+            first_small[layer, pl.ds(8 * which, 8)] = ref[...]
+    small_x = [(k, send(first_small, got.at[k - 1], at.at_x(k))) for k in (1, 3, 2)]
+    flows_one.slot(4)
+    flows_zero.slot(0)
+    own.wait()
+    for k, index in home:
+        landed(index, back.at[(y + 4 - k) % 4, quarter])
+    outer = RingGather(
+        copies, x, at.at_x(1), at.at_x(3),
+        lambda j: back.at[:, rows(64 * j, 64)],
+        lambda j, h: back.at[pl.ds(2 * h, 2), rows(64 * j, 64)],
+    )
+    outer.start()
+    flows_one.slot(5)
+    flows_zero.slot(1)
+    for k, index in small_x:
+        landed(index, got.at[k - 1])
+    of_norms = lax.broadcasted_iota(jnp.int32, first_small.shape, 1) % 8 < 2
+    others = got[0] + got[1] + got[2]
+    small_out[...] = first_small[...] + jnp.where(of_norms, others, 0.0)
+    small_z = [(k, send(small_out, got.at[2 + k], at.at_z(k))) for k in (1, 3, 2)]
+    flows_one.slot(6)
+    flows_zero.slot(2)
+    outer.relay()
+    for k, index in small_z:
+        landed(index, got.at[2 + k])
+    copies.sent([index for _, index in small_z])
+    small_out[...] = small_out[...] + (got[3] + got[4] + got[5])
+    small_y = [(k, send(small_out, got.at[5 + k], at.at_y(k))) for k in (1, 3, 2)]
+    flows_one.slot(7)
+    flows_zero.slot(3)
+    flows_one.slot(8)
+    env.done(v.summed_one)
+    for k, index in small_y:
+        landed(index, got.at[5 + k])
+    copies.sent([index for _, index in small_y])
+    small_out[...] = small_out[...] + (got[6] + got[7] + got[8])
+    small_c = send(small_out, got.at[9], at.sibling())
+    flows_zero.slot(4)
+    landed(small_c, got.at[9])
+    copies.sent([small_c])
+    small_out[...] = small_out[...] + got[9]
+    env.done(v.small_out)
+    flows_zero.slot(5)
+    outer.finish()
+    env.done(v.back)
+    for t in (6, 7, 8):
+        flows_zero.slot(t)
+    env.done(v.summed_zero)
+
+
+def copied(v):
+    names = list(flow_scratch())
+    second = types.SimpleNamespace(**{name: getattr(v, name + "_zero") for name in names})
+    return second, v.summed_zero
 
 
 def forward_outs():
@@ -1000,55 +928,66 @@
     return fused(start_body, "start", ins, outs, scratch, 52 + 21, 0, raw, 5)
 
 
-def forward_layer(layer, xg, add, stacks, tables):
+def backward_results():
+    return dict(
+        grads_one=low_shape(3 * INNER, WIDTH), grads_two=low_shape(INNER + 2 * WIDTH, WIDTH),
+        sums_one=shape_of(8, WIDTH), sums_two=shape_of(8, WIDTH),
+    )
+
+
+def backward_scratch():
+    return dict(
+        bias_rows=shape_of(SEQ, BLOCK), inner=shape_of(BLOCK, 128), dkeys=shape_of(SEQ, INNER),
+        dvalues=shape_of(SEQ, INNER), d_query=shape_of(ROWS, INNER), d_other=low_shape(2, ROWS, INNER),
+        got=low_shape(2, ROWS, INNER), hid=low_shape(ROWS, WIDTH), e_two=shape_of(ROWS, WIDTH),
+        packed=low_shape(3, ROWS, INNER), e=low_shape(2, BLOCK, WIDTH), bufs=low_shape(2, 6, 64, 384),
+    )
+
+
+def layer_one(xg, add, stacks, tables):
     wq, wd, wu, wn, small = stacks
-    cosine, sine, start_col, _ = tables
+    cosine, sine, start_col, start_row = tables
     ins = dict(
-        wq=(wq, layer), small=(small, layer), x=(xg, 0), add=(add, None), before=(small, 0), cos=(cosine, None),
-        sin=(sine, None), up=(wu, layer), dense=(wd, layer), down=(wn, layer), starts=(start_col, None),
-    )
-    outs = dict(middle=shape_of(ROWS, WIDTH), part=low_shape(2, BLOCK, WIDTH), **forward_outs())
-    return fused(functools.partial(forward_body, True), "forward", ins, outs, forward_scratch(), 1, 5)
-
-
-def backward_layer(layer, xg, add, stacks, tables, kept, kept_one):
+        wq=(wq, 1), small=(small, 1), x=(xg, 0), add=(add, None), before=(small, 0), cos=(cosine, None),
+        sin=(sine, None), up=(wu, 1), dense=(wd, 1), down=(wn, 1), starts=(start_col, None), g=(xg, 1),
+        start_row=(start_row, None),
+    )
+    scratch = forward_outs()
+    outs = dict(
+        middle=shape_of(ROWS, WIDTH), normed=scratch.pop("normed"), inverse=scratch.pop("inverse"),
+        total=low_shape(2, BLOCK, WIDTH), part_sum=shape_of(2, 64, WIDTH), **backward_results(),
+    )
+    scratch.update(
+        part=low_shape(2, BLOCK, WIDTH), part_bufs=low_shape(2, 6, 64, 384), **forward_scratch(), **backward_scratch()
+    )
+    return fused(layer_one_body, "layer_one", ins, outs, scratch, 34, 5)
+
+
+def layer_zero_back(xg, one, stacks, tables, kept):
     wq, wd, wu, wn, small = stacks
     cosine, sine, _, start_row = tables
-    later = add is None
-    if later:
-        ins = dict(part=(kept.part, None), g=(xg, 1))
-    else:
-        ins = dict(
-            g=(xg, 1), add=(add, None), n_one=(kept_one.normed, None), inv_one=(kept_one.inverse, None)
-        )
-    ins.update(
+    ins = dict(
+        g=(xg, 1), add=(one.total, None), n_one=(one.normed, None), inv_one=(one.inverse, None),
         own=(kept.own, None), other=(kept.other, None), query=(kept.query, None), mixed=(kept.mixed, None),
-        log=(kept.log, None),
-    )
-    ins.update(dense=(wd, layer), starts=(start_row, None), down=(wn, layer), up=(wu, layer), small=(small, layer))
-    ins.update(slope=(kept.slope, None), normed=(kept.normed, None))
-    ins.update(cos=(cosine, None), sin=(sine, None), wq=(wq, layer))
-    ins.update(first=(kept.first, None), second=(kept.second, None), active=(kept.active, None))
+        log=(kept.log, None), dense=(wd, 0), start_row=(start_row, None), down=(wn, 0), up=(wu, 0), small=(small, 0),
+        slope=(kept.slope, None), normed=(kept.normed, None), cos=(cosine, None), sin=(sine, None), wq=(wq, 0),
+        first=(kept.first, None), second=(kept.second, None), active=(kept.active, None),
+        sf_one=(one.sums_one, None), se_one=(one.sums_two, None), part_sum=(one.part_sum, None),
+        inverse=(kept.inverse, None), middle=(one.middle, None), params=(small, 1),
+    )
     outs = dict(
-        grads_one=low_shape(3 * INNER, WIDTH), grads_two=low_shape(INNER + 2 * WIDTH, WIDTH),
-        sums_one=shape_of(8, WIDTH), sums_two=shape_of(8, WIDTH),
+        summed_zero=low_shape(GRAD_ROWS, WIDTH), summed_one=low_shape(GRAD_ROWS, WIDTH),
+        small_out=shape_of(2, 16, WIDTH), back=low_shape(4, BLOCK, WIDTH),
     )
     scratch = dict(
-        keys=low_shape(SEQ, INNER), values=low_shape(SEQ, INNER), bias=shape_of(SEQ, BLOCK),
-        inner=shape_of(BLOCK, 128), dkeys=shape_of(SEQ, INNER), dvalues=shape_of(SEQ, INNER),
-        d_query=shape_of(ROWS, INNER), d_other=low_shape(2, ROWS, INNER), got=low_shape(2, ROWS, INNER),
-        hid=low_shape(ROWS, WIDTH), e_two=shape_of(ROWS, WIDTH), packed=low_shape(3, ROWS, INNER),
-        e=low_shape(2, BLOCK, WIDTH), bufs=low_shape(2, 6, 64, 384),
-    )
-    if later:
-        outs.update(total=low_shape(2, BLOCK, WIDTH), part_sum=shape_of(2, 64, WIDTH))
-        scratch.update(part_bufs=low_shape(2, 6, 64, 384))
-    else:
-        outs.update(total=shape_of(2, 64, WIDTH), grad=shape_of(ROWS, WIDTH))
-        scratch.update(low=low_shape(2, BLOCK, WIDTH))
-    return fused(
-        functools.partial(backward_body, later), "backward", ins, outs, scratch, 33 if later else 13, 6 if later else 7
-    )
+        keys=low_shape(SEQ, INNER), values=low_shape(SEQ, INNER), low=low_shape(2, BLOCK, WIDTH),
+        grad=shape_of(ROWS, WIDTH), total=shape_of(2, 64, WIDTH), slices=low_shape(2, 2, 64, WIDTH),
+        first_small=shape_of(2, 16, WIDTH), small_got=shape_of(10, 2, 16, WIDTH),
+        **backward_results(), **backward_scratch(), **flow_scratch(),
+    )
+    scratch.update({name + "_zero": shape for name, shape in flow_scratch().items()})
+    raw = dict(f_one=one.grads_one, e_one=one.grads_two)
+    return fused(layer_zero_back_body, "layer_zero_back", ins, outs, scratch, 2 * FLOW_COPIES + 40, 7, raw, 17)
 
 
 def start_body(env):
@@ -1232,17 +1171,24 @@
 
 
 def finish_kernel(
-    total, small, back, x_out, g1, s1, g2, s2, qkv_out, qkv_bias, dense_out, dense_bias, up_out, up_bias,
+    total, total_one, small, back, x_out, g1, s1, g2, s2, qkv_out, qkv_bias, dense_out, dense_bias, up_out, up_bias,
     down_out, down_bias, total_in, back_in, x_hold, qkv_hold, dense_hold, up_hold, down_hold, load_sems, store_sems,
 ):
     p = lax.axis_index("pipe")
     loads = [pltpu.make_async_copy(back.at[m], back_in.at[m], load_sems.at[m]) for m in range(4)]
-    loads += [
-        pltpu.make_async_copy(total.at[span], total_in.at[span], load_sems.at[4 + n])
-        for n, span in enumerate((pl.ds(1536, 768), pl.ds(480, 672), pl.ds(1152, 384), pl.ds(0, 480)))
-    ]
+    spans = (pl.ds(1536, 768), pl.ds(480, 672), pl.ds(1152, 384), pl.ds(0, 480))
     for copy in loads:
         copy.start()
+    for layer, source in enumerate((total, total_one)):
+
+        @pl.when(p == layer)
+        def _(source=source):
+            for n, span in enumerate(spans):
+                pltpu.make_async_copy(source.at[span], total_in.at[span], load_sems.at[4 + n]).start()
+
+    loads += [
+        pltpu.make_async_copy(total.at[span], total_in.at[span], load_sems.at[4 + n]) for n, span in enumerate(spans)
+    ]
     stores = []
 
     def store(source, target):
@@ -1306,17 +1252,8 @@
     )
     xg, stacks = zero.xg, [zero.wq, zero.wd, zero.wu, zero.wn, zero.smalls]
     tables = (zero.cos, zero.sin, zero.start_col, zero.start_row)
-    one = forward_layer(1, xg, zero.total, stacks, tables)
-    back_one = backward_layer(1, xg, None, stacks, tables, one, one)
-    back_zero = backward_layer(0, xg, back_one.total, stacks, tables, zero, one)
-    total, small_total, back = final(
-        [back_zero.grads_one, back_zero.grads_two, back_one.grads_one, back_one.grads_two],
-        [back_zero.sums_one, back_zero.sums_two, back_one.sums_one, back_one.sums_two],
-        [
-            back_zero.total, back_one.part_sum, back_zero.grad, zero.normed, zero.inverse,
-            one.middle, stacks[4],
-        ],
-    )
+    one = layer_one(xg, zero.total, stacks, tables)
+    last = layer_zero_back(xg, one, stacks, tables, zero)
     vector = shape_of(1, WIDTH)
     vmem, any_space = pl.BlockSpec(memory_space=pltpu.VMEM), pl.BlockSpec(memory_space=pl.ANY)
     outs = list(
@@ -1325,7 +1262,7 @@
             out_shape=[shape_of(1, 4, BLOCK, WIDTH)] + [vector] * 4
             + [shape_of(1, 3 * INNER, WIDTH), shape_of(1, 3 * INNER), shape_of(1, INNER, WIDTH), vector]
             + [shape_of(1, WIDTH, WIDTH), vector] * 2,
-            in_specs=[any_space, vmem, any_space],
+            in_specs=[any_space, any_space, vmem, any_space],
             out_specs=[any_space] + [vmem] * 4 + [any_space, vmem] * 4,
             scratch_shapes=[
                 pltpu.VMEM((GRAD_ROWS, WIDTH), bf16),
@@ -1340,7 +1277,7 @@
             ],
             compiler_params=pltpu.CompilerParams(vmem_limit_bytes=VMEM_LIMIT),
             name="finish",
-        )(total, small_total, back)
+        )(last.summed_zero, last.summed_one, last.small_out, last.back)
     )
     outs[5] = outs[5].transpose(0, 2, 1)
     return tuple(outs)

time: 194 us -> 183 us (0.943)
  Pallas kernels: 193 us -> 182 us
    pallas_call x1 -> x0, Pallas kernels: 62 us -> none  [final(): pl.pallas_call(final_kernel, out_shape=[jax.ShapeDtypeStruct((GRAD_ROWS,...]
    pallas_call x4 -> x3, Pallas kernels: 124 us -> 176 us  [fused(): pl.pallas_call(kernel, out_shape=list(outs.values()), in_specs=[any_space...]
where the time goes in v5:
time: 183 us
  Pallas kernels  182 us (99%)
    pallas_call x3, Pallas kernels, fused(): pl.pallas_call(kernel, out_shape=list(outs.values()), in_specs=[any_space...  176 us
    pallas_call x1, Pallas kernels, local(): pl.pallas_call(finish_kernel, out_shape=[shape_of(1, 4, BLOCK, WIDTH)] +...  6.73 us

profile of v5, /device:TPU:1, one launch (start us, length us, event | category | flops | bytes accessed | tf_op | source)
XLA Modules:
  0.0 183.2 jit_solution(12625918079686922490)
XLA Ops:
  0.7 56.3 %start.1 = (bf16[2,576,768]{2,1,0:T(8,128)(2,1)}, bf16[2,768,768]{2,1,0:T(8,128)(2,1)}, bf16[2,192,768]{2,1,0:T(8,128)(2,1)}, bf16[2,768,768]{2,1,0:T(8,128)(2,1...) custom-call(bf16[576,768]{1,0:T(8,128)(2,1)} %bitcast.9, ...), custom_call_target="tpu_custom_call" | custom-call | tf_op jit(solution)/shard_map/start/pallas_call | solution.py:461
  56.9 40.0 %layer_one.1 = (f32[512,768]{1,0:T(8,128)}, f32[512,768]{1,0:T(8,128)}, f32[512,128]{1,0:T(8,128)}, bf16[2,256,768]{2,1,0:T(8,128)(2,1)}, f32[2,64,768]{2,1,0:T(...) custom-call(bf16[2,576,768]{2,1,0:T(8,128)(2,1)} %get-tuple-element.62.refs_, ...), custom_call_target="tpu_custom_call" | custom-call | tf_op jit(solution)/shard_map/layer_one/pallas_call | solution.py:461
  96.9 79.3 %layer_zero_back.1 = (bf16[2304,768]{1,0:T(8,128)(2,1)}, bf16[2304,768]{1,0:T(8,128)(2,1)}, f32[2,16,768]{2,1,0:T(8,128)}, bf16[4,256,768]{2,1,0:T(8,128)(2,1)}) custom-call(bf16[2,2,256,768]{3,2,1,0:T(8,128)(2,1)} %get-tuple-element.61.refs_2_.refs_11_.refs_0_, bf16[2,256,768]{2,1,0:T(8,128)(2,1)} %get-tuple-element.72.refs_1_, ...), custom_call_target="tpu_custom_call" | custom-call | tf_op jit(solution)/shard_map/layer_zero_back/pallas_call | solution.py:461
  176.2 6.7 %finish.1 = (f32[1,4,256,768]{3,2,1,0:T(8,128)}, f32[1,768]{1,0:T(1,128)}, f32[1,768]{1,0:T(1,128)}, f32[1,768]{1,0:T(1,128)}, f32[1,768]{1,0:T(1,128)}, /*index...) custom-call(bf16[2304,768]{1,0:T(8,128)(2,1)} %get-tuple-element.92., ...), custom_call_target="tpu_custom_call" | custom-call | tf_op jit(solution)/shard_map/finish/pallas_call | solution.py:1260
